TPU v7x, 32 devices: a whole 2x2x4 slice. The times are simulated.
32 devices in a mesh: groups: 2 (over x), lon: 8 (over z, y), lat: 2 (over core).
Axes of the slice: x: 2, y: 2, z: 4, core: 2. Of those that a mesh axis runs over, the one named last changes fastest.
Arguments:
- atmosphere: bfloat16 [256, 128, 512], P(('groups', 'lat'), 'lon'), parts along dimension 0, may hold values from -6 to 6
- pole_band: int32 [256], P(('groups', 'lat')), parts along dimension 0, may hold values from 0 to 15, never falling along the last dimension, each value on 1 to 96 neighbouring positions
- key_valid: int32 [256, 128], P(('groups', 'lat'), 'lon'), parts along dimension 0, may hold values 0 or 1
- norm_gains: float32 [2, 2, 512], replicated, may hold values from 0.5 to 1.5
- attend_in: bfloat16 [2, 512, 1536], replicated, as said below
- attend_out: bfloat16 [2, 512, 512], replicated, may hold values from -0.25 to 0.25
- expand: bfloat16 [2, 512, 1024], replicated, may hold values from -0.25 to 0.25
- contract: bfloat16 [2, 1024, 512], replicated, may hold values from -0.1875 to 0.1875
Outputs:
- evolved: bfloat16 [256, 128, 512], P(('groups', 'lat'), 'lon'), parts along dimension 0
There are 2 independent parts, one for each index of `groups`. A program takes and returns all parts, laid end to end along the dimension named above; an argument that names none is the same for every part. Nothing has to cross between parts.
Inputs may be any that keep to these rules, and one draw needn't show every extreme that they name: `pole_band`: band numbers never fall along latitude, every number from 0 to the largest is used, and a band holds 1 to 96 rows. `attend_in`: query and value entries of order one over the square root of 512.
All inputs are finite; a program needn't handle non-finite values. No bound on the sum of `key_valid` on one device may be relied on, other than what follows from the above.
Results may differ from a plain program's by a relative error of at most 0.011.
Values may be sent and summed in bfloat16 or wider, within the bound.
No kernel may reach another device: no remote copies, remote signals or barrier semaphores. Data moves between devices by JAX's collectives and lax.ppermute only.
A program may use at most 128 MiB of HBM per device.

v0:
```python
import math

import jax
import jax.numpy as jnp
from jax import lax
from jax.sharding import PartitionSpec as P

D = 512
H = 8
WH = 32
WW = 16
HD = 64
SH = 16
SW = 8


norm_eps = 1e-05


def shifted_2(value, axis, steps):
    count = lax.axis_size(axis)
    pairs = [(source, (source + steps) % count) for source in range(count)]
    return lax.ppermute(value, axis, pairs)


def normalize(field, gains):
    widened = field.astype(jnp.float32)
    average = jnp.mean(widened, -1, keepdims=True)
    centred = widened - average
    spread = jnp.mean(centred * centred, -1, keepdims=True)
    return (centred * lax.rsqrt(spread + norm_eps) * gains).astype(jnp.bfloat16)


def windows_of(field):
    height, breadth = (field.shape[0], field.shape[1])
    rest = field.shape[2:]
    tiles = field.reshape((height // WH, WH, breadth // WW, WW) + rest)
    return jnp.swapaxes(tiles, 1, 2).reshape((-1, WH * WW) + rest)


def field_of(tiles, height, breadth):
    rest = tiles.shape[2:]
    grid = tiles.reshape((height // WH, breadth // WW, WH, WW) + rest)
    return jnp.swapaxes(grid, 1, 2).reshape((height, breadth) + rest)


def attend_all(packed, bands, masks):
    count, cells = (packed.shape[0], packed.shape[1])
    heads = packed.reshape(count, cells, 3, H, HD)
    scores = jnp.einsum(
        "wqhd,wkhd->whqk", heads[:, :, 0], heads[:, :, 1], preferred_element_type=jnp.float32
    )
    scores = scores * (1.0 / math.sqrt(HD))
    itself = jnp.arange(cells)[:, None] == jnp.arange(cells)[None, :]
    allowed = (bands[:, :, None] == bands[:, None, :]) & ((masks[:, None, :] == 1) | itself[None])
    scores = jnp.where(allowed[:, None], scores, -1e30)
    row_max = jnp.max(scores, -1, keepdims=True)
    raw_weights = jnp.exp(scores - row_max)
    probs = (raw_weights / jnp.sum(raw_weights, -1, keepdims=True)).astype(jnp.bfloat16)
    context = jnp.einsum(
        "whqk,wkhd->wqhd", probs, heads[:, :, 2], preferred_element_type=jnp.float32
    )
    return context.astype(jnp.bfloat16).reshape(count, cells, D)


def layer(field, bands, masks, index, norm_gains, attend_in, attend_out, expand, contract):
    height, breadth = (field.shape[0], field.shape[1])
    normed = normalize(field, norm_gains[index, 0]).reshape(-1, D)
    projected = jnp.dot(normed, attend_in[index], preferred_element_type=jnp.float32)
    projected = projected.astype(jnp.bfloat16).reshape(height, breadth, 3 * D)
    band_grid = jnp.broadcast_to(bands[:, None], (height, breadth))
    context = attend_all(windows_of(projected), windows_of(band_grid), windows_of(masks))
    context = field_of(context, height, breadth).reshape(-1, D)
    resid = field.reshape(-1, D).astype(jnp.float32) + jnp.dot(
        context, attend_out[index], preferred_element_type=jnp.float32
    )
    resid = resid.astype(jnp.bfloat16)
    normed_mlp = normalize(resid, norm_gains[index, 1])
    hidden = jax.nn.gelu(
        jnp.dot(normed_mlp, expand[index], preferred_element_type=jnp.float32), approximate=True
    )
    hidden = hidden.astype(jnp.bfloat16)
    layer_out = resid.astype(jnp.float32) + jnp.dot(
        hidden, contract[index], preferred_element_type=jnp.float32
    )
    return layer_out.astype(jnp.bfloat16).reshape(height, breadth, D)


def on_device(
    atmosphere, pole_band, key_valid, norm_gains, attend_in, attend_out, expand, contract
):
    height = atmosphere.shape[0]
    band_wire = pole_band.astype(jnp.bfloat16)
    valid_wire = key_valid.astype(jnp.bfloat16)
    upper = shifted_2((atmosphere[:SH], band_wire[:SH], valid_wire[:SH]), "lat", -1)
    lat_field = jnp.concatenate([atmosphere[SH:], upper[0]], 0)
    moved_band = jnp.concatenate([band_wire[SH:], upper[1]], 0)
    lat_valid = jnp.concatenate([valid_wire[SH:], upper[2]], 0)
    eastern = shifted_2((lat_field[:, :SW], lat_valid[:, :SW]), "lon", -1)
    shifted = jnp.concatenate([lat_field[:, SW:], eastern[0]], 1)
    moved_valid = jnp.concatenate([lat_valid[:, SW:], eastern[1]], 1)
    shifted_band = moved_band.astype(jnp.int32)
    shifted_valid = moved_valid.astype(jnp.int32)
    first = layer(
        shifted, shifted_band, shifted_valid, 0, norm_gains, attend_in, attend_out, expand, contract
    )
    lower = shifted_2(first[height - SH :], "lat", 1)
    lat_back = jnp.concatenate([lower, first[: height - SH]], 0)
    breadth = lat_back.shape[1]
    western = shifted_2(lat_back[:, breadth - SW :], "lon", 1)
    back = jnp.concatenate([western, lat_back[:, : breadth - SW]], 1)
    return layer(back, pole_band, key_valid, 1, norm_gains, attend_in, attend_out, expand, contract)


def solution(mesh):
    in_specs = (
        P(("groups", "lat"), "lon", None),
        P(("groups", "lat")),
        P(("groups", "lat"), "lon"),
        P(),
        P(),
        P(),
        P(),
        P(),
    )
    out_specs = P(("groups", "lat"), "lon", None)
    return jax.shard_map(
        on_device, mesh=mesh, in_specs=in_specs, out_specs=out_specs, check_vma=False
    )
```

profile of v0, /device:TPU:0, one launch (start us, length us, event | category | flops | bytes accessed | tf_op | source)
XLA Modules:
  0.0 152.3 jit_solution(17633214878141570745)
XLA Ops:
  5.2 5.6 %collective-permute-start.4 = (bf16[64,8]{0,1:T(8,128)(2,1)S(1)}, bf16[64,8]{0,1:T(8,128)(2,1)S(1)}, u32[]{:S(2)}, u32[]{:S(2)}) collective-permute-start(bf16[64,8]{0,1:T(8,128)(2,1)S(1)} %get-tuple-element.22), channel_id=1, source_target_pairs={{0,14},{2,0},{4,2},{6,4},{8,6},{10,8},{12,10},{14,12},{1,15},{3,1}... | collective-permute-start | bytes 3080 | tf_op jit(solution)/shard_map/ppermute | solution.py:23
  12.5 2.3 %or_and_fusion = (pred[2,512,512]{1,2,0:T(8,128)(4,1)}, pred[2,512,512]{1,2,0:T(8,128)(4,1)}) fusion(s32[2,512]{1,0:T(2,128)S(1)} %broadcast_in_dim.34, pred[2,512]{1,0:T(4,128)(4,1)S(1)} %eq.98, pred[512,512]{0,1:T(8,128)(4,1)S(1)} %iota_compare_fusion, pred[2,512]{1,0:T(4,128)(4,1)S(1)} %eq.90, s32[2,512]{1,0:T(2,128)S(1)} %broadcast_in_dim.29), kind=kLoop, calls=%fused_computation.64 | loop fusion | flops 3145728 | bytes 1320960 | tf_op jit(solution)/shard_map/and | solution.py:55
  14.8 10.1 %collective-permute-done.1 = bf16[64,8,512]{2,1,0:T(8,128)(2,1)S(1)} collective-permute-done((bf16[64,8,512]{2,1,0:T(8,128)(2,1)S(1)}, bf16[64,8,512]{2,1,0:T(8,128)(2,1)S(1)}, u32[]{:S(2)}, u32[]{:S(2)}) %collective-permute-start.1) | collective-permute-done | bytes 524320 | tf_op jit(solution)/shard_map/ppermute | solution.py:23
  26.8 3.5 %convolution_convert_fusion.1 = bf16[1024,1536]{1,0:T(8,128)(2,1)} fusion(bf16[1024,512]{1,0:T(8,128)(2,1)S(1)} %bitcast.132, bf16[2,512,1536]{2,1,0:T(8,128)(2,1)S(1)} %copy-done.2), kind=kOutput, calls=%fused_computation.37 | convolution fusion | flops 1612185600 | bytes 5767168 | tf_op jit(solution)/shard_map/dot_general | solution.py:69
  30.3 8.9 %reshape.305 = bf16[2,512,3,8,64]{4,3,2,1,0:T(8,128)(2,1)} reshape(bf16[1024,1536]{1,0:T(8,128)(2,1)} %convolution_convert_fusion.1) | data formatting | bytes 6291456 | tf_op jit(solution)/shard_map/reshape;reshape;transpose;reshape;reshape | solution.py:49
  39.1 5.2 %fusion.135 = (bf16[2,512,1,8,64]{4,3,2,1,0:T(8,128)(2,1)}, bf16[2,512,1,8,64]{4,3,2,1,0:T(8,128)(2,1)}, bf16[2,512,1,8,64]{4,3,2,1,0:T(8,128)(2,1)S(1)}) fusion(bf16[2,512,3,8,64]{4,3,2,1,0:T(8,128)(2,1)} %reshape.305), kind=kLoop, calls=%fused_computation.151 | loop fusion | bytes 6291456 | tf_op jit(solution)/shard_map/slice | solution.py:61
  44.4 3.3 %copy.37 = bf16[2,512,1,8,64]{1,4,3,0,2:T(8,128)(2,1)} copy(bf16[2,512,1,8,64]{4,3,2,1,0:T(8,128)(2,1)} %get-tuple-element.10) | data formatting | bytes 2097152
  47.7 3.3 %copy.38 = bf16[2,512,1,8,64]{1,4,3,0,2:T(8,128)(2,1)} copy(bf16[2,512,1,8,64]{4,3,2,1,0:T(8,128)(2,1)} %get-tuple-element.11) | data formatting | bytes 2097152
  51.0 2.2 %copy.39 = bf16[2,512,1,8,64]{1,4,3,0,2:T(8,128)(2,1)} copy(bf16[2,512,1,8,64]{4,3,2,1,0:T(8,128)(2,1)S(1)} %get-tuple-element.12) | data formatting | bytes 2097152
  53.3 10.9 %fusion.137 = (f32[2,8,512]{2,1,0:T(8,128)S(1)}, f32[2,8,512,512]{2,3,1,0:T(8,128)}) fusion(pred[2,512,512]{1,2,0:T(8,128)(4,1)} %get-tuple-element.16, bf16[2,512,1,8,64]{1,4,3,0,2:T(8,128)(2,1)} %copy.39, bf16[2,512,1,8,64]{1,4,3,0,2:T(8,128)(2,1)} %copy.38), kind=kOutput, calls=%fused_computation.153 | convolution fusion | flops 553648640 | bytes 19431424 | tf_op jit(solution)/shard_map/sub | solution.py:58
  64.2 7.3 %fusion.52 = bf16[2,512,8,64]{1,3,2,0:T(8,128)(2,1)S(1)} fusion(f32[2,8,512,512]{2,3,1,0:T(8,128)} %get-tuple-element.24, f32[2,8,512]{2,1,0:T(8,128)S(1)} %get-tuple-element.23, bf16[2,512,1,8,64]{1,4,3,0,2:T(8,128)(2,1)S(1)} %copy-done.1), kind=kOutput, calls=%fused_computation.76 | convolution fusion | flops 545783808 | bytes 18907136 | tf_op jit(solution)/shard_map/whqk,wkhd->wqhd/dot_general | solution.py:60
  71.5 1.1 copy.23
  75.2 4.0 %fusion.38 = bf16[1024,512]{1,0:T(8,128)(2,1)S(1)} fusion(bf16[1024,512]{1,0:T(8,128)(2,1)S(1)} %get-tuple-element.26, bf16[2,1024,512]{2,1,0:T(8,128)(2,1)} %param.15, bf16[2,512,1024]{2,1,0:T(8,128)(2,1)} %param.14, f32[512]{0:T(512)S(1)} %bitcast.141, f32[1024]{0:T(1024)S(1)} %add_rsqrt_fusion.3, f32[1024]{0:T(1024)S(1)} %broadcast_multiply_fusion.3), kind=kOutput, calls=%fused_computation.54 | convolution fusion | flops 2161115136 | bytes 5253120 | tf_op jit(solution)/shard_map/dot_general | solution.py:83
  79.4 1.5 collective-permute-done.5
  81.0 16.6 %collective-permute-done.6 = bf16[64,8,512]{2,1,0:T(8,128)(2,1)S(1)} collective-permute-done((bf16[64,8,512]{2,1,0:T(8,128)(2,1)S(1)}, bf16[64,8,512]{2,1,0:T(8,128)(2,1)S(1)}, u32[]{:S(2)}, u32[]{:S(2)}) %collective-permute-start.6) | collective-permute-done | bytes 524320 | tf_op jit(solution)/shard_map/ppermute | solution.py:23
  99.8 3.5 %convolution_convert_fusion = bf16[1024,1536]{1,0:T(8,128)(2,1)} fusion(bf16[1024,512]{1,0:T(8,128)(2,1)S(1)} %bitcast.133, bf16[2,512,1536]{2,1,0:T(8,128)(2,1)S(1)} %copy-done.3), kind=kOutput, calls=%fused_computation.36 | convolution fusion | flops 1612185600 | bytes 5767168 | tf_op jit(solution)/shard_map/dot_general | solution.py:69
  103.3 8.9 %reshape.306 = bf16[2,512,3,8,64]{4,3,2,1,0:T(8,128)(2,1)} reshape(bf16[1024,1536]{1,0:T(8,128)(2,1)} %convolution_convert_fusion) | data formatting | bytes 6291456 | tf_op jit(solution)/shard_map/reshape;reshape;transpose;reshape;reshape | solution.py:49
  112.1 5.2 %fusion.134 = (bf16[2,512,1,8,64]{4,3,2,1,0:T(8,128)(2,1)}, bf16[2,512,1,8,64]{4,3,2,1,0:T(8,128)(2,1)}, bf16[2,512,1,8,64]{4,3,2,1,0:T(8,128)(2,1)S(1)}) fusion(bf16[2,512,3,8,64]{4,3,2,1,0:T(8,128)(2,1)} %reshape.306), kind=kLoop, calls=%fused_computation.150 | loop fusion | bytes 6291456 | tf_op jit(solution)/shard_map/slice | solution.py:61
  117.4 3.3 %copy.40 = bf16[2,512,1,8,64]{1,4,3,0,2:T(8,128)(2,1)} copy(bf16[2,512,1,8,64]{4,3,2,1,0:T(8,128)(2,1)} %get-tuple-element.7) | data formatting | bytes 2097152
  120.7 3.3 %copy.41 = bf16[2,512,1,8,64]{1,4,3,0,2:T(8,128)(2,1)} copy(bf16[2,512,1,8,64]{4,3,2,1,0:T(8,128)(2,1)} %get-tuple-element.8) | data formatting | bytes 2097152
  124.0 2.2 %copy.42 = bf16[2,512,1,8,64]{1,4,3,0,2:T(8,128)(2,1)} copy(bf16[2,512,1,8,64]{4,3,2,1,0:T(8,128)(2,1)S(1)} %get-tuple-element.9) | data formatting | bytes 2097152
  126.3 10.9 %fusion.146 = (f32[2,8,512]{2,1,0:T(8,128)S(1)}, f32[2,8,512,512]{2,3,1,0:T(8,128)}) fusion(pred[2,512,512]{1,2,0:T(8,128)(4,1)} %get-tuple-element.15, bf16[2,512,1,8,64]{1,4,3,0,2:T(8,128)(2,1)} %copy.42, bf16[2,512,1,8,64]{1,4,3,0,2:T(8,128)(2,1)} %copy.41), kind=kOutput, calls=%fused_computation.154 | convolution fusion | flops 553648640 | bytes 19431424 | tf_op jit(solution)/shard_map/sub | solution.py:58
  137.2 7.3 %fusion.53 = bf16[2,512,8,64]{1,3,2,0:T(8,128)(2,1)S(1)} fusion(f32[2,8,512,512]{2,3,1,0:T(8,128)} %get-tuple-element.28, f32[2,8,512]{2,1,0:T(8,128)S(1)} %get-tuple-element.27, bf16[2,512,1,8,64]{1,4,3,0,2:T(8,128)(2,1)S(1)} %copy-done), kind=kOutput, calls=%fused_computation.77 | convolution fusion | flops 545783808 | bytes 18907136 | tf_op jit(solution)/shard_map/whqk,wkhd->wqhd/dot_general | solution.py:60
  147.3 5.0 %fusion.39 = bf16[1024,512]{1,0:T(8,128)(2,1)} fusion(bf16[1024,512]{1,0:T(8,128)(2,1)S(1)} %get-tuple-element.30, bf16[2,1024,512]{2,1,0:T(8,128)(2,1)} %param.15, bf16[2,512,1024]{2,1,0:T(8,128)(2,1)} %param.14, f32[512]{0:T(512)S(1)} %bitcast.140, f32[1024]{0:T(1024)S(1)} %add_rsqrt_fusion.2, f32[1024]{0:T(1024)S(1)} %broadcast_multiply_fusion.2), kind=kOutput, calls=%fused_computation.55 | convolution fusion | flops 2161115136 | bytes 5253120 | tf_op jit(solution)/shard_map/dot_general | solution.py:83
  (73 shorter events, 16.3 us)
Async XLA Ops:
  0.0 10.7 %slice-start = ((bf16[64,16,512]{2,1,0:T(8,128)(2,1)}), bf16[48,16,512]{2,1,0:T(8,128)(2,1)S(1)}, s32[]{:S(2)}) async-start(bf16[64,16,512]{2,1,0:T(8,128)(2,1)} %param.8), calls=%async_computation | async-start | bytes 1572864 | tf_op jit(solution)/shard_map/slice | solution.py:96
  0.7 11.2 %collective-permute-start.2 = (bf16[16]{0:T(256)(128)(2,1)S(1)}, bf16[16]{0:T(256)(128)(2,1)S(1)}, u32[]{:S(2)}, u32[]{:S(2)}) collective-permute-start(bf16[16]{0:T(256)(128)(2,1)S(1)} %bitcast.143), channel_id=1, source_target_pairs={{0,1},{1,0},{2,3},{3,2},{4,5},{5,4},{6,7},{7,6},{8,9},{9,8},{10,11... | collective-permute-start | bytes 104 | tf_op jit(solution)/shard_map/ppermute | solution.py:23
  1.9 3.2 %collective-permute-start.3 = (bf16[16,16]{0,1:T(8,128)(2,1)S(1)}, bf16[16,16]{0,1:T(8,128)(2,1)S(1)}, u32[]{:S(2)}, u32[]{:S(2)}) collective-permute-start(bf16[16,16]{0,1:T(8,128)(2,1)S(1)} %bitcast.137), channel_id=1, source_target_pairs={{0,1},{1,0},{2,3},{3,2},{4,5},{5,4},{6,7},{7,6},{8,9},{9,8},{10,11... | collective-permute-start | bytes 1544 | tf_op jit(solution)/shard_map/ppermute | solution.py:23
  2.9 8.5 %copy-start.6 = (s32[64]{0:T(128)S(1)}, s32[64]{0:T(128)}, u32[]{:S(2)}) copy-start(s32[64]{0:T(128)} %param.9) | copy-start | bytes 772
  2.9 7.8 %collective-permute-start = (bf16[16,16,512]{2,1,0:T(8,128)(2,1)S(1)}, bf16[16,16,512]{2,1,0:T(8,128)(2,1)S(1)}, u32[]{:S(2)}, u32[]{:S(2)}) collective-permute-start(bf16[16,16,512]{2,1,0:T(8,128)(2,1)S(1)} %slice.103), channel_id=1, source_target_pairs={{0,1},{1,0},{2,3},{3,2},{4,5},{5,4},{6,7},{7,6},{8,9},{9,8},{10,11... | collective-permute-start | bytes 786440 | tf_op jit(solution)/shard_map/ppermute | solution.py:23
  5.2 7.1 %collective-permute-start.4 = (bf16[64,8]{0,1:T(8,128)(2,1)S(1)}, bf16[64,8]{0,1:T(8,128)(2,1)S(1)}, u32[]{:S(2)}, u32[]{:S(2)}) collective-permute-start(bf16[64,8]{0,1:T(8,128)(2,1)S(1)} %get-tuple-element.22), channel_id=1, source_target_pairs={{0,14},{2,0},{4,2},{6,4},{8,6},{10,8},{12,10},{14,12},{1,15},{3,1}... | collective-permute-start | bytes 3080 | tf_op jit(solution)/shard_map/ppermute | solution.py:23
  10.8 14.1 %collective-permute-start.1 = (bf16[64,8,512]{2,1,0:T(8,128)(2,1)S(1)}, bf16[64,8,512]{2,1,0:T(8,128)(2,1)S(1)}, u32[]{:S(2)}, u32[]{:S(2)}) collective-permute-start(bf16[64,8,512]{2,1,0:T(8,128)(2,1)S(1)} %get-tuple-element.14), channel_id=1, source_target_pairs={{0,14},{2,0},{4,2},{6,4},{8,6},{10,8},{12,10},{14,12},{1,15},{3,1}... | collective-permute-start | bytes 1572872 | tf_op jit(solution)/shard_map/ppermute | solution.py:23
  24.9 1.9 %copy-start.2 = (bf16[2,512,1536]{2,1,0:T(8,128)(2,1)S(1)}, bf16[2,512,1536]{2,1,0:T(8,128)(2,1)}, u32[]{:S(2)}) copy-start(bf16[2,512,1536]{2,1,0:T(8,128)(2,1)} %param.12) | copy-start | bytes 9437188
  53.3 10.9 %copy-start.1 = (bf16[2,512,1,8,64]{1,4,3,0,2:T(8,128)(2,1)S(1)}, bf16[2,512,1,8,64]{1,4,3,0,2:T(8,128)(2,1)}, u32[]{:S(2)}) copy-start(bf16[2,512,1,8,64]{1,4,3,0,2:T(8,128)(2,1)} %copy.37) | copy-start | bytes 3145732
  72.6 1.2 copy-start.4
  79.3 1.6 %collective-permute-start.5 = (bf16[16,16,512]{2,1,0:T(8,128)(2,1)S(1)}, bf16[16,16,512]{2,1,0:T(8,128)(2,1)S(1)}, u32[]{:S(2)}, u32[]{:S(2)}) collective-permute-start(bf16[16,16,512]{2,1,0:T(8,128)(2,1)S(1)} %bitcast.136), channel_id=1, source_target_pairs={{0,1},{1,0},{2,3},{3,2},{4,5},{5,4},{6,7},{7,6},{8,9},{9,8},{10,11... | collective-permute-start | bytes 786440 | tf_op jit(solution)/shard_map/ppermute | solution.py:23
  81.0 16.7 %collective-permute-start.6 = (bf16[64,8,512]{2,1,0:T(8,128)(2,1)S(1)}, bf16[64,8,512]{2,1,0:T(8,128)(2,1)S(1)}, u32[]{:S(2)}, u32[]{:S(2)}) collective-permute-start(bf16[64,8,512]{2,1,0:T(8,128)(2,1)S(1)} %fusion.107), channel_id=1, source_target_pairs={{0,2},{2,4},{4,6},{6,8},{8,10},{10,12},{12,14},{14,0},{1,3},{3,5},... | collective-permute-start | bytes 1572872 | tf_op jit(solution)/shard_map/ppermute | solution.py:23
  97.9 1.9 %copy-start.3 = (bf16[2,512,1536]{2,1,0:T(8,128)(2,1)S(1)}, bf16[2,512,1536]{2,1,0:T(8,128)(2,1)}, u32[]{:S(2)}) copy-start(bf16[2,512,1536]{2,1,0:T(8,128)(2,1)} %param.12) | copy-start | bytes 9437188
  126.3 10.9 %copy-start = (bf16[2,512,1,8,64]{1,4,3,0,2:T(8,128)(2,1)S(1)}, bf16[2,512,1,8,64]{1,4,3,0,2:T(8,128)(2,1)}, u32[]{:S(2)}) copy-start(bf16[2,512,1,8,64]{1,4,3,0,2:T(8,128)(2,1)} %copy.40) | copy-start | bytes 3145732
  144.5 1.3 copy-start.5
where the time goes:
time: 153 us; the launch traced here: 152 us
  matrix products  54.2 us (35%)
  local copies, waits for them, and re-layouts  53.9 us (35%)
  waiting for transfers between devices  28.2 us (18%)
  other arithmetic  8.38 us (5%)
  starting transfers between devices  7.29 us (5%)
    ppermute x7, waiting for transfers between devices, shifted_2(): return lax.ppermute(value, axis, pairs)  28.2 us
    sub x2, matrix products, attend_all(): raw_weights = jnp.exp(scores - row_max)  21.8 us
    unnamed x22, local copies, waits for them, and re-layouts  20.7 us
    another operation x2, local copies, waits for them, and re-layouts, attend_all(): heads = packed.reshape(count, cells, 3, H, HD)  17.7 us
    dot_general x2, matrix products, attend_all(): jnp.einsum('whqk,wkhd->wqhd', probs, heads[:, :, 2], preferred_element_ty...  14.7 us
    slice x2, local copies, waits for them, and re-layouts, attend_all(): heads[:, :, 2]  10.5 us
    dot_general x2, matrix products, layer(): jnp.dot(hidden, contract[index], preferred_element_type=jnp.float32)  9.07 us
    ppermute x7, starting transfers between devices, shifted_2(): return lax.ppermute(value, axis, pairs)  7.29 us
  transfers between devices with their start and end apart: 7, of which 3 were waited for; matrix products, arithmetic and copies ran while one was open for 4% of the time, Pallas kernels for 0%

commit v1 on v0

v1 whole, which is shorter than its diff:
```python
import functools
import math

import jax
import jax.numpy as jnp
from jax import lax
from jax.experimental import pallas as pl
from jax.experimental.pallas import tpu as pltpu
from jax.sharding import PartitionSpec as P

D = 512
H = 8
WH = 32
WW = 16
HD = 64
SH = 16
SW = 8

norm_eps = 1e-05

F32 = jnp.float32
BF16 = jnp.bfloat16
CLASSES = 128
META = 16
QSCALE = math.log2(math.e) / math.sqrt(HD)
TRANSPOSED_RIGHT = (((1,), (1,)), ((), ()))
TRANSPOSED_LEFT = (((0,), (0,)), ((), ()))
VMEM = pl.BlockSpec(memory_space=pltpu.VMEM)
SMEM = pl.BlockSpec(memory_space=pltpu.SMEM)


def product(left, right):
    return jnp.dot(left, right, preferred_element_type=F32)


def normalize(field, gains):
    average = jnp.mean(field, -1, keepdims=True)
    centred = field - average
    spread = jnp.mean(centred * centred, -1, keepdims=True)
    return (centred * lax.rsqrt(spread + norm_eps) * gains).astype(BF16)


def gelu(value):
    inner = math.sqrt(2.0 / math.pi) * (value + 0.044715 * value * value * value)
    return 0.5 * value * (1.0 + jnp.tanh(inner))


def half_columns(block, start):
    part = block.astype(F32)[:, start : start + SW]
    return part.reshape(block.shape[0] * SW, D)


def mask_lanes(valid, start, lanes):
    rows = valid.shape[0]
    column = lax.broadcasted_iota(jnp.int32, (valid.shape[1], lanes), 0)
    cell = lax.broadcasted_iota(jnp.int32, (valid.shape[1], lanes), 1)
    pick = (column == start + lax.rem(cell, SW)).astype(F32).astype(BF16)
    spread = product(valid.astype(F32).astype(BF16), pick)
    row = lax.broadcasted_iota(jnp.int32, (rows, lanes), 0)
    own = lax.div(lax.broadcasted_iota(jnp.int32, (rows, lanes), 1), SW)
    return jnp.sum(jnp.where(row == own, spread, 0.0), 0, keepdims=True)


def band_lanes(bands, start, rows, lanes):
    own = lax.div(lax.broadcasted_iota(jnp.int32, (1, lanes), 1), SW)
    found = jnp.zeros((1, lanes), jnp.int32)
    for row in range(rows):
        found = jnp.where(own == row, bands[start + row], found)
    return found.astype(F32)


def meta_rows(masks, bands):
    row = lax.broadcasted_iota(jnp.int32, (META, masks.shape[1]), 0)
    return jnp.where(row == 0, masks, jnp.where(row == 1, bands, 0.0)).astype(BF16)


def meta_of(ref, cells):
    tail = ref[pl.ds(cells, META), :].astype(F32)
    return tail[0:1, :cells], tail[1:2, :cells]


def project(field, gain, attend_in, at, query, key, value):
    rows = pl.ds(at, field.shape[0])
    normed = normalize(field, gain)
    query[rows, :] = (product(normed, attend_in[:, :D]) * QSCALE).astype(BF16)
    key[rows, :] = product(normed, attend_in[:, D : 2 * D]).astype(BF16)
    value[rows, :] = product(normed, attend_in[:, 2 * D :]).astype(BF16)


def set_bias(bias, bands, masks):
    cells = bands.shape[1]
    classes = lax.broadcasted_iota(jnp.int32, (CLASSES, cells), 0).astype(F32)
    one_hot = (classes == bands).astype(F32).astype(BF16)
    same = lax.dot_general(one_hot, one_hot, TRANSPOSED_LEFT, preferred_element_type=F32)
    asking = lax.broadcasted_iota(jnp.int32, (cells, cells), 0)
    asked = lax.broadcasted_iota(jnp.int32, (cells, cells), 1)
    allowed = (same > 0.5) & ((masks > 0.5) | (asking == asked))
    bias[...] = jnp.where(allowed, 0.0, -1e30)


def attend(query, key, value, bias, context):
    first = lax.broadcasted_iota(jnp.int32, (1, 2 * HD), 1) < HD
    for pair in range(H // 2):
        lanes = slice(2 * HD * pair, 2 * HD * (pair + 1))
        queries, keys, values = query[:, lanes], key[:, lanes], value[:, lanes]
        zero, one = jnp.zeros_like(queries), jnp.ones_like(values)
        sides = (
            (jnp.where(first, queries, zero), jnp.where(first, values, one)),
            (jnp.where(first, zero, queries), jnp.where(first, one, values)),
        )
        sums = []
        for own_queries, own_values in sides:
            scores = lax.dot_general(
                own_queries, keys, TRANSPOSED_RIGHT, preferred_element_type=F32
            )
            scores = scores + bias[...]
            row_max = jnp.max(scores, -1, keepdims=True)
            weights = jnp.exp2(scores - row_max).astype(BF16)
            sums.append(product(weights, own_values))
        above = jnp.where(first, sums[0], sums[1])
        below = pltpu.roll(jnp.where(first, sums[1], sums[0]), HD, 1)
        context[:, lanes] = (above / below).astype(BF16)


def finish(field, context, attend_out, gain, expand, contract):
    resid = (field + product(context, attend_out)).astype(BF16).astype(F32)
    normed = normalize(resid, gain)
    hidden = gelu(product(normed, expand)).astype(BF16)
    return resid + product(hidden, contract)


def pack_kernel(block, bands, valid, main, side, corner, row_end):
    height = block.shape[0]
    places = ((main, SH, height - SH, 0), (side, height - SH, height, 0),
              (corner, 0, SH, 0), (row_end, 0, SH, SW))
    for out, low, high, column in places:
        cells = (high - low) * SW
        out[pl.ds(0, cells), :] = half_columns(block[low:high], column).astype(BF16)
        masks = mask_lanes(valid[low:high], column, D)
        out[pl.ds(cells, META), :] = meta_rows(masks, band_lanes(bands, low, high - low, D))


def window_a_kernel(
    block, bands, valid, taken, gains, attend_in, attend_out, expand, contract,
    away, home, query, key, value, bias, context,
):
    height = block.shape[0]
    rows = height - 2 * SH
    cells = rows * SW
    local = half_columns(block[SH : SH + rows], SW)
    remote = taken[pl.ds(0, cells), :].astype(F32)
    project(local, gains[0:1], attend_in, 0, query, key, value)
    project(remote, gains[0:1], attend_in, cells, query, key, value)
    row_bands = band_lanes(bands, SH, rows, cells)
    masks, _ = meta_of(taken, cells)
    set_bias(
        bias,
        jnp.concatenate([row_bands, row_bands], 1),
        jnp.concatenate([mask_lanes(valid[SH : SH + rows], SW, cells), masks], 1),
    )
    attend(query, key, value, bias, context)
    field = jnp.concatenate([local, remote], 0)
    out = finish(field, context[...], attend_out[...], gains[1:2], expand[...], contract[...])
    out = out.astype(BF16)
    home[...] = out[:cells]
    away[...] = out[cells:]


def window_b_kernel(
    block, bands, valid, taken_side, taken_corner, taken_end,
    gains, attend_in, attend_out, expand, contract,
    away_side, away_corner, home_side, home_end, query, key, value, bias, context,
):
    height = block.shape[0]
    cells = SH * SW
    parts = [half_columns(block[height - SH :], SW)]
    bands_here = [band_lanes(bands, height - SH, SH, cells)]
    masks_here = [mask_lanes(valid[height - SH :], SW, cells)]
    for taken in (taken_end, taken_side, taken_corner):
        parts.append(taken[pl.ds(0, cells), :].astype(F32))
        masks, row_bands = meta_of(taken, cells)
        masks_here.append(masks)
        bands_here.append(row_bands)
    field = jnp.concatenate(parts, 0)
    project(field, gains[0:1], attend_in, 0, query, key, value)
    set_bias(bias, jnp.concatenate(bands_here, 1), jnp.concatenate(masks_here, 1))
    attend(query, key, value, bias, context)
    out = finish(field, context[...], attend_out[...], gains[1:2], expand[...], contract[...])
    out = out.astype(BF16)
    for index, ref in enumerate((home_side, home_end, away_side, away_corner)):
        ref[...] = out[index * cells : (index + 1) * cells]


def second_kernel(
    home, home_side, near_end, far, far_side, far_corner, bands, valid,
    gains, attend_in, attend_out, expand, contract,
    out_ref, query, key, value, bias, context,
):
    half = SH * SW
    low, high = pl.ds(0, half), pl.ds(half, half)
    windows = (
        (near_end[...], home[low, :], far_corner[...], far[low, :]),
        (home[high, :], home_side[...], far[high, :], far_side[...]),
    )
    for index, parts in enumerate(windows):
        field = jnp.concatenate([part.astype(F32) for part in parts], 0)
        project(field, gains[0:1], attend_in, 0, query, key, value)
        rows = slice(index * WH, (index + 1) * WH)
        row_bands = band_lanes(bands, index * WH, WH, 2 * half)
        set_bias(
            bias,
            jnp.concatenate([row_bands, row_bands], 1),
            jnp.concatenate(
                [mask_lanes(valid[rows], SW, 2 * half), mask_lanes(valid[rows], 0, 2 * half)], 1
            ),
        )
        attend(query, key, value, bias, context)
        out = finish(field, context[...], attend_out[...], gains[1:2], expand[...], contract[...])
        right = out[: 2 * half].reshape(WH, SW, D)
        left = out[2 * half :].reshape(WH, SW, D)
        out_ref[pl.ds(index * WH, WH)] = jnp.concatenate([left, right], 1).astype(BF16)


def call(kernel, name, shapes, specs, scratch, flops, *operands):
    size = sum(operand.size * operand.dtype.itemsize for operand in operands)
    return pl.pallas_call(
        kernel,
        out_shape=[jax.ShapeDtypeStruct(shape, BF16) for shape in shapes],
        in_specs=specs,
        out_specs=[VMEM] * len(shapes),
        scratch_shapes=scratch,
        compiler_params=pltpu.CompilerParams(vmem_limit_bytes=40 * 2**20),
        cost_estimate=pl.CostEstimate(flops=flops, bytes_accessed=size, transcendentals=0),
        name=name,
    )(*operands)


def on_device(
    atmosphere, pole_band, key_valid, norm_gains, attend_in, attend_out, expand, contract
):
    height, breadth = atmosphere.shape[0], atmosphere.shape[1]
    assert height == 2 * WH and breadth == WW
    lons, lats = lax.axis_size("lon"), lax.axis_size("lat")

    def moved(value, lon_step, lat_step):
        pairs = [
            (lon * lats + lat, (lon + lon_step) % lons * lats + (lat + lat_step) % lats)
            for lon in range(lons)
            for lat in range(lats)
        ]
        return lax.ppermute(value, ("lon", "lat"), pairs)

    cells = WH * WW
    quarter = cells // 4
    scratch = (
        [pltpu.VMEM((cells, D), BF16)] * 3
        + [pltpu.VMEM((cells, cells), F32), pltpu.VMEM((cells, D), BF16)]
    )
    hidden = expand.shape[-1]
    flops = 2 * cells * D * (4 * D + 2 * hidden) + 4 * cells * cells * D

    main, side, corner, row_end = call(
        pack_kernel, "pack",
        [(2 * quarter + META, D)] + [(quarter + META, D)] * 3,
        [VMEM, SMEM, VMEM], [], 10**6, atmosphere, pole_band, key_valid,
    )
    far_main = moved(main, -1, 0)
    far_side = moved(side, -1, 0)
    far_corner = moved(corner, -1, -1)
    near_end = moved(row_end, 0, -1)

    layer_weights = [
        (norm_gains[k], attend_in[k], attend_out[k], expand[k], contract[k]) for k in range(2)
    ]
    place = (atmosphere, pole_band, key_valid)
    where = [VMEM, SMEM, VMEM]
    away, home = call(
        window_a_kernel, "window_a", [(2 * quarter, D)] * 2, where + [VMEM] * 6, scratch, flops,
        *place, far_main, *layer_weights[0],
    )
    back_main = moved(away, 1, 0)
    away_side, away_corner, home_side, home_end = call(
        window_b_kernel, "window_b", [(quarter, D)] * 4, where + [VMEM] * 8, scratch, flops,
        *place, far_side, far_corner, near_end, *layer_weights[0],
    )
    back_side = moved(away_side, 1, 0)
    back_corner = moved(away_corner, 1, 1)
    back_end = moved(home_end, 0, 1)
    return call(
        second_kernel, "second", [(height, breadth, D)],
        [VMEM] * 6 + [SMEM] + [VMEM] * 6, scratch, 2 * flops,
        home, home_side, back_end, back_main, back_side, back_corner,
        pole_band, key_valid, *layer_weights[1],
    )[0]


def solution(mesh):
    in_specs = (
        P(("groups", "lat"), "lon", None),
        P(("groups", "lat")),
        P(("groups", "lat"), "lon"),
        P(),
        P(),
        P(),
        P(),
        P(),
    )
    out_specs = P(("groups", "lat"), "lon", None)
    return jax.shard_map(
        on_device, mesh=mesh, in_specs=in_specs, out_specs=out_specs, check_vma=False
    )
```

time: 153 us -> 60.2 us (0.39)
  matrix products: 54.2 us -> 0 us
  local copies, waits for them, and re-layouts: 53.9 us -> 7.56 us
  Pallas kernels: 0 us -> 26.6 us
  waiting for transfers between devices: 28.2 us -> 14 us
  other arithmetic: 8.38 us -> 0 us
  starting transfers between devices: 7.29 us -> 11.6 us
    dot_general x8 -> x0, matrix products: 32.4 us -> none  [the longest x2 14.7 us: attend_all(): jnp.einsum('whqk,wkhd->wqhd', probs, heads[:, :, 2], preferred_element_ty...]
    pallas_call x0 -> x4, Pallas kernels: none -> 26.6 us  [call(): pl.pallas_call(kernel, out_shape=[jax.ShapeDtypeStruct(shape, BF16) for s...]
    sub x2 -> x0, matrix products: 21.8 us -> none  [attend_all(): raw_weights = jnp.exp(scores - row_max)]
    another operation x2 -> x0, local copies, waits for them, and re-layouts: 17.7 us -> none  [attend_all(): heads = packed.reshape(count, cells, 3, H, HD)]
    unnamed x22 -> x15, local copies, waits for them, and re-layouts: 20.7 us -> 5.44 us
    ppermute x7 -> x8, waiting for transfers between devices: 28.2 us -> 14 us  [moved(): return lax.ppermute(value, ('lon', 'lat'), pairs)]
    slice x9 -> x0, local copies, waits for them, and re-layouts: 12.4 us -> none  [the longest x2 10.5 us: attend_all(): heads[:, :, 2]]
    ppermute x7 -> x8, starting transfers between devices: 7.29 us -> 11.6 us  [moved(): return lax.ppermute(value, ('lon', 'lat'), pairs)]
  transfers between devices with their start and end apart: 7 -> 8, of which waited for: 3 -> 3; matrix products, arithmetic and copies ran while one was open for 4% -> 4% of each run, Pallas kernels for 0% -> 22%
where the time goes in v1:
time: 60.2 us; the launch traced here: 59.9 us
  Pallas kernels  26.6 us (44%)
  waiting for transfers between devices  14 us (23%)
  starting transfers between devices  11.6 us (19%)
  local copies, waits for them, and re-layouts  7.56 us (13%)
    pallas_call x4, Pallas kernels, call(): pl.pallas_call(kernel, out_shape=[jax.ShapeDtypeStruct(shape, BF16) for s...  26.6 us
    ppermute x8, waiting for transfers between devices, moved(): return lax.ppermute(value, ('lon', 'lat'), pairs)  14 us
    ppermute x8, starting transfers between devices, moved(): return lax.ppermute(value, ('lon', 'lat'), pairs)  11.6 us
    unnamed x15, local copies, waits for them, and re-layouts  5.44 us
    squeeze x1, local copies, waits for them, and re-layouts, on_device(): expand[k]  1.71 us
  transfers between devices with their start and end apart: 8, of which 3 were waited for; matrix products, arithmetic and copies ran while one was open for 4% of the time, Pallas kernels for 22%

profile of v1, /device:TPU:0, one launch (start us, length us, event | category | flops | bytes accessed | tf_op | source)
XLA Modules:
  0.0 59.9 jit_solution(15251588130337334326)
XLA Ops:
  0.0 0.8 %copy.10.valid = s32[64,16]{1,0:T(8,128)S(1)} copy(s32[64,16]{0,1:T(8,128)} %param.10) | data formatting | bytes 8192 | tf_op args[2]
  0.8 1.2 %copy-done = bf16[64,16,512]{2,1,0:T(8,128)(2,1)S(1)} copy-done((bf16[64,16,512]{2,1,0:T(8,128)(2,1)S(1)}, bf16[64,16,512]{2,1,0:T(8,128)(2,1)}, u32[]{:S(2)}) %copy-start) | copy-done | bytes 1048600
  2.0 0.7 %copy-done.1 = s32[64]{0:T(128)S(1)} copy-done((s32[64]{0:T(128)S(1)}, s32[64]{0:T(128)}, u32[]{:S(2)}) %copy-start.1) | copy-done | bytes 280
  2.7 0.7 %pack.1 = (bf16[272,512]{1,0:T(8,128)(2,1)S(1)}, bf16[144,512]{1,0:T(8,128)(2,1)S(1)}, bf16[144,512]{1,0:T(8,128)(2,1)S(1)}, bf16[144,512]{1,0:T(8,128)(2,1)S(1)}) custom-call(bf16[64,16,512]{2,1,0:T(8,128)(2,1)S(1)} %copy-done, s32[64]{0:T(128)S(1)} %copy-done.1, s32[64,16]{1,0:T(8,128)S(1)} %copy.10.valid), custom_call_target="tpu_custom_call" | custom-call | flops 1000000 | bytes 1052928 | tf_op jit(solution)/shard_map/pack/pallas_call | solution.py:226
  3.4 6.1 %collective-permute-start.1 = (bf16[144,512]{1,0:T(8,128)(2,1)S(1)}, bf16[144,512]{1,0:T(8,128)(2,1)S(1)}, u32[]{:S(2)}, u32[]{:S(2)}) collective-permute-start(bf16[144,512]{1,0:T(8,128)(2,1)S(1)} %get-tuple-element.17), channel_id=1, source_target_pairs={{0,14},{1,15},{2,0},{3,1},{4,2},{5,3},{6,4},{7,5},{8,6},{9,7},{10,... | collective-permute-start | bytes 442376 | tf_op jit(solution)/shard_map/ppermute | solution.py:251
  9.4 0.6 %collective-permute-start.3 = (bf16[144,512]{1,0:T(8,128)(2,1)S(1)}, bf16[144,512]{1,0:T(8,128)(2,1)S(1)}, u32[]{:S(2)}, u32[]{:S(2)}) collective-permute-start(bf16[144,512]{1,0:T(8,128)(2,1)S(1)} %get-tuple-element.19), channel_id=1, source_target_pairs={{0,1},{1,0},{2,3},{3,2},{4,5},{5,4},{6,7},{7,6},{8,9},{9,8},{10,11... | collective-permute-start | bytes 442376 | tf_op jit(solution)/shard_map/ppermute | solution.py:251
  10.1 1.4 %collective-permute-start = (bf16[272,512]{1,0:T(8,128)(2,1)S(1)}, bf16[272,512]{1,0:T(8,128)(2,1)S(1)}, u32[]{:S(2)}, u32[]{:S(2)}) collective-permute-start(bf16[272,512]{1,0:T(8,128)(2,1)S(1)} %get-tuple-element.15), channel_id=1, source_target_pairs={{0,14},{1,15},{2,0},{3,1},{4,2},{5,3},{6,4},{7,5},{8,6},{9,7},{10,... | collective-permute-start | bytes 835592 | tf_op jit(solution)/shard_map/ppermute | solution.py:251
  11.5 1.7 %slice_bitcast_fusion.3 = (bf16[512,1024]{1,0:T(8,128)(2,1)S(1)}, bf16[512,1024]{1,0:T(8,128)(2,1)S(1)}) fusion(bf16[2,512,1024]{2,1,0:T(8,128)(2,1)} %param.14), kind=kLoop, calls=%fused_computation.3 | loop fusion | bytes 4194304 | tf_op jit(solution)/shard_map/squeeze | solution.py:273
  13.2 0.1 slice_bitcast_fusion.2
  13.4 1.7 %copy-done.3 = bf16[2,512,1536]{2,1,0:T(8,128)(2,1)S(1)} copy-done((bf16[2,512,1536]{2,1,0:T(8,128)(2,1)S(1)}, bf16[2,512,1536]{2,1,0:T(8,128)(2,1)}, u32[]{:S(2)}) %copy-start.3) | copy-done | bytes 3145752
  15.1 0.2 slice_bitcast_fusion
  15.3 0.5 copy-done.6
  15.8 0.5 copy-done.5
  16.3 0.1 slice_bitcast_fusion.6
  16.4 5.3 %collective-permute-done.taken = bf16[272,512]{1,0:T(8,128)(2,1)S(1)} collective-permute-done((bf16[272,512]{1,0:T(8,128)(2,1)S(1)}, bf16[272,512]{1,0:T(8,128)(2,1)S(1)}, u32[]{:S(2)}, u32[]{:S(2)}) %collective-permute-start) | collective-permute-done | bytes 278560 | tf_op jit(solution)/shard_map/ppermute | solution.py:251
  21.7 6.4 %window_a.1 = (bf16[256,512]{1,0:T(8,128)(2,1)S(1)}, bf16[256,512]{1,0:T(8,128)(2,1)S(1)}) custom-call(bf16[64,16,512]{2,1,0:T(8,128)(2,1)S(1)} %copy-done, s32[64]{0:T(128)S(1)} %copy-done.1, s32[64,16]{1,0:T(8,128)S(1)} %copy.10.valid, bf16[272,512]{1,0:T(8,128)(2,1)S(1)} %collective-permute-done.taken, f32[2,512]{1,0:T(2,128)S(1)} %get-tuple-element.34.gains, ...), custom_call_target="tpu_custom_call" | custom-call | flops 2684354560 | bytes 5529856 | tf_op jit(solution)/shard_map/window_a/pallas_call | solution.py:226
  28.1 0.5 collective-permute-start.5
  28.6 6.6 %window_b.1 = (bf16[128,512]{1,0:T(8,128)(2,1)S(1)}, bf16[128,512]{1,0:T(8,128)(2,1)S(1)}, bf16[128,512]{1,0:T(8,128)(2,1)S(1)}, bf16[128,512]{1,0:T(8,128)(2,1)S(1)}) custom-call(bf16[64,16,512]{2,1,0:T(8,128)(2,1)S(1)} %copy-done, s32[64]{0:T(128)S(1)} %copy-done.1, s32[64,16]{1,0:T(8,128)S(1)} %copy.10.valid, ...), custom_call_target="tpu_custom_call" | custom-call | flops 2684354560 | bytes 5693696 | tf_op jit(solution)/shard_map/window_b/pallas_call | solution.py:226
  35.2 0.1 collective-permute-start.4
  35.3 0.7 %collective-permute-start.6 = (bf16[128,512]{1,0:T(8,128)(2,1)S(1)}, bf16[128,512]{1,0:T(8,128)(2,1)S(1)}, u32[]{:S(2)}, u32[]{:S(2)}) collective-permute-start(bf16[128,512]{1,0:T(8,128)(2,1)S(1)} %get-tuple-element.23), channel_id=1, source_target_pairs={{0,2},{1,3},{2,4},{3,5},{4,6},{5,7},{6,8},{7,9},{8,10},{9,11},{10,... | collective-permute-start | bytes 393224 | tf_op jit(solution)/shard_map/ppermute | solution.py:251
  36.0 2.2 %collective-permute-start.7 = (bf16[128,512]{1,0:T(8,128)(2,1)S(1)}, bf16[128,512]{1,0:T(8,128)(2,1)S(1)}, u32[]{:S(2)}, u32[]{:S(2)}) collective-permute-start(bf16[128,512]{1,0:T(8,128)(2,1)S(1)} %get-tuple-element.24), channel_id=1, source_target_pairs={{0,3},{1,2},{2,5},{3,4},{4,7},{5,6},{6,9},{7,8},{8,11},{9,10},{10,... | collective-permute-start | bytes 393224 | tf_op jit(solution)/shard_map/ppermute | solution.py:251
  38.2 6.4 %collective-permute-done.6.far_side = bf16[128,512]{1,0:T(8,128)(2,1)S(1)} collective-permute-done((bf16[128,512]{1,0:T(8,128)(2,1)S(1)}, bf16[128,512]{1,0:T(8,128)(2,1)S(1)}, u32[]{:S(2)}, u32[]{:S(2)}) %collective-permute-start.6) | collective-permute-done | bytes 131104 | tf_op jit(solution)/shard_map/ppermute | solution.py:251
  44.6 2.3 %collective-permute-done.7.far_corner = bf16[128,512]{1,0:T(8,128)(2,1)S(1)} collective-permute-done((bf16[128,512]{1,0:T(8,128)(2,1)S(1)}, bf16[128,512]{1,0:T(8,128)(2,1)S(1)}, u32[]{:S(2)}, u32[]{:S(2)}) %collective-permute-start.7) | collective-permute-done | bytes 131104 | tf_op jit(solution)/shard_map/ppermute | solution.py:251
  46.9 13.0 %second.1 = bf16[64,16,512]{2,1,0:T(8,128)(2,1)} custom-call(bf16[256,512]{1,0:T(8,128)(2,1)S(1)} %get-tuple-element.16.home, bf16[128,512]{1,0:T(8,128)(2,1)S(1)} %get-tuple-element.20.home_side, bf16[128,512]{1,0:T(8,128)(2,1)S(1)} %collective-permute-done.4.near_end, bf16[256,512]{1,0:T(8,128)(2,1)S(1)} %collective-permute-done.5.far, ...), custom_call_target="tpu_custom_call" | custom-call | flops 5368709120 | bytes 5251328 | tf_op jit(solution)/shard_map/second/pallas_call | solution.py:226
  (16 shorter events, 0.0 us)
Async XLA Ops:
  0.8 1.2 %copy-start = (bf16[64,16,512]{2,1,0:T(8,128)(2,1)S(1)}, bf16[64,16,512]{2,1,0:T(8,128)(2,1)}, u32[]{:S(2)}) copy-start(bf16[64,16,512]{2,1,0:T(8,128)(2,1)} %block.5) | copy-start | bytes 3145732
  2.0 0.7 %copy-start.1 = (s32[64]{0:T(128)S(1)}, s32[64]{0:T(128)}, u32[]{:S(2)}) copy-start(s32[64]{0:T(128)} %bands.7) | copy-start | bytes 772
  3.4 25.2 %collective-permute-start.1 = (bf16[144,512]{1,0:T(8,128)(2,1)S(1)}, bf16[144,512]{1,0:T(8,128)(2,1)S(1)}, u32[]{:S(2)}, u32[]{:S(2)}) collective-permute-start(bf16[144,512]{1,0:T(8,128)(2,1)S(1)} %get-tuple-element.17), channel_id=1, source_target_pairs={{0,14},{1,15},{2,0},{3,1},{4,2},{5,3},{6,4},{7,5},{8,6},{9,7},{10,... | collective-permute-start | bytes 442376 | tf_op jit(solution)/shard_map/ppermute | solution.py:251
  9.4 19.2 %collective-permute-start.2 = (bf16[144,512]{1,0:T(8,128)(2,1)S(1)}, bf16[144,512]{1,0:T(8,128)(2,1)S(1)}, u32[]{:S(2)}, u32[]{:S(2)}) collective-permute-start(bf16[144,512]{1,0:T(8,128)(2,1)S(1)} %get-tuple-element.18), channel_id=1, source_target_pairs={{0,15},{1,14},{2,1},{3,0},{4,3},{5,2},{6,5},{7,4},{8,7},{9,6},{10,... | collective-permute-start | bytes 442376 | tf_op jit(solution)/shard_map/ppermute | solution.py:251
  9.4 19.2 %collective-permute-start.3 = (bf16[144,512]{1,0:T(8,128)(2,1)S(1)}, bf16[144,512]{1,0:T(8,128)(2,1)S(1)}, u32[]{:S(2)}, u32[]{:S(2)}) collective-permute-start(bf16[144,512]{1,0:T(8,128)(2,1)S(1)} %get-tuple-element.19), channel_id=1, source_target_pairs={{0,1},{1,0},{2,3},{3,2},{4,5},{5,4},{6,7},{7,6},{8,9},{9,8},{10,11... | collective-permute-start | bytes 442376 | tf_op jit(solution)/shard_map/ppermute | solution.py:251
  10.1 3.1 %copy-start.4 = (bf16[2,1024,512]{2,1,0:T(8,128)(2,1)S(1)}, bf16[2,1024,512]{2,1,0:T(8,128)(2,1)}, u32[]{:S(2)}) copy-start(bf16[2,1024,512]{2,1,0:T(8,128)(2,1)} %param.15) | copy-start | bytes 6291460
  10.1 11.6 %collective-permute-start = (bf16[272,512]{1,0:T(8,128)(2,1)S(1)}, bf16[272,512]{1,0:T(8,128)(2,1)S(1)}, u32[]{:S(2)}, u32[]{:S(2)}) collective-permute-start(bf16[272,512]{1,0:T(8,128)(2,1)S(1)} %get-tuple-element.15), channel_id=1, source_target_pairs={{0,14},{1,15},{2,0},{3,1},{4,2},{5,3},{6,4},{7,5},{8,6},{9,7},{10,... | collective-permute-start | bytes 835592 | tf_op jit(solution)/shard_map/ppermute | solution.py:251
  13.2 1.9 %copy-start.3 = (bf16[2,512,1536]{2,1,0:T(8,128)(2,1)S(1)}, bf16[2,512,1536]{2,1,0:T(8,128)(2,1)}, u32[]{:S(2)}) copy-start(bf16[2,512,1536]{2,1,0:T(8,128)(2,1)} %param.12) | copy-start | bytes 9437188
  15.1 0.7 %copy-start.6 = (f32[2,2,512]{2,1,0:T(2,128)S(1)}, f32[2,2,512]{2,1,0:T(2,128)}, u32[]{:S(2)}) copy-start(f32[2,2,512]{2,1,0:T(2,128)} %param.11) | copy-start | bytes 24580
  15.1 1.2 %copy-start.5 = (bf16[2,512,512]{2,1,0:T(8,128)(2,1)S(1)}, bf16[2,512,512]{2,1,0:T(8,128)(2,1)}, u32[]{:S(2)}) copy-start(bf16[2,512,512]{2,1,0:T(8,128)(2,1)} %param.13) | copy-start | bytes 3145732
  28.1 18.9 %copy-start.2 = (s32[64]{0:T(128)S(1)}, s32[64]{0:T(128)}, u32[]{:S(2)}) copy-start(s32[64]{0:T(128)} %bands.7) | copy-start | bytes 772
  28.1 18.8 %collective-permute-start.5 = (bf16[256,512]{1,0:T(8,128)(2,1)S(1)}, bf16[256,512]{1,0:T(8,128)(2,1)S(1)}, u32[]{:S(2)}, u32[]{:S(2)}) collective-permute-start(bf16[256,512]{1,0:T(8,128)(2,1)S(1)} %get-tuple-element.22), channel_id=1, source_target_pairs={{0,2},{1,3},{2,4},{3,5},{4,6},{5,7},{6,8},{7,9},{8,10},{9,11},{10,... | collective-permute-start | bytes 786440 | tf_op jit(solution)/shard_map/ppermute | solution.py:251
  35.2 3.0 %collective-permute-start.4 = (bf16[128,512]{1,0:T(8,128)(2,1)S(1)}, bf16[128,512]{1,0:T(8,128)(2,1)S(1)}, u32[]{:S(2)}, u32[]{:S(2)}) collective-permute-start(bf16[128,512]{1,0:T(8,128)(2,1)S(1)} %get-tuple-element.21), channel_id=1, source_target_pairs={{0,1},{1,0},{2,3},{3,2},{4,5},{5,4},{6,7},{7,6},{8,9},{9,8},{10,11... | collective-permute-start | bytes 393224 | tf_op jit(solution)/shard_map/ppermute | solution.py:251
  35.3 9.3 %collective-permute-start.6 = (bf16[128,512]{1,0:T(8,128)(2,1)S(1)}, bf16[128,512]{1,0:T(8,128)(2,1)S(1)}, u32[]{:S(2)}, u32[]{:S(2)}) collective-permute-start(bf16[128,512]{1,0:T(8,128)(2,1)S(1)} %get-tuple-element.23), channel_id=1, source_target_pairs={{0,2},{1,3},{2,4},{3,5},{4,6},{5,7},{6,8},{7,9},{8,10},{9,11},{10,... | collective-permute-start | bytes 393224 | tf_op jit(solution)/shard_map/ppermute | solution.py:251
  36.0 10.9 %collective-permute-start.7 = (bf16[128,512]{1,0:T(8,128)(2,1)S(1)}, bf16[128,512]{1,0:T(8,128)(2,1)S(1)}, u32[]{:S(2)}, u32[]{:S(2)}) collective-permute-start(bf16[128,512]{1,0:T(8,128)(2,1)S(1)} %get-tuple-element.24), channel_id=1, source_target_pairs={{0,3},{1,2},{2,5},{3,4},{4,7},{5,6},{6,9},{7,8},{8,11},{9,10},{10,... | collective-permute-start | bytes 393224 | tf_op jit(solution)/shard_map/ppermute | solution.py:251

commit v2 on v1

v2 whole, which is shorter than its diff:
```python
import functools
import math

import jax
import jax.numpy as jnp
from jax import lax
from jax.experimental import pallas as pl
from jax.experimental.pallas import tpu as pltpu
from jax.sharding import PartitionSpec as P

D = 512
H = 8
WH = 32
WW = 16
HD = 64
SH = 16
SW = 8

norm_eps = 1e-05

F32 = jnp.float32
BF16 = jnp.bfloat16
CLASSES = 128
META = 16
QSCALE = math.log2(math.e) / math.sqrt(HD)
TRANSPOSED_RIGHT = (((1,), (1,)), ((), ()))
TRANSPOSED_LEFT = (((0,), (0,)), ((), ()))
VMEM = pl.BlockSpec(memory_space=pltpu.VMEM)
SMEM = pl.BlockSpec(memory_space=pltpu.SMEM)
HBM = pl.BlockSpec(memory_space=pltpu.HBM)


def product(left, right):
    return jnp.dot(left, right, preferred_element_type=F32)


def normalize(field, gains):
    average = jnp.mean(field, -1, keepdims=True)
    centred = field - average
    spread = jnp.mean(centred * centred, -1, keepdims=True)
    return (centred * lax.rsqrt(spread + norm_eps) * gains).astype(BF16)


def gelu(value):
    scale = math.sqrt(2.0 / math.pi)
    bent = jnp.tanh(value * (scale + (scale * 0.044715) * (value * value)))
    half = 0.5 * value
    return half + half * bent


def half_columns(block, start):
    part = block.astype(F32)[:, start : start + SW]
    return part.reshape(block.shape[0] * SW, D)


def mask_lanes(valid, low, start, lanes):
    columns, height = valid.shape
    row = lax.broadcasted_iota(jnp.int32, (height, lanes), 0)
    cell = lax.broadcasted_iota(jnp.int32, (height, lanes), 1)
    pick = (row == low + lax.div(cell, SW)).astype(F32).astype(BF16)
    spread = product(valid[...].astype(F32).astype(BF16), pick)
    column = lax.broadcasted_iota(jnp.int32, (columns, lanes), 0)
    own = start + lax.rem(lax.broadcasted_iota(jnp.int32, (columns, lanes), 1), SW)
    return jnp.sum(jnp.where(column == own, spread, 0.0), 0, keepdims=True)


def band_lanes(bands, start, rows, lanes):
    own = lax.div(lax.broadcasted_iota(jnp.int32, (1, lanes), 1), SW)
    found = jnp.zeros((1, lanes), jnp.int32)
    for row in range(rows):
        found = jnp.where(own == row, bands[start + row], found)
    return found.astype(F32)


def meta_rows(masks, bands):
    row = lax.broadcasted_iota(jnp.int32, (META, masks.shape[1]), 0)
    return jnp.where(row == 0, masks, jnp.where(row == 1, bands, 0.0)).astype(BF16)


def meta_of(ref, cells):
    tail = ref[pl.ds(cells, META), :].astype(F32)
    return tail[0:1, :cells], tail[1:2, :cells]


def in_turn(count, stages):
    state = [None] * count
    for step in range(count + len(stages) - 1):
        for index, stage in enumerate(stages):
            piece = step - index
            if 0 <= piece < count:
                state[piece] = stage(piece, state[piece])


def project(field, gain, attend_in, at, query, key, value):
    rows = pl.ds(at, field.shape[0])
    normed = normalize(field, gain)
    query[rows, :] = (product(normed, attend_in[:, :D]) * QSCALE).astype(BF16)
    key[rows, :] = product(normed, attend_in[:, D : 2 * D]).astype(BF16)
    value[rows, :] = product(normed, attend_in[:, 2 * D :]).astype(BF16)


def set_bias(bias, bands, masks):
    cells = bands.shape[1]
    classes = lax.broadcasted_iota(jnp.int32, (CLASSES, cells), 0).astype(F32)
    one_hot = (classes == bands).astype(F32).astype(BF16)
    same = lax.dot_general(one_hot, one_hot, TRANSPOSED_LEFT, preferred_element_type=F32)
    asking = lax.broadcasted_iota(jnp.int32, (cells, cells), 0)
    asked = lax.broadcasted_iota(jnp.int32, (cells, cells), 1)
    allowed = (same > 0.5) & ((masks > 0.5) | (asking == asked))
    bias[...] = jnp.where(allowed, 0.0, -1e30)


def attend(query, key, value, bias, context, low, count):
    first = lax.broadcasted_iota(jnp.int32, (1, 2 * HD), 1) < HD
    rows = pl.ds(low, count)
    sums = {}

    def lanes(unit):
        return slice(2 * HD * (unit // 2), 2 * HD * (unit // 2 + 1))

    def own(unit, inside, outside):
        return jnp.where(first, inside, outside) if unit % 2 == 0 else jnp.where(first, outside, inside)

    def score(unit, _):
        queries = query[rows, lanes(unit)]
        queries = own(unit, queries, jnp.zeros_like(queries))
        scores = lax.dot_general(
            queries, key[:, lanes(unit)], TRANSPOSED_RIGHT, preferred_element_type=F32
        )
        return scores + bias[rows, :]

    def weigh(unit, scores):
        return jnp.exp2(scores - jnp.max(scores, -1, keepdims=True)).astype(BF16)

    def gather(unit, weights):
        values = value[:, lanes(unit)]
        sums[unit] = product(weights, own(unit, values, jnp.ones_like(values)))
        if unit % 2 == 1:
            even, odd = sums.pop(unit - 1), sums.pop(unit)
            above = jnp.where(first, even, odd)
            below = pltpu.roll(jnp.where(first, odd, even), HD, 1)
            context[rows, lanes(unit)] = (above / below).astype(BF16)

    in_turn(H, (score, weigh, gather))


def finish(fields, context, low, piece, attend_out, gain, expand, contract, write):
    def start(index, _):
        rows = pl.ds(low + index * piece, piece)
        added = fields[index] + product(context[rows, :], attend_out[...])
        resid = added.astype(BF16).astype(F32)
        return resid, normalize(resid, gain)

    def widen(index, state):
        return state[0], product(state[1], expand[...])

    def bend(index, state):
        return state[0], gelu(state[1]).astype(BF16)

    def end(index, state):
        write(index, state[0] + product(state[1], contract[...]))

    in_turn(len(fields), (start, widen, bend, end))


def pack_main_kernel(block_hbm, valid_hbm, main, block, valid, sems):
    height = block_hbm.shape[0]
    rows = height - 2 * SH
    copies = (
        pltpu.make_async_copy(valid_hbm, valid, sems.at[0]),
        pltpu.make_async_copy(block_hbm.at[pl.ds(SH, rows)], block, sems.at[1]),
    )
    for copy in copies:
        copy.start()
    copies[0].wait()
    masks = mask_lanes(valid, SH, 0, D)
    main[pl.ds(rows * SW, META), :] = meta_rows(masks, jnp.zeros_like(masks))
    copies[1].wait()
    main[pl.ds(0, rows * SW), :] = half_columns(block[...], 0).astype(BF16)


def early_kernel(
    block, bands, valid, main, gains, attend_in,
    side, corner, row_end, query, key, value,
):
    height = block.shape[0]
    rows = height - 2 * SH
    places = ((side, height - SH, 0), (corner, 0, 0), (row_end, 0, SW))
    for out, low, column in places:
        cells = SH * SW
        out[pl.ds(0, cells), :] = half_columns(block[low : low + SH], column).astype(BF16)
        masks = mask_lanes(valid, low, column, D)
        out[pl.ds(cells, META), :] = meta_rows(masks, band_lanes(bands, low, SH, D))
    local = half_columns(block[SH:], SW)
    project(local, gains[0:1], attend_in, 0, query, key, value)


def window_a_kernel(
    block, bands, valid, taken, near_query, near_key, near_value,
    gains, attend_in, attend_out, expand, contract,
    away, home, query, key, value, bias, context,
):
    height = block.shape[0]
    rows = height - 2 * SH
    cells = rows * SW
    for near, whole in ((near_query, query), (near_key, key), (near_value, value)):
        whole[pl.ds(0, cells), :] = near[pl.ds(0, cells), :]
    local = half_columns(block[SH : SH + rows], SW)
    remote = taken[pl.ds(0, cells), :].astype(F32)
    project(remote, gains[0:1], attend_in, cells, query, key, value)
    row_bands = band_lanes(bands, SH, rows, cells)
    masks, _ = meta_of(taken, cells)
    set_bias(
        bias,
        jnp.concatenate([row_bands, row_bands], 1),
        jnp.concatenate([mask_lanes(valid, SH, SW, cells), masks], 1),
    )
    attend(query, key, value, bias, context, 0, 2 * cells)

    def write(index, out):
        (home, away)[index][...] = out.astype(BF16)

    finish([local, remote], context, 0, cells, attend_out, gains[1:2], expand, contract, write)


def window_b_away_kernel(
    bands, valid, taken_side, taken_corner, taken_end, near_query, near_key, near_value,
    gains, attend_in, attend_out, expand, contract,
    away_side, away_corner, query, key, value, bias, context,
):
    height = bands.shape[0]
    cells = SH * SW
    for near, whole in ((near_query, query), (near_key, key), (near_value, value)):
        whole[pl.ds(0, cells), :] = near[pl.ds(near.shape[0] - cells, cells), :]
    fields = []
    bands_here = [band_lanes(bands, height - SH, SH, cells)]
    masks_here = [mask_lanes(valid, height - SH, SW, cells)]
    for taken in (taken_end, taken_side, taken_corner):
        fields.append(taken[pl.ds(0, cells), :].astype(F32))
        masks, row_bands = meta_of(taken, cells)
        masks_here.append(masks)
        bands_here.append(row_bands)
    project(jnp.concatenate(fields, 0), gains[0:1], attend_in, cells, query, key, value)
    set_bias(bias, jnp.concatenate(bands_here, 1), jnp.concatenate(masks_here, 1))
    attend(query, key, value, bias, context, 2 * cells, 2 * cells)

    def write(index, out):
        (away_side, away_corner)[index][...] = out.astype(BF16)

    finish(fields[1:], context, 2 * cells, cells, attend_out, gains[1:2], expand, contract, write)


def window_b_home_kernel(
    block, taken_end, query, key, value, bias, gains, attend_out, expand, contract,
    home_side, home_end, context,
):
    height = block.shape[0]
    cells = SH * SW
    attend(query, key, value, bias, context, 0, 2 * cells)
    fields = [half_columns(block[height - SH :], SW), taken_end[pl.ds(0, cells), :].astype(F32)]

    def write(index, out):
        (home_side, home_end)[index][...] = out.astype(BF16)

    finish(fields, context, 0, cells, attend_out, gains[1:2], expand, contract, write)


def second_early_kernel(
    home, home_side, near_end, far, bands, valid, gains, attend_in,
    query, key, value, bias,
):
    part = SH * SW
    low, high = slice(0, part), slice(part, 2 * part)
    windows = ((near_end[...], home[low], far[low]), (home[high], home_side[...], far[high]))
    for index, parts in enumerate(windows):
        field = jnp.concatenate([piece.astype(F32) for piece in parts], 0)
        project(field, gains[0:1], attend_in, 0, query.at[index], key.at[index], value.at[index])
        row = index * WH
        row_bands = band_lanes(bands, row, WH, 2 * part)
        near_masks = mask_lanes(valid, row, SW, 2 * part)
        far_masks = mask_lanes(valid, row, 0, 2 * part)
        far_bands = row_bands
        if index == 0:
            far_bands = jnp.concatenate([row_bands[:, part:], row_bands[:, :part]], 1)
            far_masks = jnp.concatenate([far_masks[:, part:], far_masks[:, :part]], 1)
        set_bias(
            bias.at[index],
            jnp.concatenate([row_bands, far_bands], 1),
            jnp.concatenate([near_masks, far_masks], 1),
        )


def second_kernel(
    home, home_side, near_end, far, far_side, far_corner,
    early_query, early_key, early_value, bias,
    gains, attend_in, attend_out, expand, contract,
    out_ref, query, key, value, context,
):
    part = SH * SW
    low, high = slice(0, part), slice(part, 2 * part)
    windows = (
        (near_end[...], home[low], far[low], far_corner[...]),
        (home[high], home_side[...], far[high], far_side[...]),
    )
    windows = [[piece.astype(F32) for piece in parts] for parts in windows]
    late = 3 * part
    for early, whole in ((early_query, query), (early_key, key), (early_value, value)):
        whole[:, pl.ds(0, late), :] = early[:, pl.ds(0, late), :]
    for index, parts in enumerate(windows):
        project(parts[3], gains[0:1], attend_in, late, query.at[index], key.at[index], value.at[index])
    for index in range(len(windows)):
        attend(
            query.at[index], key.at[index], value.at[index], bias.at[index],
            context.at[pl.ds(4 * part * index, 4 * part)], 0, 4 * part,
        )
    fields = [jnp.concatenate(parts[at : at + 2], 0) for parts in windows for at in (0, 2)]
    near = {}

    def write(index, out):
        window = index // 2
        if index % 2 == 0:
            near[window] = out
            return
        if window == 0:
            out = jnp.concatenate([out[part:], out[:part]], 0)
        both = [piece.reshape(WH, SW, D) for piece in (out, near.pop(window))]
        out_ref[pl.ds(window * WH, WH)] = jnp.concatenate(both, 1).astype(BF16)

    finish(fields, context, 0, 2 * part, attend_out, gains[1:2], expand, contract, write)


def call(kernel, name, shapes, specs, scratch, flops, *operands, limit=40):
    size = sum(operand.size * operand.dtype.itemsize for operand in operands)
    shapes = [shape if isinstance(shape, jax.ShapeDtypeStruct) else jax.ShapeDtypeStruct(shape, BF16)
              for shape in shapes]
    return pl.pallas_call(
        kernel,
        out_shape=shapes,
        in_specs=specs,
        out_specs=[VMEM] * len(shapes),
        scratch_shapes=scratch,
        compiler_params=pltpu.CompilerParams(vmem_limit_bytes=limit * 2**20),
        cost_estimate=pl.CostEstimate(flops=flops, bytes_accessed=size, transcendentals=0),
        name=name,
    )(*operands)


def on_device(
    atmosphere, pole_band, key_valid, norm_gains, attend_in, attend_out, expand, contract
):
    height, breadth = atmosphere.shape[0], atmosphere.shape[1]
    assert height == 2 * WH and breadth == WW
    lons, lats = lax.axis_size("lon"), lax.axis_size("lat")

    def moved(value, lon_step, lat_step):
        pairs = [
            (lon * lats + lat, (lon + lon_step) % lons * lats + (lat + lat_step) % lats)
            for lon in range(lons)
            for lat in range(lats)
        ]
        return lax.ppermute(value, ("lon", "lat"), pairs)

    cells = WH * WW
    half, quarter = cells // 2, cells // 4
    wide = pltpu.VMEM((cells, D), BF16)
    bias_shape = jax.ShapeDtypeStruct((cells, cells), F32)
    bias_scratch = pltpu.VMEM((cells, cells), F32)
    hidden = expand.shape[-1]
    each = 2 * D * 3 * D
    flops = cells * 2 * D * (D + 2 * hidden) + 4 * cells * cells * D

    valid = key_valid.T
    main = call(
        pack_main_kernel, "pack_main", [(half + META, D)], [HBM] * 2,
        [pltpu.VMEM((WH, breadth, D), BF16), pltpu.VMEM(valid.shape, valid.dtype),
         pltpu.SemaphoreType.DMA((2,))],
        10**6, atmosphere, valid, limit=62,
    )[0]
    far_main = moved(main, -1, 0)

    weights = [
        (norm_gains[k], attend_in[k], attend_out[k], expand[k], contract[k]) for k in range(2)
    ]
    side, corner, row_end, *near = call(
        early_kernel, "early", [(quarter + META, D)] * 3 + [(half + quarter, D)] * 3,
        [VMEM, SMEM] + [VMEM] * 4, [], each * (half + quarter),
        atmosphere, pole_band, valid, main, *weights[0][:2],
    )
    far_side = moved(side, -1, 0)
    far_corner = moved(corner, -1, -1)
    near_end = moved(row_end, 0, -1)

    away, home = call(
        window_a_kernel, "window_a", [(half, D)] * 2, [VMEM, SMEM] + [VMEM] * 10,
        [wide] * 3 + [bias_scratch, wide], flops + each * half,
        atmosphere, pole_band, valid, far_main, *near, *weights[0],
    )
    back_main = moved(away, 1, 0)
    away_side, away_corner, *inside = call(
        window_b_away_kernel, "window_b_away",
        [(quarter, D)] * 2 + [(cells, D)] * 3 + [bias_shape], [SMEM] + [VMEM] * 12,
        [wide], flops // 2 + each * 3 * quarter,
        pole_band, valid, far_side, far_corner, near_end, *near, *weights[0],
    )
    back_side = moved(away_side, 1, 0)
    back_corner = moved(away_corner, 1, 1)
    home_side, home_end = call(
        window_b_home_kernel, "window_b_home", [(quarter, D)] * 2, [VMEM] * 10,
        [wide], flops // 2,
        atmosphere, near_end, *inside, weights[0][0], *weights[0][2:],
    )
    back_end = moved(home_end, 0, 1)
    pair = (2, cells, D)
    inside = call(
        second_early_kernel, "second_early",
        [pair] * 3 + [jax.ShapeDtypeStruct((2, cells, cells), F32)],
        [VMEM] * 4 + [SMEM] + [VMEM] * 3, [], each * 6 * quarter,
        home, home_side, back_end, back_main, pole_band, valid, *weights[1][:2],
    )
    return call(
        second_kernel, "second", [(height, breadth, D)], [VMEM] * 15,
        [pltpu.VMEM(pair, BF16)] * 3 + [pltpu.VMEM((2 * cells, D), BF16)],
        2 * flops + each * 2 * quarter,
        home, home_side, back_end, back_main, back_side, back_corner, *inside, *weights[1],
    )[0]


def solution(mesh):
    in_specs = (
        P(("groups", "lat"), "lon", None),
        P(("groups", "lat")),
        P(("groups", "lat"), "lon"),
        P(),
        P(),
        P(),
        P(),
        P(),
    )
    out_specs = P(("groups", "lat"), "lon", None)
    return jax.shard_map(
        on_device, mesh=mesh, in_specs=in_specs, out_specs=out_specs, check_vma=False
    )
```

time: 60.2 us -> 51.8 us (0.86)
  waiting for transfers between devices: 14 us -> 6.98 us
  local copies, waits for them, and re-layouts: 7.56 us -> 4.61 us
  Pallas kernels: 26.6 us -> 28.7 us
    ppermute x8, waiting for transfers between devices: 14 us -> 6.98 us  [moved(): return lax.ppermute(value, ('lon', 'lat'), pairs)]
    unnamed x15 -> x14, local copies, waits for them, and re-layouts: 5.44 us -> 1.34 us
    pallas_call x4 -> x7, Pallas kernels: 26.6 us -> 28.7 us  [call(): pl.pallas_call(kernel, out_shape=shapes, in_specs=specs, out_specs=[VMEM]...]
    squeeze x1, local copies, waits for them, and re-layouts: 0.2 us -> 2.19 us  [on_device(): attend_in[k]]
    squeeze x1, local copies, waits for them, and re-layouts: 1.71 us -> 0.17 us  [on_device(): expand[k]]
    squeeze x1, local copies, waits for them, and re-layouts: 0.01 us -> 0.7 us  [on_device(): norm_gains[k]]
  transfers between devices with their start and end apart: 8 -> 8, of which waited for: 3 -> 3; matrix products, arithmetic and copies ran while one was open for 4% -> 6% of each run, Pallas kernels for 22% -> 33%
where the time goes in v2:
time: 51.8 us; the launch traced here: 51.5 us
  Pallas kernels  28.7 us (55%)
  starting transfers between devices  11.1 us (21%)
  waiting for transfers between devices  6.98 us (13%)
  local copies, waits for them, and re-layouts  4.61 us (9%)
    pallas_call x7, Pallas kernels, call(): pl.pallas_call(kernel, out_shape=shapes, in_specs=specs, out_specs=[VMEM]...  28.7 us
    ppermute x8, starting transfers between devices, moved(): return lax.ppermute(value, ('lon', 'lat'), pairs)  11.1 us
    ppermute x8, waiting for transfers between devices, moved(): return lax.ppermute(value, ('lon', 'lat'), pairs)  6.98 us
    squeeze x1, local copies, waits for them, and re-layouts, on_device(): attend_in[k]  2.19 us
    unnamed x14, local copies, waits for them, and re-layouts  1.34 us
  transfers between devices with their start and end apart: 8, of which 3 were waited for; matrix products, arithmetic and copies ran while one was open for 6% of the time, Pallas kernels for 33%

profile of v2, /device:TPU:0, one launch (start us, length us, event | category | flops | bytes accessed | tf_op | source)
XLA Modules:
  0.0 51.5 jit_solution(3124808946817447647)
XLA Ops:
  0.0 1.8 %pack_main.1.main = bf16[272,512]{1,0:T(8,128)(2,1)} custom-call(bf16[64,16,512]{2,1,0:T(8,128)(2,1)} %block.5, s32[16,64]{1,0:T(8,128)} %bitcast.21), custom_call_target="tpu_custom_call" | custom-call | flops 1000000 | bytes 1052672 | tf_op jit(solution)/shard_map/pack_main/pallas_call | solution.py:336
  1.8 6.1 %collective-permute-start = (bf16[272,512]{1,0:T(8,128)(2,1)}, bf16[272,512]{1,0:T(8,128)(2,1)S(1)}, u32[]{:S(2)}, u32[]{:S(2)}) collective-permute-start(bf16[272,512]{1,0:T(8,128)(2,1)} %pack_main.1.main), channel_id=1, source_target_pairs={{0,14},{1,15},{2,0},{3,1},{4,2},{5,3},{6,4},{7,5},{8,6},{9,7},{10,... | collective-permute-start | bytes 835592 | tf_op jit(solution)/shard_map/ppermute | solution.py:361
  7.9 0.7 %slice_bitcast_fusion.8 = (f32[2,512]{1,0:T(2,128)S(1)}, f32[2,512]{1,0:T(2,128)S(1)}) fusion(f32[2,2,512]{2,1,0:T(2,128)} %param.11), kind=kLoop, calls=%fused_computation.8 | loop fusion | bytes 16384 | tf_op jit(solution)/shard_map/squeeze | solution.py:382
  8.6 2.2 %slice_bitcast_fusion = (bf16[512,1536]{1,0:T(8,128)(2,1)S(1)}, bf16[512,1536]{1,0:T(8,128)(2,1)S(1)}) fusion(bf16[2,512,1536]{2,1,0:T(8,128)(2,1)} %param.12), kind=kLoop, calls=%fused_computation | loop fusion | bytes 6291456 | tf_op jit(solution)/shard_map/squeeze | solution.py:382
  10.8 1.6 %early.1 = (bf16[144,512]{1,0:T(8,128)(2,1)S(1)}, bf16[144,512]{1,0:T(8,128)(2,1)S(1)}, bf16[144,512]{1,0:T(8,128)(2,1)S(1)}, bf16[384,512]{1,0:T(8,128)(2,1)S(1...) custom-call(bf16[64,16,512]{2,1,0:T(8,128)(2,1)S(1)} %copy-done, s32[64]{0:T(128)S(1)} %copy-done.3, ...), custom_call_target="tpu_custom_call" | custom-call | flops 603979776 | bytes 2908416 | tf_op jit(solution)/shard_map/early/pallas_call | solution.py:336
  12.4 0.1 collective-permute-start.1
  12.5 0.5 %collective-permute-start.2 = (bf16[144,512]{1,0:T(8,128)(2,1)S(1)}, bf16[144,512]{1,0:T(8,128)(2,1)S(1)}, u32[]{:S(2)}, u32[]{:S(2)}) collective-permute-start(bf16[144,512]{1,0:T(8,128)(2,1)S(1)} %get-tuple-element.30), channel_id=1, source_target_pairs={{0,14},{1,15},{2,0},{3,1},{4,2},{5,3},{6,4},{7,5},{8,6},{9,7},{10,... | collective-permute-start | bytes 442376 | tf_op jit(solution)/shard_map/ppermute | solution.py:361
  13.0 1.2 %collective-permute-start.3 = (bf16[144,512]{1,0:T(8,128)(2,1)S(1)}, bf16[144,512]{1,0:T(8,128)(2,1)S(1)}, u32[]{:S(2)}, u32[]{:S(2)}) collective-permute-start(bf16[144,512]{1,0:T(8,128)(2,1)S(1)} %get-tuple-element.31), channel_id=1, source_target_pairs={{0,15},{1,14},{2,1},{3,0},{4,3},{5,2},{6,5},{7,4},{8,7},{9,6},{10,... | collective-permute-start | bytes 442376 | tf_op jit(solution)/shard_map/ppermute | solution.py:361
  14.2 0.1 slice_bitcast_fusion.2
  14.4 0.3 copy-done.5
  14.6 0.2 slice_bitcast_fusion.3
  14.8 1.0 %copy-done.6 = bf16[2,512,512]{2,1,0:T(8,128)(2,1)S(1)} copy-done((bf16[2,512,512]{2,1,0:T(8,128)(2,1)S(1)}, bf16[2,512,512]{2,1,0:T(8,128)(2,1)}, u32[]{:S(2)}) %copy-start.6) | copy-done | bytes 1048600
  15.9 5.9 %window_a.1 = (bf16[256,512]{1,0:T(8,128)(2,1)S(1)}, bf16[256,512]{1,0:T(8,128)(2,1)S(1)}) custom-call(bf16[64,16,512]{2,1,0:T(8,128)(2,1)S(1)} %copy-done, s32[64]{0:T(128)S(1)} %copy-done.3, s32[16,64]{1,0:T(8,128)S(1)} %bitcast.23, bf16[272,512]{1,0:T(8,128)(2,1)S(1)} %collective-permute-done.taken, bf16[384,512]{1,0:T(8,128)(2,1)S(1)} %get-tuple-element.25.near_query, ...), custom_call_target="tpu_custom_call" | custom-call | flops 2281701376 | bytes 6709504 | tf_op jit(solution)/shard_map/window_a/pallas_call | solution.py:336
  21.8 1.8 %collective-permute-start.5 = (bf16[256,512]{1,0:T(8,128)(2,1)S(1)}, bf16[256,512]{1,0:T(8,128)(2,1)S(1)}, u32[]{:S(2)}, u32[]{:S(2)}) collective-permute-start(bf16[256,512]{1,0:T(8,128)(2,1)S(1)} %get-tuple-element.38), channel_id=1, source_target_pairs={{0,2},{1,3},{2,4},{3,5},{4,6},{5,7},{6,8},{7,9},{8,10},{9,11},{10,... | collective-permute-start | bytes 786440 | tf_op jit(solution)/shard_map/ppermute | solution.py:361
  23.6 4.2 %window_b_away.1 = (bf16[128,512]{1,0:T(8,128)(2,1)S(1)}, bf16[128,512]{1,0:T(8,128)(2,1)S(1)}, bf16[512,512]{1,0:T(8,128)(2,1)S(1)}, bf16[512,512]{1,0:T(8,128)...) custom-call(s32[64]{0:T(128)S(1)} %copy-done.3, s32[16,64]{1,0:T(8,128)S(1)} %bitcast.24, ...), custom_call_target="tpu_custom_call" | custom-call | flops 1543503872 | bytes 5824768 | tf_op jit(solution)/shard_map/window_b_away/pallas_call | solution.py:336
  27.8 2.6 %window_b_home.1 = (bf16[128,512]{1,0:T(8,128)(2,1)S(1)}, bf16[128,512]{1,0:T(8,128)(2,1)S(1)}) custom-call(bf16[64,16,512]{2,1,0:T(8,128)(2,1)S(1)} %copy-done, bf16[144,512]{1,0:T(8,128)(2,1)S(1)} %collective-permute-done.1.taken_end, bf16[512,512]{1,0:T(8,128)(2,1)S(1)} %get-tuple-element.32.query, bf16[512,512]{1,0:T(8,128)(2,1)S(1)} %get-tuple-element.33.key, ...), custom_call_target="tpu_custom_call" | custom-call | flops 939524096 | bytes 6443008 | tf_op jit(solution)/shard_map/window_b_home/pallas_call | solution.py:336
  30.3 0.1 collective-permute-start.4
  30.4 1.3 %collective-permute-start.6 = (bf16[128,512]{1,0:T(8,128)(2,1)S(1)}, bf16[128,512]{1,0:T(8,128)(2,1)S(1)}, u32[]{:S(2)}, u32[]{:S(2)}) collective-permute-start(bf16[128,512]{1,0:T(8,128)(2,1)S(1)} %get-tuple-element.39), channel_id=1, source_target_pairs={{0,2},{1,3},{2,4},{3,5},{4,6},{5,7},{6,8},{7,9},{8,10},{9,11},{10,... | collective-permute-start | bytes 393224 | tf_op jit(solution)/shard_map/ppermute | solution.py:361
  31.7 0.1 collective-permute-start.7
  31.8 1.3 %collective-permute-done.5.far = bf16[256,512]{1,0:T(8,128)(2,1)S(1)} collective-permute-done((bf16[256,512]{1,0:T(8,128)(2,1)S(1)}, bf16[256,512]{1,0:T(8,128)(2,1)S(1)}, u32[]{:S(2)}, u32[]{:S(2)}) %collective-permute-start.5) | collective-permute-done | bytes 262176 | tf_op jit(solution)/shard_map/ppermute | solution.py:361
  33.1 2.6 %second_early.1 = (bf16[2,512,512]{2,1,0:T(8,128)(2,1)S(1)}, bf16[2,512,512]{2,1,0:T(8,128)(2,1)S(1)}, bf16[2,512,512]{2,1,0:T(8,128)(2,1)S(1)}, f32[2,512,512]{2,1,0:T(8,128)S(1)}) custom-call(bf16[256,512]{1,0:T(8,128)(2,1)S(1)} %get-tuple-element.28.home, bf16[128,512]{1,0:T(8,128)(2,1)S(1)} %get-tuple-element.36.home_side, ...), custom_call_target="tpu_custom_call" | custom-call | flops 1207959552 | bytes 2367744 | tf_op jit(solution)/shard_map/second_early/pallas_call | solution.py:336
  35.7 3.8 %collective-permute-done.6.far_side = bf16[128,512]{1,0:T(8,128)(2,1)S(1)} collective-permute-done((bf16[128,512]{1,0:T(8,128)(2,1)S(1)}, bf16[128,512]{1,0:T(8,128)(2,1)S(1)}, u32[]{:S(2)}, u32[]{:S(2)}) %collective-permute-start.6) | collective-permute-done | bytes 131104 | tf_op jit(solution)/shard_map/ppermute | solution.py:361
  39.5 1.9 %collective-permute-done.7.far_corner = bf16[128,512]{1,0:T(8,128)(2,1)S(1)} collective-permute-done((bf16[128,512]{1,0:T(8,128)(2,1)S(1)}, bf16[128,512]{1,0:T(8,128)(2,1)S(1)}, u32[]{:S(2)}, u32[]{:S(2)}) %collective-permute-start.7) | collective-permute-done | bytes 131104 | tf_op jit(solution)/shard_map/ppermute | solution.py:361
  41.4 10.1 %second.1 = bf16[64,16,512]{2,1,0:T(8,128)(2,1)} custom-call(bf16[256,512]{1,0:T(8,128)(2,1)S(1)} %get-tuple-element.28.home, bf16[128,512]{1,0:T(8,128)(2,1)S(1)} %get-tuple-element.36.home_side, bf16[128,512]{1,0:T(8,128)(2,1)S(1)} %collective-permute-done.4.near_end, bf16[256,512]{1,0:T(8,128)(2,1)S(1)} %collective-permute-done.5.far, ...), custom_call_target="tpu_custom_call" | custom-call | flops 4160749568 | bytes 10489856 | tf_op jit(solution)/shard_map/second/pallas_call | solution.py:336
  (18 shorter events, 0.1 us)
Async XLA Ops:
  1.8 14.1 %collective-permute-start = (bf16[272,512]{1,0:T(8,128)(2,1)}, bf16[272,512]{1,0:T(8,128)(2,1)S(1)}, u32[]{:S(2)}, u32[]{:S(2)}) collective-permute-start(bf16[272,512]{1,0:T(8,128)(2,1)} %pack_main.1.main), channel_id=1, source_target_pairs={{0,14},{1,15},{2,0},{3,1},{4,2},{5,3},{6,4},{7,5},{8,6},{9,7},{10,... | collective-permute-start | bytes 835592 | tf_op jit(solution)/shard_map/ppermute | solution.py:361
  8.6 2.2 %copy-start = (bf16[64,16,512]{2,1,0:T(8,128)(2,1)S(1)}, bf16[64,16,512]{2,1,0:T(8,128)(2,1)}, u32[]{:S(2)}) copy-start(bf16[64,16,512]{2,1,0:T(8,128)(2,1)} %block.5) | copy-start | bytes 3145732
  8.6 2.2 %copy-start.1 = (bf16[272,512]{1,0:T(8,128)(2,1)S(1)}, bf16[272,512]{1,0:T(8,128)(2,1)}, u32[]{:S(2)}) copy-start(bf16[272,512]{1,0:T(8,128)(2,1)} %pack_main.1.main) | copy-start | bytes 835588
  8.6 2.2 %copy-start.2 = (s32[64,16]{0,1:T(8,128)S(1)}, s32[64,16]{0,1:T(8,128)}, u32[]{:S(2)}) copy-start(s32[64,16]{0,1:T(8,128)} %param.10) | copy-start | bytes 12292
  8.6 2.2 %copy-start.3 = (s32[64]{0:T(128)S(1)}, s32[64]{0:T(128)}, u32[]{:S(2)}) copy-start(s32[64]{0:T(128)} %bands.7) | copy-start | bytes 772
  10.8 3.4 %copy-start.4 = (bf16[2,1024,512]{2,1,0:T(8,128)(2,1)S(1)}, bf16[2,1024,512]{2,1,0:T(8,128)(2,1)}, u32[]{:S(2)}) copy-start(bf16[2,1024,512]{2,1,0:T(8,128)(2,1)} %param.15) | copy-start | bytes 6291460
  12.4 11.2 %collective-permute-start.1 = (bf16[144,512]{1,0:T(8,128)(2,1)S(1)}, bf16[144,512]{1,0:T(8,128)(2,1)S(1)}, u32[]{:S(2)}, u32[]{:S(2)}) collective-permute-start(bf16[144,512]{1,0:T(8,128)(2,1)S(1)} %get-tuple-element.29), channel_id=1, source_target_pairs={{0,1},{1,0},{2,3},{3,2},{4,5},{5,4},{6,7},{7,6},{8,9},{9,8},{10,11... | collective-permute-start | bytes 442376 | tf_op jit(solution)/shard_map/ppermute | solution.py:361
  12.5 11.1 %collective-permute-start.2 = (bf16[144,512]{1,0:T(8,128)(2,1)S(1)}, bf16[144,512]{1,0:T(8,128)(2,1)S(1)}, u32[]{:S(2)}, u32[]{:S(2)}) collective-permute-start(bf16[144,512]{1,0:T(8,128)(2,1)S(1)} %get-tuple-element.30), channel_id=1, source_target_pairs={{0,14},{1,15},{2,0},{3,1},{4,2},{5,3},{6,4},{7,5},{8,6},{9,7},{10,... | collective-permute-start | bytes 442376 | tf_op jit(solution)/shard_map/ppermute | solution.py:361
  13.0 1.6 %copy-start.5 = (bf16[2,512,1024]{2,1,0:T(8,128)(2,1)S(1)}, bf16[2,512,1024]{2,1,0:T(8,128)(2,1)}, u32[]{:S(2)}) copy-start(bf16[2,512,1024]{2,1,0:T(8,128)(2,1)} %param.14) | copy-start | bytes 6291460
  13.0 10.5 %collective-permute-start.3 = (bf16[144,512]{1,0:T(8,128)(2,1)S(1)}, bf16[144,512]{1,0:T(8,128)(2,1)S(1)}, u32[]{:S(2)}, u32[]{:S(2)}) collective-permute-start(bf16[144,512]{1,0:T(8,128)(2,1)S(1)} %get-tuple-element.31), channel_id=1, source_target_pairs={{0,15},{1,14},{2,1},{3,0},{4,3},{5,2},{6,5},{7,4},{8,7},{9,6},{10,... | collective-permute-start | bytes 442376 | tf_op jit(solution)/shard_map/ppermute | solution.py:361
  14.6 1.2 %copy-start.6 = (bf16[2,512,512]{2,1,0:T(8,128)(2,1)S(1)}, bf16[2,512,512]{2,1,0:T(8,128)(2,1)}, u32[]{:S(2)}) copy-start(bf16[2,512,512]{2,1,0:T(8,128)(2,1)} %param.13) | copy-start | bytes 3145732
  21.8 11.3 %collective-permute-start.5 = (bf16[256,512]{1,0:T(8,128)(2,1)S(1)}, bf16[256,512]{1,0:T(8,128)(2,1)S(1)}, u32[]{:S(2)}, u32[]{:S(2)}) collective-permute-start(bf16[256,512]{1,0:T(8,128)(2,1)S(1)} %get-tuple-element.38), channel_id=1, source_target_pairs={{0,2},{1,3},{2,4},{3,5},{4,6},{5,7},{6,8},{7,9},{8,10},{9,11},{10,... | collective-permute-start | bytes 786440 | tf_op jit(solution)/shard_map/ppermute | solution.py:361
  30.3 1.5 %collective-permute-start.4 = (bf16[128,512]{1,0:T(8,128)(2,1)S(1)}, bf16[128,512]{1,0:T(8,128)(2,1)S(1)}, u32[]{:S(2)}, u32[]{:S(2)}) collective-permute-start(bf16[128,512]{1,0:T(8,128)(2,1)S(1)} %get-tuple-element.37), channel_id=1, source_target_pairs={{0,1},{1,0},{2,3},{3,2},{4,5},{5,4},{6,7},{7,6},{8,9},{9,8},{10,11... | collective-permute-start | bytes 393224 | tf_op jit(solution)/shard_map/ppermute | solution.py:361
  30.4 9.0 %collective-permute-start.6 = (bf16[128,512]{1,0:T(8,128)(2,1)S(1)}, bf16[128,512]{1,0:T(8,128)(2,1)S(1)}, u32[]{:S(2)}, u32[]{:S(2)}) collective-permute-start(bf16[128,512]{1,0:T(8,128)(2,1)S(1)} %get-tuple-element.39), channel_id=1, source_target_pairs={{0,2},{1,3},{2,4},{3,5},{4,6},{5,7},{6,8},{7,9},{8,10},{9,11},{10,... | collective-permute-start | bytes 393224 | tf_op jit(solution)/shard_map/ppermute | solution.py:361
  31.7 9.6 %collective-permute-start.7 = (bf16[128,512]{1,0:T(8,128)(2,1)S(1)}, bf16[128,512]{1,0:T(8,128)(2,1)S(1)}, u32[]{:S(2)}, u32[]{:S(2)}) collective-permute-start(bf16[128,512]{1,0:T(8,128)(2,1)S(1)} %get-tuple-element.40), channel_id=1, source_target_pairs={{0,3},{1,2},{2,5},{3,4},{4,7},{5,6},{6,9},{7,8},{8,11},{9,10},{10,... | collective-permute-start | bytes 393224 | tf_op jit(solution)/shard_map/ppermute | solution.py:361

commit v3 on v2

--- a/solution.py
+++ b/solution.py
@@ -183,6 +183,7 @@
     block, bands, valid, main, gains, attend_in,
     side, corner, row_end, query, key, value,
 ):
+    gains, attend_in = (ref.at[0] for ref in (gains, attend_in))
     height = block.shape[0]
     rows = height - 2 * SH
     places = ((side, height - SH, 0), (corner, 0, 0), (row_end, 0, SW))
@@ -200,6 +201,7 @@
     gains, attend_in, attend_out, expand, contract,
     away, home, query, key, value, bias, context,
 ):
+    gains, attend_in, attend_out, expand, contract = (ref.at[0] for ref in (gains, attend_in, attend_out, expand, contract))
     height = block.shape[0]
     rows = height - 2 * SH
     cells = rows * SW
@@ -228,6 +230,7 @@
     gains, attend_in, attend_out, expand, contract,
     away_side, away_corner, query, key, value, bias, context,
 ):
+    gains, attend_in, attend_out, expand, contract = (ref.at[0] for ref in (gains, attend_in, attend_out, expand, contract))
     height = bands.shape[0]
     cells = SH * SW
     for near, whole in ((near_query, query), (near_key, key), (near_value, value)):
@@ -254,6 +257,7 @@
     block, taken_end, query, key, value, bias, gains, attend_out, expand, contract,
     home_side, home_end, context,
 ):
+    gains, attend_out, expand, contract = (ref.at[0] for ref in (gains, attend_out, expand, contract))
     height = block.shape[0]
     cells = SH * SW
     attend(query, key, value, bias, context, 0, 2 * cells)
@@ -269,6 +273,7 @@
     home, home_side, near_end, far, bands, valid, gains, attend_in,
     query, key, value, bias,
 ):
+    gains, attend_in = (ref.at[1] for ref in (gains, attend_in))
     part = SH * SW
     low, high = slice(0, part), slice(part, 2 * part)
     windows = ((near_end[...], home[low], far[low]), (home[high], home_side[...], far[high]))
@@ -296,6 +301,7 @@
     gains, attend_in, attend_out, expand, contract,
     out_ref, query, key, value, context,
 ):
+    gains, attend_in, attend_out, expand, contract = (ref.at[1] for ref in (gains, attend_in, attend_out, expand, contract))
     part = SH * SW
     low, high = slice(0, part), slice(part, 2 * part)
     windows = (
@@ -330,7 +336,7 @@
 
 
 def call(kernel, name, shapes, specs, scratch, flops, *operands, limit=40):
-    size = sum(operand.size * operand.dtype.itemsize for operand in operands)
+    flops = 1
     shapes = [shape if isinstance(shape, jax.ShapeDtypeStruct) else jax.ShapeDtypeStruct(shape, BF16)
               for shape in shapes]
     return pl.pallas_call(
@@ -340,7 +346,7 @@
         out_specs=[VMEM] * len(shapes),
         scratch_shapes=scratch,
         compiler_params=pltpu.CompilerParams(vmem_limit_bytes=limit * 2**20),
-        cost_estimate=pl.CostEstimate(flops=flops, bytes_accessed=size, transcendentals=0),
+        cost_estimate=pl.CostEstimate(flops=flops, bytes_accessed=flops, transcendentals=0),
         name=name,
     )(*operands)
 
@@ -378,13 +384,11 @@
     )[0]
     far_main = moved(main, -1, 0)
 
-    weights = [
-        (norm_gains[k], attend_in[k], attend_out[k], expand[k], contract[k]) for k in range(2)
-    ]
+    weights = (norm_gains, attend_in, attend_out, expand, contract)
     side, corner, row_end, *near = call(
         early_kernel, "early", [(quarter + META, D)] * 3 + [(half + quarter, D)] * 3,
         [VMEM, SMEM] + [VMEM] * 4, [], each * (half + quarter),
-        atmosphere, pole_band, valid, main, *weights[0][:2],
+        atmosphere, pole_band, valid, main, *weights[:2],
     )
     far_side = moved(side, -1, 0)
     far_corner = moved(corner, -1, -1)
@@ -393,21 +397,21 @@
     away, home = call(
         window_a_kernel, "window_a", [(half, D)] * 2, [VMEM, SMEM] + [VMEM] * 10,
         [wide] * 3 + [bias_scratch, wide], flops + each * half,
-        atmosphere, pole_band, valid, far_main, *near, *weights[0],
+        atmosphere, pole_band, valid, far_main, *near, *weights,
     )
     back_main = moved(away, 1, 0)
     away_side, away_corner, *inside = call(
         window_b_away_kernel, "window_b_away",
         [(quarter, D)] * 2 + [(cells, D)] * 3 + [bias_shape], [SMEM] + [VMEM] * 12,
         [wide], flops // 2 + each * 3 * quarter,
-        pole_band, valid, far_side, far_corner, near_end, *near, *weights[0],
+        pole_band, valid, far_side, far_corner, near_end, *near, *weights,
     )
     back_side = moved(away_side, 1, 0)
     back_corner = moved(away_corner, 1, 1)
     home_side, home_end = call(
         window_b_home_kernel, "window_b_home", [(quarter, D)] * 2, [VMEM] * 10,
         [wide], flops // 2,
-        atmosphere, near_end, *inside, weights[0][0], *weights[0][2:],
+        atmosphere, near_end, *inside, weights[0], *weights[2:],
     )
     back_end = moved(home_end, 0, 1)
     pair = (2, cells, D)
@@ -415,13 +419,13 @@
         second_early_kernel, "second_early",
         [pair] * 3 + [jax.ShapeDtypeStruct((2, cells, cells), F32)],
         [VMEM] * 4 + [SMEM] + [VMEM] * 3, [], each * 6 * quarter,
-        home, home_side, back_end, back_main, pole_band, valid, *weights[1][:2],
+        home, home_side, back_end, back_main, pole_band, valid, *weights[:2],
     )
     return call(
         second_kernel, "second", [(height, breadth, D)], [VMEM] * 15,
         [pltpu.VMEM(pair, BF16)] * 3 + [pltpu.VMEM((2 * cells, D), BF16)],
         2 * flops + each * 2 * quarter,
-        home, home_side, back_end, back_main, back_side, back_corner, *inside, *weights[1],
+        home, home_side, back_end, back_main, back_side, back_corner, *inside, *weights,
     )[0]
 
 

time: 51.8 us -> 58.9 us (1.14)
  local copies, waits for them, and re-layouts: 4.61 us -> 9.33 us
  Pallas kernels: 28.7 us -> 31.8 us
  waiting for transfers between devices: 6.98 us -> 5.85 us
    unnamed x14 -> x30, local copies, waits for them, and re-layouts: 1.34 us -> 9.33 us
    squeeze x5 -> x0, local copies, waits for them, and re-layouts: 3.27 us -> none  [the longest x1 2.19 us: on_device(): attend_in[k]]
    pallas_call x7, Pallas kernels: 28.7 us -> 31.8 us  [call(): pl.pallas_call(kernel, out_shape=shapes, in_specs=specs, out_specs=[VMEM]...]
    ppermute x8, waiting for transfers between devices: 6.98 us -> 5.85 us  [moved(): return lax.ppermute(value, ('lon', 'lat'), pairs)]
  transfers between devices with their start and end apart: 8 -> 8, of which waited for: 3 -> 3; matrix products, arithmetic and copies ran while one was open for 6% -> 0% of each run, Pallas kernels for 33% -> 29%
where the time goes in v3:
time: 58.9 us; the launch traced here: 58.4 us
  Pallas kernels  31.8 us (54%)
  starting transfers between devices  11.3 us (19%)
  local copies, waits for them, and re-layouts  9.33 us (16%)
  waiting for transfers between devices  5.85 us (10%)
    pallas_call x7, Pallas kernels, call(): pl.pallas_call(kernel, out_shape=shapes, in_specs=specs, out_specs=[VMEM]...  31.8 us
    ppermute x8, starting transfers between devices, moved(): return lax.ppermute(value, ('lon', 'lat'), pairs)  11.3 us
    unnamed x30, local copies, waits for them, and re-layouts  9.33 us
    ppermute x8, waiting for transfers between devices, moved(): return lax.ppermute(value, ('lon', 'lat'), pairs)  5.85 us
  transfers between devices with their start and end apart: 8, of which 3 were waited for; matrix products, arithmetic and copies ran while one was open for 0% of the time, Pallas kernels for 29%

profile of v3, /device:TPU:0, one launch (start us, length us, event | category | flops | bytes accessed | tf_op | source)
XLA Modules:
  0.0 58.4 jit_solution(11663614117374648308)
XLA Ops:
  0.0 1.8 %pack_main.1.main = bf16[272,512]{1,0:T(8,128)(2,1)} custom-call(bf16[64,16,512]{2,1,0:T(8,128)(2,1)} %block.5, s32[16,64]{1,0:T(8,128)} %bitcast.1), custom_call_target="tpu_custom_call" | custom-call | flops 1 | bytes 1 | tf_op jit(solution)/shard_map/pack_main/pallas_call | solution.py:342
  1.8 6.1 %collective-permute-start = (bf16[272,512]{1,0:T(8,128)(2,1)}, bf16[272,512]{1,0:T(8,128)(2,1)S(1)}, u32[]{:S(2)}, u32[]{:S(2)}) collective-permute-start(bf16[272,512]{1,0:T(8,128)(2,1)} %pack_main.1.main), channel_id=1, source_target_pairs={{0,14},{1,15},{2,0},{3,1},{4,2},{5,3},{6,4},{7,5},{8,6},{9,7},{10,... | collective-permute-start | bytes 835592 | tf_op jit(solution)/shard_map/ppermute | solution.py:367
  7.9 1.9 %copy-done = bf16[2,512,1536]{2,1,0:T(8,128)(2,1)S(1)} copy-done((bf16[2,512,1536]{2,1,0:T(8,128)(2,1)S(1)}, bf16[2,512,1536]{2,1,0:T(8,128)(2,1)}, u32[]{:S(2)}) %copy-start) | copy-done | bytes 3145752
  9.8 1.2 %copy-done.7 = bf16[64,16,512]{2,1,0:T(8,128)(2,1)S(1)} copy-done((bf16[64,16,512]{2,1,0:T(8,128)(2,1)S(1)}, bf16[64,16,512]{2,1,0:T(8,128)(2,1)}, u32[]{:S(2)}) %copy-start.7) | copy-done | bytes 1048600
  11.0 1.0 %copy-done.9 = bf16[272,512]{1,0:T(8,128)(2,1)S(1)} copy-done((bf16[272,512]{1,0:T(8,128)(2,1)S(1)}, bf16[272,512]{1,0:T(8,128)(2,1)}, u32[]{:S(2)}) %copy-start.9) | copy-done | bytes 278552
  11.9 0.7 %copy-done.10 = f32[2,2,512]{2,1,0:T(2,128)S(1)} copy-done((f32[2,2,512]{2,1,0:T(2,128)S(1)}, f32[2,2,512]{2,1,0:T(2,128)}, u32[]{:S(2)}) %copy-start.10) | copy-done | bytes 8216
  12.6 0.7 %copy-done.12 = s32[64,16]{0,1:T(8,128)S(1)} copy-done((s32[64,16]{0,1:T(8,128)S(1)}, s32[64,16]{0,1:T(8,128)}, u32[]{:S(2)}) %copy-start.12) | copy-done | bytes 4120
  13.3 0.7 %copy-done.13 = s32[64]{0:T(128)S(1)} copy-done((s32[64]{0:T(128)S(1)}, s32[64]{0:T(128)}, u32[]{:S(2)}) %copy-start.13) | copy-done | bytes 280
  14.0 1.6 %early.1 = (bf16[144,512]{1,0:T(8,128)(2,1)S(1)}, bf16[144,512]{1,0:T(8,128)(2,1)S(1)}, bf16[144,512]{1,0:T(8,128)(2,1)S(1)}, bf16[384,512]{1,0:T(8,128)(2,1)S(1...) custom-call(bf16[64,16,512]{2,1,0:T(8,128)(2,1)S(1)} %copy-done.7, s32[64]{0:T(128)S(1)} %copy-done.13, ...), custom_call_target="tpu_custom_call" | custom-call | flops 1 | bytes 1 | tf_op jit(solution)/shard_map/early/pallas_call | solution.py:342
  15.7 0.6 collective-permute-start.2
  16.2 1.2 %collective-permute-start.3 = (bf16[144,512]{1,0:T(8,128)(2,1)S(1)}, bf16[144,512]{1,0:T(8,128)(2,1)S(1)}, u32[]{:S(2)}, u32[]{:S(2)}) collective-permute-start(bf16[144,512]{1,0:T(8,128)(2,1)S(1)} %get-tuple-element.31), channel_id=1, source_target_pairs={{0,15},{1,14},{2,1},{3,0},{4,3},{5,2},{6,5},{7,4},{8,7},{9,6},{10,... | collective-permute-start | bytes 442376 | tf_op jit(solution)/shard_map/ppermute | solution.py:367
  17.4 1.6 %copy-done.2 = bf16[2,512,1024]{2,1,0:T(8,128)(2,1)S(1)} copy-done((bf16[2,512,1024]{2,1,0:T(8,128)(2,1)S(1)}, bf16[2,512,1024]{2,1,0:T(8,128)(2,1)}, u32[]{:S(2)}) %copy-start.2) | copy-done | bytes 2097176
  19.0 1.6 %copy-done.4 = bf16[2,1024,512]{2,1,0:T(8,128)(2,1)S(1)} copy-done((bf16[2,1024,512]{2,1,0:T(8,128)(2,1)S(1)}, bf16[2,1024,512]{2,1,0:T(8,128)(2,1)}, u32[]{:S(2)}) %copy-start.4) | copy-done | bytes 2097176
  20.6 6.0 %window_a.1 = (bf16[256,512]{1,0:T(8,128)(2,1)S(1)}, bf16[256,512]{1,0:T(8,128)(2,1)S(1)}) custom-call(bf16[64,16,512]{2,1,0:T(8,128)(2,1)S(1)} %copy-done.7, s32[64]{0:T(128)S(1)} %copy-done.13, s32[16,64]{1,0:T(8,128)S(1)} %bitcast.3, bf16[272,512]{1,0:T(8,128)(2,1)S(1)} %collective-permute-done.taken, bf16[384,512]{1,0:T(8,128)(2,1)S(1)} %get-tuple-element.25.near_query, ...), custom_call_target="tpu_custom_call" | custom-call | flops 1 | bytes 1 | tf_op jit(solution)/shard_map/window_a/pallas_call | solution.py:342
  26.6 0.9 %collective-permute-start.5 = (bf16[256,512]{1,0:T(8,128)(2,1)S(1)}, bf16[256,512]{1,0:T(8,128)(2,1)S(1)}, u32[]{:S(2)}, u32[]{:S(2)}) collective-permute-start(bf16[256,512]{1,0:T(8,128)(2,1)S(1)} %get-tuple-element.38), channel_id=1, source_target_pairs={{0,2},{1,3},{2,4},{3,5},{4,6},{5,7},{6,8},{7,9},{8,10},{9,11},{10,... | collective-permute-start | bytes 786440 | tf_op jit(solution)/shard_map/ppermute | solution.py:367
  27.5 4.3 %window_b_away.1 = (bf16[128,512]{1,0:T(8,128)(2,1)S(1)}, bf16[128,512]{1,0:T(8,128)(2,1)S(1)}, bf16[512,512]{1,0:T(8,128)(2,1)S(1)}, bf16[512,512]{1,0:T(8,128)...) custom-call(s32[64]{0:T(128)S(1)} %copy-done.13, s32[16,64]{1,0:T(8,128)S(1)} %bitcast.4, ...), custom_call_target="tpu_custom_call" | custom-call | flops 1 | bytes 1 | tf_op jit(solution)/shard_map/window_b_away/pallas_call | solution.py:342
  31.8 2.7 %window_b_home.1 = (bf16[128,512]{1,0:T(8,128)(2,1)S(1)}, bf16[128,512]{1,0:T(8,128)(2,1)S(1)}) custom-call(bf16[64,16,512]{2,1,0:T(8,128)(2,1)S(1)} %copy-done.8, bf16[144,512]{1,0:T(8,128)(2,1)S(1)} %collective-permute-done.1.taken_end, bf16[512,512]{1,0:T(8,128)(2,1)S(1)} %get-tuple-element.32.query, bf16[512,512]{1,0:T(8,128)(2,1)S(1)} %get-tuple-element.33.key, ...), custom_call_target="tpu_custom_call" | custom-call | flops 1 | bytes 1 | tf_op jit(solution)/shard_map/window_b_home/pallas_call | solution.py:342
  34.6 0.1 collective-permute-start.4
  34.7 2.4 %collective-permute-start.6 = (bf16[128,512]{1,0:T(8,128)(2,1)S(1)}, bf16[128,512]{1,0:T(8,128)(2,1)S(1)}, u32[]{:S(2)}, u32[]{:S(2)}) collective-permute-start(bf16[128,512]{1,0:T(8,128)(2,1)S(1)} %get-tuple-element.39), channel_id=1, source_target_pairs={{0,2},{1,3},{2,4},{3,5},{4,6},{5,7},{6,8},{7,9},{8,10},{9,11},{10,... | collective-permute-start | bytes 393224 | tf_op jit(solution)/shard_map/ppermute | solution.py:367
  37.2 0.9 %collective-permute-done.5.far = bf16[256,512]{1,0:T(8,128)(2,1)S(1)} collective-permute-done((bf16[256,512]{1,0:T(8,128)(2,1)S(1)}, bf16[256,512]{1,0:T(8,128)(2,1)S(1)}, u32[]{:S(2)}, u32[]{:S(2)}) %collective-permute-start.5) | collective-permute-done | bytes 262176 | tf_op jit(solution)/shard_map/ppermute | solution.py:367
  38.1 2.6 %second_early.1 = (bf16[2,512,512]{2,1,0:T(8,128)(2,1)S(1)}, bf16[2,512,512]{2,1,0:T(8,128)(2,1)S(1)}, bf16[2,512,512]{2,1,0:T(8,128)(2,1)S(1)}, f32[2,512,512]{2,1,0:T(8,128)S(1)}) custom-call(bf16[256,512]{1,0:T(8,128)(2,1)S(1)} %get-tuple-element.28.home, bf16[128,512]{1,0:T(8,128)(2,1)S(1)} %get-tuple-element.36.home_side, ...), custom_call_target="tpu_custom_call" | custom-call | flops 1 | bytes 1 | tf_op jit(solution)/shard_map/second_early/pallas_call | solution.py:342
  40.7 2.9 %collective-permute-done.6.far_side = bf16[128,512]{1,0:T(8,128)(2,1)S(1)} collective-permute-done((bf16[128,512]{1,0:T(8,128)(2,1)S(1)}, bf16[128,512]{1,0:T(8,128)(2,1)S(1)}, u32[]{:S(2)}, u32[]{:S(2)}) %collective-permute-start.6) | collective-permute-done | bytes 131104 | tf_op jit(solution)/shard_map/ppermute | solution.py:367
  43.6 2.1 %collective-permute-done.7.far_corner = bf16[128,512]{1,0:T(8,128)(2,1)S(1)} collective-permute-done((bf16[128,512]{1,0:T(8,128)(2,1)S(1)}, bf16[128,512]{1,0:T(8,128)(2,1)S(1)}, u32[]{:S(2)}, u32[]{:S(2)}) %collective-permute-start.7) | collective-permute-done | bytes 131104 | tf_op jit(solution)/shard_map/ppermute | solution.py:367
  45.7 12.8 %second.1 = bf16[64,16,512]{2,1,0:T(8,128)(2,1)} custom-call(bf16[256,512]{1,0:T(8,128)(2,1)S(1)} %get-tuple-element.28.home, bf16[128,512]{1,0:T(8,128)(2,1)S(1)} %get-tuple-element.36.home_side, bf16[128,512]{1,0:T(8,128)(2,1)S(1)} %collective-permute-done.4.near_end, bf16[256,512]{1,0:T(8,128)(2,1)S(1)} %collective-permute-done.5.far, ...), custom_call_target="tpu_custom_call" | custom-call | flops 1 | bytes 1 | tf_op jit(solution)/shard_map/second/pallas_call | solution.py:342
  (29 shorter events, 0.2 us)
Async XLA Ops:
  1.8 15.6 %collective-permute-start = (bf16[272,512]{1,0:T(8,128)(2,1)}, bf16[272,512]{1,0:T(8,128)(2,1)S(1)}, u32[]{:S(2)}, u32[]{:S(2)}) collective-permute-start(bf16[272,512]{1,0:T(8,128)(2,1)} %pack_main.1.main), channel_id=1, source_target_pairs={{0,14},{1,15},{2,0},{3,1},{4,2},{5,3},{6,4},{7,5},{8,6},{9,7},{10,... | collective-permute-start | bytes 835592 | tf_op jit(solution)/shard_map/ppermute | solution.py:367
  7.9 1.9 %copy-start = (bf16[2,512,1536]{2,1,0:T(8,128)(2,1)S(1)}, bf16[2,512,1536]{2,1,0:T(8,128)(2,1)}, u32[]{:S(2)}) copy-start(bf16[2,512,1536]{2,1,0:T(8,128)(2,1)} %attend_in.9) | copy-start | bytes 9437188
  9.8 1.2 %copy-start.7 = (bf16[64,16,512]{2,1,0:T(8,128)(2,1)S(1)}, bf16[64,16,512]{2,1,0:T(8,128)(2,1)}, u32[]{:S(2)}) copy-start(bf16[64,16,512]{2,1,0:T(8,128)(2,1)} %block.5) | copy-start | bytes 3145732
  11.0 1.0 %copy-start.9 = (bf16[272,512]{1,0:T(8,128)(2,1)S(1)}, bf16[272,512]{1,0:T(8,128)(2,1)}, u32[]{:S(2)}) copy-start(bf16[272,512]{1,0:T(8,128)(2,1)} %pack_main.1.main) | copy-start | bytes 835588
  11.9 0.7 %copy-start.10 = (f32[2,2,512]{2,1,0:T(2,128)S(1)}, f32[2,2,512]{2,1,0:T(2,128)}, u32[]{:S(2)}) copy-start(f32[2,2,512]{2,1,0:T(2,128)} %gains.11) | copy-start | bytes 24580
  12.6 0.7 %copy-start.12 = (s32[64,16]{0,1:T(8,128)S(1)}, s32[64,16]{0,1:T(8,128)}, u32[]{:S(2)}) copy-start(s32[64,16]{0,1:T(8,128)} %param.10) | copy-start | bytes 12292
  13.3 0.7 %copy-start.13 = (s32[64]{0:T(128)S(1)}, s32[64]{0:T(128)}, u32[]{:S(2)}) copy-start(s32[64]{0:T(128)} %bands.7) | copy-start | bytes 772
  14.0 3.4 %copy-start.1 = (bf16[2,512,1536]{2,1,0:T(8,128)(2,1)S(1)}, bf16[2,512,1536]{2,1,0:T(8,128)(2,1)}, u32[]{:S(2)}) copy-start(bf16[2,512,1536]{2,1,0:T(8,128)(2,1)} %attend_in.9) | copy-start | bytes 9437188
  14.0 3.4 %copy-start.6 = (bf16[2,512,512]{2,1,0:T(8,128)(2,1)S(1)}, bf16[2,512,512]{2,1,0:T(8,128)(2,1)}, u32[]{:S(2)}) copy-start(bf16[2,512,512]{2,1,0:T(8,128)(2,1)} %attend_out.7) | copy-start | bytes 3145732
  15.6 11.9 %collective-permute-start.1 = (bf16[144,512]{1,0:T(8,128)(2,1)S(1)}, bf16[144,512]{1,0:T(8,128)(2,1)S(1)}, u32[]{:S(2)}, u32[]{:S(2)}) collective-permute-start(bf16[144,512]{1,0:T(8,128)(2,1)S(1)} %get-tuple-element.29), channel_id=1, source_target_pairs={{0,1},{1,0},{2,3},{3,2},{4,5},{5,4},{6,7},{7,6},{8,9},{9,8},{10,11... | collective-permute-start | bytes 442376 | tf_op jit(solution)/shard_map/ppermute | solution.py:367
  15.7 11.8 %collective-permute-start.2 = (bf16[144,512]{1,0:T(8,128)(2,1)S(1)}, bf16[144,512]{1,0:T(8,128)(2,1)S(1)}, u32[]{:S(2)}, u32[]{:S(2)}) collective-permute-start(bf16[144,512]{1,0:T(8,128)(2,1)S(1)} %get-tuple-element.30), channel_id=1, source_target_pairs={{0,14},{1,15},{2,0},{3,1},{4,2},{5,3},{6,4},{7,5},{8,6},{9,7},{10,... | collective-permute-start | bytes 442376 | tf_op jit(solution)/shard_map/ppermute | solution.py:367
  16.2 11.2 %collective-permute-start.3 = (bf16[144,512]{1,0:T(8,128)(2,1)S(1)}, bf16[144,512]{1,0:T(8,128)(2,1)S(1)}, u32[]{:S(2)}, u32[]{:S(2)}) collective-permute-start(bf16[144,512]{1,0:T(8,128)(2,1)S(1)} %get-tuple-element.31), channel_id=1, source_target_pairs={{0,15},{1,14},{2,1},{3,0},{4,3},{5,2},{6,5},{7,4},{8,7},{9,6},{10,... | collective-permute-start | bytes 442376 | tf_op jit(solution)/shard_map/ppermute | solution.py:367
  17.4 1.6 %copy-start.2 = (bf16[2,512,1024]{2,1,0:T(8,128)(2,1)S(1)}, bf16[2,512,1024]{2,1,0:T(8,128)(2,1)}, u32[]{:S(2)}) copy-start(bf16[2,512,1024]{2,1,0:T(8,128)(2,1)} %expand.7) | copy-start | bytes 6291460
  19.0 1.6 %copy-start.4 = (bf16[2,1024,512]{2,1,0:T(8,128)(2,1)S(1)}, bf16[2,1024,512]{2,1,0:T(8,128)(2,1)}, u32[]{:S(2)}) copy-start(bf16[2,1024,512]{2,1,0:T(8,128)(2,1)} %contract.7) | copy-start | bytes 6291460
  20.6 6.9 %copy-start.3 = (bf16[2,512,1024]{2,1,0:T(8,128)(2,1)S(1)}, bf16[2,512,1024]{2,1,0:T(8,128)(2,1)}, u32[]{:S(2)}) copy-start(bf16[2,512,1024]{2,1,0:T(8,128)(2,1)} %expand.7) | copy-start | bytes 6291460
  20.6 6.9 %copy-start.5 = (bf16[2,1024,512]{2,1,0:T(8,128)(2,1)S(1)}, bf16[2,1024,512]{2,1,0:T(8,128)(2,1)}, u32[]{:S(2)}) copy-start(bf16[2,1024,512]{2,1,0:T(8,128)(2,1)} %contract.7) | copy-start | bytes 6291460
  26.6 5.2 %copy-start.8 = (bf16[64,16,512]{2,1,0:T(8,128)(2,1)S(1)}, bf16[64,16,512]{2,1,0:T(8,128)(2,1)}, u32[]{:S(2)}) copy-start(bf16[64,16,512]{2,1,0:T(8,128)(2,1)} %block.5) | copy-start | bytes 3145732
  26.6 11.5 %collective-permute-start.5 = (bf16[256,512]{1,0:T(8,128)(2,1)S(1)}, bf16[256,512]{1,0:T(8,128)(2,1)S(1)}, u32[]{:S(2)}, u32[]{:S(2)}) collective-permute-start(bf16[256,512]{1,0:T(8,128)(2,1)S(1)} %get-tuple-element.38), channel_id=1, source_target_pairs={{0,2},{1,3},{2,4},{3,5},{4,6},{5,7},{6,8},{7,9},{8,10},{9,11},{10,... | collective-permute-start | bytes 786440 | tf_op jit(solution)/shard_map/ppermute | solution.py:367
  31.8 6.3 %copy-start.11 = (f32[2,2,512]{2,1,0:T(2,128)S(1)}, f32[2,2,512]{2,1,0:T(2,128)}, u32[]{:S(2)}) copy-start(f32[2,2,512]{2,1,0:T(2,128)} %gains.11) | copy-start | bytes 24580
  31.8 6.3 %copy-start.14 = (s32[64]{0:T(128)S(1)}, s32[64]{0:T(128)}, u32[]{:S(2)}) copy-start(s32[64]{0:T(128)} %bands.7) | copy-start | bytes 772
  34.6 2.6 %collective-permute-start.4 = (bf16[128,512]{1,0:T(8,128)(2,1)S(1)}, bf16[128,512]{1,0:T(8,128)(2,1)S(1)}, u32[]{:S(2)}, u32[]{:S(2)}) collective-permute-start(bf16[128,512]{1,0:T(8,128)(2,1)S(1)} %get-tuple-element.37), channel_id=1, source_target_pairs={{0,1},{1,0},{2,3},{3,2},{4,5},{5,4},{6,7},{7,6},{8,9},{9,8},{10,11... | collective-permute-start | bytes 393224 | tf_op jit(solution)/shard_map/ppermute | solution.py:367
  34.7 8.9 %collective-permute-start.6 = (bf16[128,512]{1,0:T(8,128)(2,1)S(1)}, bf16[128,512]{1,0:T(8,128)(2,1)S(1)}, u32[]{:S(2)}, u32[]{:S(2)}) collective-permute-start(bf16[128,512]{1,0:T(8,128)(2,1)S(1)} %get-tuple-element.39), channel_id=1, source_target_pairs={{0,2},{1,3},{2,4},{3,5},{4,6},{5,7},{6,8},{7,9},{8,10},{9,11},{10,... | collective-permute-start | bytes 393224 | tf_op jit(solution)/shard_map/ppermute | solution.py:367
  37.1 8.6 %collective-permute-start.7 = (bf16[128,512]{1,0:T(8,128)(2,1)S(1)}, bf16[128,512]{1,0:T(8,128)(2,1)S(1)}, u32[]{:S(2)}, u32[]{:S(2)}) collective-permute-start(bf16[128,512]{1,0:T(8,128)(2,1)S(1)} %get-tuple-element.40), channel_id=1, source_target_pairs={{0,3},{1,2},{2,5},{3,4},{4,7},{5,6},{6,9},{7,8},{8,11},{9,10},{10,... | collective-permute-start | bytes 393224 | tf_op jit(solution)/shard_map/ppermute | solution.py:367

commit v4 on v2

--- a/solution.py
+++ b/solution.py
@@ -144,9 +144,9 @@
     in_turn(H, (score, weigh, gather))
 
 
-def finish(fields, context, low, piece, attend_out, gain, expand, contract, write):
+def finish(fields, context, lows, attend_out, gain, expand, contract, write):
     def start(index, _):
-        rows = pl.ds(low + index * piece, piece)
+        rows = pl.ds(lows[index], fields[index].shape[0])
         added = fields[index] + product(context[rows, :], attend_out[...])
         resid = added.astype(BF16).astype(F32)
         return resid, normalize(resid, gain)
@@ -163,7 +163,7 @@
     in_turn(len(fields), (start, widen, bend, end))
 
 
-def pack_main_kernel(block_hbm, valid_hbm, main, block, valid, sems):
+def pack_main_kernel(block_hbm, valid_hbm, main, token, block, valid, sems):
     height = block_hbm.shape[0]
     rows = height - 2 * SH
     copies = (
@@ -172,6 +172,7 @@
     )
     for copy in copies:
         copy.start()
+    token[...] = jnp.zeros_like(token)
     copies[0].wait()
     masks = mask_lanes(valid, SH, 0, D)
     main[pl.ds(rows * SW, META), :] = meta_rows(masks, jnp.zeros_like(masks))
@@ -180,118 +181,120 @@
 
 
 def early_kernel(
-    block, bands, valid, main, gains, attend_in,
-    side, corner, row_end, query, key, value,
+    block, bands, valid, token, gains, attend_in,
+    side, corner, row_end, cells_here, query, key, value, notes,
 ):
     height = block.shape[0]
-    rows = height - 2 * SH
-    places = ((side, height - SH, 0), (corner, 0, 0), (row_end, 0, SW))
-    for out, low, column in places:
-        cells = SH * SW
-        out[pl.ds(0, cells), :] = half_columns(block[low : low + SH], column).astype(BF16)
+    part = SH * SW
+    for out, low, column in ((side, height - SH, 0), (corner, 0, 0), (row_end, 0, SW)):
+        out[pl.ds(0, part), :] = half_columns(block[low : low + SH], column).astype(BF16)
         masks = mask_lanes(valid, low, column, D)
-        out[pl.ds(cells, META), :] = meta_rows(masks, band_lanes(bands, low, SH, D))
+        out[pl.ds(part, META), :] = meta_rows(masks, band_lanes(bands, low, SH, D))
     local = half_columns(block[SH:], SW)
+    cells_here[...] = local.astype(BF16)
+    window_notes = [
+        (band_lanes(bands, SH, height - SH, D), mask_lanes(valid, SH, SW, D)),
+    ]
+    for row in range(0, height, WH):
+        row_bands = band_lanes(bands, row, WH, 2 * part)
+        window_notes.append((
+            jnp.concatenate([row_bands, row_bands], 1),
+            jnp.concatenate(
+                [mask_lanes(valid, row, SW, 2 * part), mask_lanes(valid, row, 0, 2 * part)], 1
+            ),
+        ))
+    for index, pair in enumerate(window_notes):
+        for offset, lanes in enumerate(pair):
+            notes[pl.ds(2 * index + offset, 1), :] = lanes
     project(local, gains[0:1], attend_in, 0, query, key, value)
 
 
 def window_a_kernel(
-    block, bands, valid, taken, near_query, near_key, near_value,
+    cells_here, notes, taken, near_query, near_key, near_value,
     gains, attend_in, attend_out, expand, contract,
     away, home, query, key, value, bias, context,
 ):
-    height = block.shape[0]
-    rows = height - 2 * SH
-    cells = rows * SW
+    cells = away.shape[0]
     for near, whole in ((near_query, query), (near_key, key), (near_value, value)):
         whole[pl.ds(0, cells), :] = near[pl.ds(0, cells), :]
-    local = half_columns(block[SH : SH + rows], SW)
+    local = cells_here[pl.ds(0, cells), :].astype(F32)
     remote = taken[pl.ds(0, cells), :].astype(F32)
     project(remote, gains[0:1], attend_in, cells, query, key, value)
-    row_bands = band_lanes(bands, SH, rows, cells)
+    row_bands = notes[0:1, :cells]
     masks, _ = meta_of(taken, cells)
     set_bias(
         bias,
         jnp.concatenate([row_bands, row_bands], 1),
-        jnp.concatenate([mask_lanes(valid, SH, SW, cells), masks], 1),
+        jnp.concatenate([notes[1:2, :cells], masks], 1),
     )
     attend(query, key, value, bias, context, 0, 2 * cells)
 
     def write(index, out):
         (home, away)[index][...] = out.astype(BF16)
 
-    finish([local, remote], context, 0, cells, attend_out, gains[1:2], expand, contract, write)
+    finish([local, remote], context, (0, cells), attend_out, gains[1:2], expand, contract, write)
 
 
 def window_b_away_kernel(
-    bands, valid, taken_side, taken_corner, taken_end, near_query, near_key, near_value,
+    window_a_first, notes, taken_side, taken_corner, taken_end, near_query, near_key, near_value,
     gains, attend_in, attend_out, expand, contract,
-    away_side, away_corner, query, key, value, bias, context,
-):
-    height = bands.shape[0]
-    cells = SH * SW
+    away_side, away_corner, home_end, query, key, value, bias, context,
+):
+    cells = away_side.shape[0]
+    skip = near_query.shape[0] - cells
     for near, whole in ((near_query, query), (near_key, key), (near_value, value)):
-        whole[pl.ds(0, cells), :] = near[pl.ds(near.shape[0] - cells, cells), :]
+        whole[pl.ds(0, cells), :] = near[pl.ds(skip, cells), :]
     fields = []
-    bands_here = [band_lanes(bands, height - SH, SH, cells)]
-    masks_here = [mask_lanes(valid, height - SH, SW, cells)]
+    bands_here = [notes[0:1, skip : skip + cells]]
+    masks_here = [notes[1:2, skip : skip + cells]]
     for taken in (taken_end, taken_side, taken_corner):
         fields.append(taken[pl.ds(0, cells), :].astype(F32))
         masks, row_bands = meta_of(taken, cells)
         masks_here.append(masks)
         bands_here.append(row_bands)
+    bands_here[2] = bands_here[0]
     project(jnp.concatenate(fields, 0), gains[0:1], attend_in, cells, query, key, value)
     set_bias(bias, jnp.concatenate(bands_here, 1), jnp.concatenate(masks_here, 1))
-    attend(query, key, value, bias, context, 2 * cells, 2 * cells)
+    attend(query, key, value, bias, context, cells, 3 * cells)
 
     def write(index, out):
-        (away_side, away_corner)[index][...] = out.astype(BF16)
-
-    finish(fields[1:], context, 2 * cells, cells, attend_out, gains[1:2], expand, contract, write)
-
-
-def window_b_home_kernel(
-    block, taken_end, query, key, value, bias, gains, attend_out, expand, contract,
-    home_side, home_end, context,
-):
-    height = block.shape[0]
-    cells = SH * SW
-    attend(query, key, value, bias, context, 0, 2 * cells)
-    fields = [half_columns(block[height - SH :], SW), taken_end[pl.ds(0, cells), :].astype(F32)]
+        out = out.astype(BF16)
+        if index == 0:
+            away_side[...], away_corner[...] = out[:cells], out[cells:]
+        else:
+            home_end[...] = out
+
+    fields = [jnp.concatenate(fields[1:], 0), fields[0]]
+    finish(fields, context, (2 * cells, cells), attend_out, gains[1:2], expand, contract, write)
+
+
+def between_kernel(
+    cells_here, query, key, value, bias, gains, attend_out, expand, contract,
+    home, notes, next_gains, next_attend_in,
+    home_side, next_query, next_key, next_value, next_bias, context,
+):
+    part = home_side.shape[0]
+    attend(query, key, value, bias, context, 0, part)
+    near = cells_here[pl.ds(cells_here.shape[0] - part, part), :]
+    kept = []
 
     def write(index, out):
-        (home_side, home_end)[index][...] = out.astype(BF16)
-
-    finish(fields, context, 0, cells, attend_out, gains[1:2], expand, contract, write)
-
-
-def second_early_kernel(
-    home, home_side, near_end, far, bands, valid, gains, attend_in,
-    query, key, value, bias,
-):
-    part = SH * SW
-    low, high = slice(0, part), slice(part, 2 * part)
-    windows = ((near_end[...], home[low], far[low]), (home[high], home_side[...], far[high]))
-    for index, parts in enumerate(windows):
-        field = jnp.concatenate([piece.astype(F32) for piece in parts], 0)
-        project(field, gains[0:1], attend_in, 0, query.at[index], key.at[index], value.at[index])
-        row = index * WH
-        row_bands = band_lanes(bands, row, WH, 2 * part)
-        near_masks = mask_lanes(valid, row, SW, 2 * part)
-        far_masks = mask_lanes(valid, row, 0, 2 * part)
-        far_bands = row_bands
-        if index == 0:
-            far_bands = jnp.concatenate([row_bands[:, part:], row_bands[:, :part]], 1)
-            far_masks = jnp.concatenate([far_masks[:, part:], far_masks[:, :part]], 1)
-        set_bias(
-            bias.at[index],
-            jnp.concatenate([row_bands, far_bands], 1),
-            jnp.concatenate([near_masks, far_masks], 1),
-        )
+        home_side[...] = out.astype(BF16)
+        kept.append(out.astype(BF16).astype(F32))
+
+    finish([near.astype(F32)], context, (0,), attend_out, gains[1:2], expand, contract, write)
+    for index in range(2):
+        set_bias(next_bias.at[index], notes[2 * index + 2 : 2 * index + 3],
+                 notes[2 * index + 3 : 2 * index + 4])
+    pieces = ((0, part, home[:part].astype(F32)),
+              (1, 0, jnp.concatenate([home[part:].astype(F32), kept[0]], 0)))
+    for index, at, field in pieces:
+        project(field, next_gains[0:1], next_attend_in, at,
+                next_query.at[index], next_key.at[index], next_value.at[index])
 
 
 def second_kernel(
-    home, home_side, near_end, far, far_side, far_corner,
+    home, home_side, far, far_side, far_corner, near_end,
     early_query, early_key, early_value, bias,
     gains, attend_in, attend_out, expand, contract,
     out_ref, query, key, value, context,
@@ -299,15 +302,14 @@
     part = SH * SW
     low, high = slice(0, part), slice(part, 2 * part)
     windows = (
-        (near_end[...], home[low], far[low], far_corner[...]),
+        (near_end[...], home[low], far_corner[...], far[low]),
         (home[high], home_side[...], far[high], far_side[...]),
     )
     windows = [[piece.astype(F32) for piece in parts] for parts in windows]
-    late = 3 * part
-    for early, whole in ((early_query, query), (early_key, key), (early_value, value)):
-        whole[:, pl.ds(0, late), :] = early[:, pl.ds(0, late), :]
-    for index, parts in enumerate(windows):
-        project(parts[3], gains[0:1], attend_in, late, query.at[index], key.at[index], value.at[index])
+    pieces = ((0, 0, windows[0][0]), (0, 2 * part, jnp.concatenate(windows[0][2:], 0)),
+              (1, 2 * part, jnp.concatenate(windows[1][2:], 0)))
+    for index, at, field in pieces:
+        project(field, gains[0:1], attend_in, at, query.at[index], key.at[index], value.at[index])
     for index in range(len(windows)):
         attend(
             query.at[index], key.at[index], value.at[index], bias.at[index],
@@ -321,15 +323,14 @@
         if index % 2 == 0:
             near[window] = out
             return
-        if window == 0:
-            out = jnp.concatenate([out[part:], out[:part]], 0)
         both = [piece.reshape(WH, SW, D) for piece in (out, near.pop(window))]
         out_ref[pl.ds(window * WH, WH)] = jnp.concatenate(both, 1).astype(BF16)
 
-    finish(fields, context, 0, 2 * part, attend_out, gains[1:2], expand, contract, write)
-
-
-def call(kernel, name, shapes, specs, scratch, flops, *operands, limit=40):
+    lows = [2 * part * at for at in range(len(fields))]
+    finish(fields, context, lows, attend_out, gains[1:2], expand, contract, write)
+
+
+def call(kernel, name, shapes, specs, scratch, flops, *operands, limit=40, aliases=()):
     size = sum(operand.size * operand.dtype.itemsize for operand in operands)
     shapes = [shape if isinstance(shape, jax.ShapeDtypeStruct) else jax.ShapeDtypeStruct(shape, BF16)
               for shape in shapes]
@@ -341,6 +342,7 @@
         scratch_shapes=scratch,
         compiler_params=pltpu.CompilerParams(vmem_limit_bytes=limit * 2**20),
         cost_estimate=pl.CostEstimate(flops=flops, bytes_accessed=size, transcendentals=0),
+        input_output_aliases=dict(aliases),
         name=name,
     )(*operands)
 
@@ -370,58 +372,57 @@
     flops = cells * 2 * D * (D + 2 * hidden) + 4 * cells * cells * D
 
     valid = key_valid.T
-    main = call(
-        pack_main_kernel, "pack_main", [(half + META, D)], [HBM] * 2,
-        [pltpu.VMEM((WH, breadth, D), BF16), pltpu.VMEM(valid.shape, valid.dtype),
-         pltpu.SemaphoreType.DMA((2,))],
+    valid_scratch = pltpu.VMEM(valid.shape, valid.dtype)
+    main, token = call(
+        pack_main_kernel, "pack_main", [(half + META, D), (META, 2 * HD)], [HBM] * 2,
+        [pltpu.VMEM((WH, breadth, D), BF16), valid_scratch, pltpu.SemaphoreType.DMA((2,))],
         10**6, atmosphere, valid, limit=62,
-    )[0]
+    )
     far_main = moved(main, -1, 0)
 
     weights = [
         (norm_gains[k], attend_in[k], attend_out[k], expand[k], contract[k]) for k in range(2)
     ]
-    side, corner, row_end, *near = call(
-        early_kernel, "early", [(quarter + META, D)] * 3 + [(half + quarter, D)] * 3,
+    side, corner, row_end, here, *near, notes = call(
+        early_kernel, "early",
+        [(quarter + META, D)] * 3 + [(half + quarter, D)] * 4
+        + [jax.ShapeDtypeStruct((META, D), F32)],
         [VMEM, SMEM] + [VMEM] * 4, [], each * (half + quarter),
-        atmosphere, pole_band, valid, main, *weights[0][:2],
+        atmosphere, pole_band, valid, token, *weights[0][:2],
     )
     far_side = moved(side, -1, 0)
     far_corner = moved(corner, -1, -1)
     near_end = moved(row_end, 0, -1)
 
     away, home = call(
-        window_a_kernel, "window_a", [(half, D)] * 2, [VMEM, SMEM] + [VMEM] * 10,
+        window_a_kernel, "window_a", [(half, D)] * 2, [VMEM] * 11,
         [wide] * 3 + [bias_scratch, wide], flops + each * half,
-        atmosphere, pole_band, valid, far_main, *near, *weights[0],
+        here, notes, far_main, *near, *weights[0],
     )
     back_main = moved(away, 1, 0)
-    away_side, away_corner, *inside = call(
+    away_side, away_corner, home_end, *inside = call(
         window_b_away_kernel, "window_b_away",
-        [(quarter, D)] * 2 + [(cells, D)] * 3 + [bias_shape], [SMEM] + [VMEM] * 12,
-        [wide], flops // 2 + each * 3 * quarter,
-        pole_band, valid, far_side, far_corner, near_end, *near, *weights[0],
+        [(quarter, D)] * 3 + [(cells, D)] * 3 + [bias_shape], [VMEM] * 13,
+        [wide], 3 * flops // 4 + each * 3 * quarter,
+        home, notes, far_side, far_corner, near_end, *near, *weights[0],
+    )
+    pair = (2, cells, D)
+    home_side, *inside = call(
+        between_kernel, "between",
+        [(quarter, D)] + [pair] * 3 + [jax.ShapeDtypeStruct((2, cells, cells), F32)],
+        [VMEM] * 13, [wide], flops // 4 + each * 3 * quarter,
+        here, *inside, weights[0][0], *weights[0][2:],
+        home, notes, *weights[1][:2],
     )
     back_side = moved(away_side, 1, 0)
     back_corner = moved(away_corner, 1, 1)
-    home_side, home_end = call(
-        window_b_home_kernel, "window_b_home", [(quarter, D)] * 2, [VMEM] * 10,
-        [wide], flops // 2,
-        atmosphere, near_end, *inside, weights[0][0], *weights[0][2:],
-    )
     back_end = moved(home_end, 0, 1)
-    pair = (2, cells, D)
-    inside = call(
-        second_early_kernel, "second_early",
-        [pair] * 3 + [jax.ShapeDtypeStruct((2, cells, cells), F32)],
-        [VMEM] * 4 + [SMEM] + [VMEM] * 3, [], each * 6 * quarter,
-        home, home_side, back_end, back_main, pole_band, valid, *weights[1][:2],
-    )
     return call(
-        second_kernel, "second", [(height, breadth, D)], [VMEM] * 15,
-        [pltpu.VMEM(pair, BF16)] * 3 + [pltpu.VMEM((2 * cells, D), BF16)],
-        2 * flops + each * 2 * quarter,
-        home, home_side, back_end, back_main, back_side, back_corner, *inside, *weights[1],
+        second_kernel, "second", [(height, breadth, D)] + [pair] * 3, [VMEM] * 15,
+        [pltpu.VMEM((2 * cells, D), BF16)],
+        2 * flops + each * 5 * quarter,
+        home, home_side, back_main, back_side, back_corner, back_end, *inside, *weights[1],
+        aliases=((6, 1), (7, 2), (8, 3)),
     )[0]
 
 

time: 51.8 us -> 50.5 us (0.975)
  waiting for transfers between devices: 6.98 us -> 5.03 us
  starting transfers between devices: 11.1 us -> 12.1 us
    ppermute x8, waiting for transfers between devices: 6.98 us -> 5.03 us  [moved(): return lax.ppermute(value, ('lon', 'lat'), pairs)]
    ppermute x8, starting transfers between devices: 11.1 us -> 12.1 us  [moved(): return lax.ppermute(value, ('lon', 'lat'), pairs)]
    pallas_call x7 -> x6, Pallas kernels: 28.7 us -> 28.4 us  [call(): pl.pallas_call(kernel, out_shape=shapes, in_specs=specs, out_specs=[VMEM]...]
  transfers between devices with their start and end apart: 8 -> 8, of which waited for: 3 -> 2; matrix products, arithmetic and copies ran while one was open for 6% -> 6% of each run, Pallas kernels for 33% -> 30%
where the time goes in v4:
time: 50.5 us; the launch traced here: 50.2 us
  Pallas kernels  28.4 us (56%)
  starting transfers between devices  12.1 us (24%)
  waiting for transfers between devices  5.03 us (10%)
  local copies, waits for them, and re-layouts  4.54 us (9%)
    pallas_call x6, Pallas kernels, call(): pl.pallas_call(kernel, out_shape=shapes, in_specs=specs, out_specs=[VMEM]...  28.4 us
    ppermute x8, starting transfers between devices, moved(): return lax.ppermute(value, ('lon', 'lat'), pairs)  12.1 us
    ppermute x8, waiting for transfers between devices, moved(): return lax.ppermute(value, ('lon', 'lat'), pairs)  5.03 us
    squeeze x1, local copies, waits for them, and re-layouts, on_device(): attend_in[k]  2.17 us
    unnamed x14, local copies, waits for them, and re-layouts  1.28 us
  transfers between devices with their start and end apart: 8, of which 2 were waited for; matrix products, arithmetic and copies ran while one was open for 6% of the time, Pallas kernels for 30%

profile of v4, /device:TPU:0, one launch (start us, length us, event | category | flops | bytes accessed | tf_op | source)
XLA Modules:
  0.0 50.2 jit_solution(3099853439715270312)
XLA Ops:
  0.0 1.8 %pack_main.1 = (bf16[272,512]{1,0:T(8,128)(2,1)}, bf16[16,128]{1,0:T(8,128)(2,1)}) custom-call(bf16[64,16,512]{2,1,0:T(8,128)(2,1)} %block.1, s32[16,64]{1,0:T(8,128)} %bitcast.21), custom_call_target="tpu_custom_call" | custom-call | flops 1000000 | bytes 1052672 | tf_op jit(solution)/shard_map/pack_main/pallas_call | solution.py:337
  1.8 6.1 %collective-permute-start = (bf16[272,512]{1,0:T(8,128)(2,1)}, bf16[272,512]{1,0:T(8,128)(2,1)S(1)}, u32[]{:S(2)}, u32[]{:S(2)}) collective-permute-start(bf16[272,512]{1,0:T(8,128)(2,1)} %get-tuple-element.33), channel_id=1, source_target_pairs={{0,14},{1,15},{2,0},{3,1},{4,2},{5,3},{6,4},{7,5},{8,6},{9,7},{10,... | collective-permute-start | bytes 835592 | tf_op jit(solution)/shard_map/ppermute | solution.py:363
  7.9 0.7 %slice_bitcast_fusion.8 = (f32[2,512]{1,0:T(2,128)S(1)}, f32[2,512]{1,0:T(2,128)S(1)}) fusion(f32[2,2,512]{2,1,0:T(2,128)} %param.11), kind=kLoop, calls=%fused_computation.8 | loop fusion | bytes 16384 | tf_op jit(solution)/shard_map/squeeze | solution.py:384
  8.6 2.2 %slice_bitcast_fusion = (bf16[512,1536]{1,0:T(8,128)(2,1)S(1)}, bf16[512,1536]{1,0:T(8,128)(2,1)S(1)}) fusion(bf16[2,512,1536]{2,1,0:T(8,128)(2,1)} %param.12), kind=kLoop, calls=%fused_computation | loop fusion | bytes 6291456 | tf_op jit(solution)/shard_map/squeeze | solution.py:384
  10.8 0.0 copy-start.4
  10.8 1.6 %early.1 = (bf16[144,512]{1,0:T(8,128)(2,1)S(1)}, bf16[144,512]{1,0:T(8,128)(2,1)S(1)}, bf16[144,512]{1,0:T(8,128)(2,1)S(1)}, bf16[384,512]{1,0:T(8,128)(2,1)S(1...) custom-call(bf16[64,16,512]{2,1,0:T(8,128)(2,1)S(1)} %copy-done, ...), custom_call_target="tpu_custom_call" | custom-call | flops 603979776 | bytes 2633984 | tf_op jit(solution)/shard_map/early/pallas_call | solution.py:337
  12.4 0.6 %collective-permute-start.1 = (bf16[144,512]{1,0:T(8,128)(2,1)S(1)}, bf16[144,512]{1,0:T(8,128)(2,1)S(1)}, u32[]{:S(2)}, u32[]{:S(2)}) collective-permute-start(bf16[144,512]{1,0:T(8,128)(2,1)S(1)} %get-tuple-element.38), channel_id=1, source_target_pairs={{0,14},{1,15},{2,0},{3,1},{4,2},{5,3},{6,4},{7,5},{8,6},{9,7},{10,... | collective-permute-start | bytes 442376 | tf_op jit(solution)/shard_map/ppermute | solution.py:363
  13.0 0.3 collective-permute-start.2
  13.3 1.2 %collective-permute-start.3 = (bf16[144,512]{1,0:T(8,128)(2,1)S(1)}, bf16[144,512]{1,0:T(8,128)(2,1)S(1)}, u32[]{:S(2)}, u32[]{:S(2)}) collective-permute-start(bf16[144,512]{1,0:T(8,128)(2,1)S(1)} %get-tuple-element.40), channel_id=1, source_target_pairs={{0,1},{1,0},{2,3},{3,2},{4,5},{5,4},{6,7},{7,6},{8,9},{9,8},{10,11... | collective-permute-start | bytes 442376 | tf_op jit(solution)/shard_map/ppermute | solution.py:363
  14.5 0.2 slice_bitcast_fusion.3
  14.7 0.2 copy-done.5
  14.9 0.1 slice_bitcast_fusion.2
  15.0 1.1 %copy-done.6 = bf16[2,512,512]{2,1,0:T(8,128)(2,1)S(1)} copy-done((bf16[2,512,512]{2,1,0:T(8,128)(2,1)S(1)}, bf16[2,512,512]{2,1,0:T(8,128)(2,1)}, u32[]{:S(2)}) %copy-start.6) | copy-done | bytes 1048600
  16.1 0.1 slice_bitcast_fusion.6
  16.2 0.0 collective-permute-done.taken
  16.2 5.4 %window_a.1 = (bf16[256,512]{1,0:T(8,128)(2,1)S(1)}, bf16[256,512]{1,0:T(8,128)(2,1)S(1)}) custom-call(bf16[384,512]{1,0:T(8,128)(2,1)S(1)} %get-tuple-element.31.cells_here, f32[16,512]{1,0:T(8,128)S(1)} %get-tuple-element.32.notes, bf16[272,512]{1,0:T(8,128)(2,1)S(1)} %collective-permute-done.taken, bf16[384,512]{1,0:T(8,128)(2,1)S(1)} %get-tuple-element.34.near_query, ...), custom_call_target="tpu_custom_call" | custom-call | flops 2281701376 | bytes 6082560 | tf_op jit(solution)/shard_map/window_a/pallas_call | solution.py:337
  21.6 1.3 %collective-permute-start.4 = (bf16[256,512]{1,0:T(8,128)(2,1)S(1)}, bf16[256,512]{1,0:T(8,128)(2,1)S(1)}, u32[]{:S(2)}, u32[]{:S(2)}) collective-permute-start(bf16[256,512]{1,0:T(8,128)(2,1)S(1)} %get-tuple-element.46), channel_id=1, source_target_pairs={{0,2},{1,3},{2,4},{3,5},{4,6},{5,7},{6,8},{7,9},{8,10},{9,11},{10,... | collective-permute-start | bytes 786440 | tf_op jit(solution)/shard_map/ppermute | solution.py:363
  22.9 5.1 %window_b_away.1 = (bf16[128,512]{1,0:T(8,128)(2,1)S(1)}, bf16[128,512]{1,0:T(8,128)(2,1)S(1)}, bf16[128,512]{1,0:T(8,128)(2,1)S(1)}, bf16[512,512]{1,0:T(8,128)...) custom-call(bf16[256,512]{1,0:T(8,128)(2,1)S(1)} %get-tuple-element.37.window_a_first., ...), custom_call_target="tpu_custom_call" | custom-call | flops 2013265920 | bytes 6115328 | tf_op jit(solution)/shard_map/window_b_away/pallas_call | solution.py:337
  28.0 1.9 %collective-permute-start.5 = (bf16[128,512]{1,0:T(8,128)(2,1)S(1)}, bf16[128,512]{1,0:T(8,128)(2,1)S(1)}, u32[]{:S(2)}, u32[]{:S(2)}) collective-permute-start(bf16[128,512]{1,0:T(8,128)(2,1)S(1)} %get-tuple-element.47), channel_id=1, source_target_pairs={{0,2},{1,3},{2,4},{3,5},{4,6},{5,7},{6,8},{7,9},{8,10},{9,11},{10,... | collective-permute-start | bytes 393224 | tf_op jit(solution)/shard_map/ppermute | solution.py:363
  29.9 0.8 %collective-permute-start.6 = (bf16[128,512]{1,0:T(8,128)(2,1)S(1)}, bf16[128,512]{1,0:T(8,128)(2,1)S(1)}, u32[]{:S(2)}, u32[]{:S(2)}) collective-permute-start(bf16[128,512]{1,0:T(8,128)(2,1)S(1)} %get-tuple-element.48), channel_id=1, source_target_pairs={{0,3},{1,2},{2,5},{3,4},{4,7},{5,6},{6,9},{7,8},{8,11},{9,10},{10,... | collective-permute-start | bytes 393224 | tf_op jit(solution)/shard_map/ppermute | solution.py:363
  30.7 3.0 %between.1 = (bf16[128,512]{1,0:T(8,128)(2,1)S(1)}, bf16[2,512,512]{2,1,0:T(8,128)(2,1)S(1)}, bf16[2,512,512]{2,1,0:T(8,128)(2,1)S(1)}, bf16[2,512,512]{2,1,0:T(8,128)(2,1)S(1)}, f32[2,512,512]{2,1,0:T(8,128)S(1)}) custom-call(bf16[384,512]{1,0:T(8,128)(2,1)S(1)} %get-tuple-element.31.cells_here, bf16[512,512]{1,0:T(8,128)(2,1)S(1)} %get-tuple-element.41.query, ...), custom_call_target="tpu_custom_call" | custom-call | flops 1073741824 | bytes 7512064 | tf_op jit(solution)/shard_map/between/pallas_call | solution.py:337
  33.7 3.3 %collective-permute-done.5.far_side = bf16[128,512]{1,0:T(8,128)(2,1)S(1)} collective-permute-done((bf16[128,512]{1,0:T(8,128)(2,1)S(1)}, bf16[128,512]{1,0:T(8,128)(2,1)S(1)}, u32[]{:S(2)}, u32[]{:S(2)}) %collective-permute-start.5) | collective-permute-done | bytes 131104 | tf_op jit(solution)/shard_map/ppermute | solution.py:363
  37.1 1.7 %collective-permute-done.6.far_corner = bf16[128,512]{1,0:T(8,128)(2,1)S(1)} collective-permute-done((bf16[128,512]{1,0:T(8,128)(2,1)S(1)}, bf16[128,512]{1,0:T(8,128)(2,1)S(1)}, u32[]{:S(2)}, u32[]{:S(2)}) %collective-permute-start.6) | collective-permute-done | bytes 131104 | tf_op jit(solution)/shard_map/ppermute | solution.py:363
  38.7 11.4 %second.1 = (bf16[64,16,512]{2,1,0:T(8,128)(2,1)}, bf16[2,512,512]{2,1,0:T(8,128)(2,1)S(1)}, bf16[2,512,512]{2,1,0:T(8,128)(2,1)S(1)}, bf16[2,512,512]{2,1,0:T(8,128)(2,1)S(1)}) custom-call(bf16[256,512]{1,0:T(8,128)(2,1)S(1)} %get-tuple-element.37.window_a_first.home, ...), custom_call_target="tpu_custom_call", output_to_operand_aliasing={{1}: (6, {}), {2}: (7, {}), {3}: (8, {})} | custom-call | flops 4764729344 | bytes 10489856 | tf_op jit(solution)/shard_map/second/pallas_call | solution.py:337
  (17 shorter events, 0.0 us)
Async XLA Ops:
  1.8 14.4 %collective-permute-start = (bf16[272,512]{1,0:T(8,128)(2,1)}, bf16[272,512]{1,0:T(8,128)(2,1)S(1)}, u32[]{:S(2)}, u32[]{:S(2)}) collective-permute-start(bf16[272,512]{1,0:T(8,128)(2,1)} %get-tuple-element.33), channel_id=1, source_target_pairs={{0,14},{1,15},{2,0},{3,1},{4,2},{5,3},{6,4},{7,5},{8,6},{9,7},{10,... | collective-permute-start | bytes 835592 | tf_op jit(solution)/shard_map/ppermute | solution.py:363
  8.6 2.2 %copy-start = (bf16[64,16,512]{2,1,0:T(8,128)(2,1)S(1)}, bf16[64,16,512]{2,1,0:T(8,128)(2,1)}, u32[]{:S(2)}) copy-start(bf16[64,16,512]{2,1,0:T(8,128)(2,1)} %block.1) | copy-start | bytes 3145732
  8.6 2.2 %copy-start.1 = (s32[64,16]{0,1:T(8,128)S(1)}, s32[64,16]{0,1:T(8,128)}, u32[]{:S(2)}) copy-start(s32[64,16]{0,1:T(8,128)} %param.10) | copy-start | bytes 12292
  8.6 2.2 %copy-start.2 = (bf16[16,128]{1,0:T(8,128)(2,1)S(1)}, bf16[16,128]{1,0:T(8,128)(2,1)}, u32[]{:S(2)}) copy-start(bf16[16,128]{1,0:T(8,128)(2,1)} %get-tuple-element.30.token) | copy-start | bytes 12292
  8.6 2.2 %copy-start.3 = (s32[64]{0:T(128)S(1)}, s32[64]{0:T(128)}, u32[]{:S(2)}) copy-start(s32[64]{0:T(128)} %bands.1) | copy-start | bytes 772
  10.8 3.8 %copy-start.4 = (bf16[2,512,1024]{2,1,0:T(8,128)(2,1)S(1)}, bf16[2,512,1024]{2,1,0:T(8,128)(2,1)}, u32[]{:S(2)}) copy-start(bf16[2,512,1024]{2,1,0:T(8,128)(2,1)} %param.14) | copy-start | bytes 6291460
  12.4 10.4 %collective-permute-start.1 = (bf16[144,512]{1,0:T(8,128)(2,1)S(1)}, bf16[144,512]{1,0:T(8,128)(2,1)S(1)}, u32[]{:S(2)}, u32[]{:S(2)}) collective-permute-start(bf16[144,512]{1,0:T(8,128)(2,1)S(1)} %get-tuple-element.38), channel_id=1, source_target_pairs={{0,14},{1,15},{2,0},{3,1},{4,2},{5,3},{6,4},{7,5},{8,6},{9,7},{10,... | collective-permute-start | bytes 442376 | tf_op jit(solution)/shard_map/ppermute | solution.py:363
  13.0 9.9 %collective-permute-start.2 = (bf16[144,512]{1,0:T(8,128)(2,1)S(1)}, bf16[144,512]{1,0:T(8,128)(2,1)S(1)}, u32[]{:S(2)}, u32[]{:S(2)}) collective-permute-start(bf16[144,512]{1,0:T(8,128)(2,1)S(1)} %get-tuple-element.39), channel_id=1, source_target_pairs={{0,15},{1,14},{2,1},{3,0},{4,3},{5,2},{6,5},{7,4},{8,7},{9,6},{10,... | collective-permute-start | bytes 442376 | tf_op jit(solution)/shard_map/ppermute | solution.py:363
  13.3 1.6 %copy-start.5 = (bf16[2,1024,512]{2,1,0:T(8,128)(2,1)S(1)}, bf16[2,1024,512]{2,1,0:T(8,128)(2,1)}, u32[]{:S(2)}) copy-start(bf16[2,1024,512]{2,1,0:T(8,128)(2,1)} %param.15) | copy-start | bytes 6291460
  13.3 9.6 %collective-permute-start.3 = (bf16[144,512]{1,0:T(8,128)(2,1)S(1)}, bf16[144,512]{1,0:T(8,128)(2,1)S(1)}, u32[]{:S(2)}, u32[]{:S(2)}) collective-permute-start(bf16[144,512]{1,0:T(8,128)(2,1)S(1)} %get-tuple-element.40), channel_id=1, source_target_pairs={{0,1},{1,0},{2,3},{3,2},{4,5},{5,4},{6,7},{7,6},{8,9},{9,8},{10,11... | collective-permute-start | bytes 442376 | tf_op jit(solution)/shard_map/ppermute | solution.py:363
  14.9 1.2 %copy-start.6 = (bf16[2,512,512]{2,1,0:T(8,128)(2,1)S(1)}, bf16[2,512,512]{2,1,0:T(8,128)(2,1)}, u32[]{:S(2)}) copy-start(bf16[2,512,512]{2,1,0:T(8,128)(2,1)} %param.13) | copy-start | bytes 3145732
  21.6 17.2 %collective-permute-start.4 = (bf16[256,512]{1,0:T(8,128)(2,1)S(1)}, bf16[256,512]{1,0:T(8,128)(2,1)S(1)}, u32[]{:S(2)}, u32[]{:S(2)}) collective-permute-start(bf16[256,512]{1,0:T(8,128)(2,1)S(1)} %get-tuple-element.46), channel_id=1, source_target_pairs={{0,2},{1,3},{2,4},{3,5},{4,6},{5,7},{6,8},{7,9},{8,10},{9,11},{10,... | collective-permute-start | bytes 786440 | tf_op jit(solution)/shard_map/ppermute | solution.py:363
  28.0 9.1 %collective-permute-start.5 = (bf16[128,512]{1,0:T(8,128)(2,1)S(1)}, bf16[128,512]{1,0:T(8,128)(2,1)S(1)}, u32[]{:S(2)}, u32[]{:S(2)}) collective-permute-start(bf16[128,512]{1,0:T(8,128)(2,1)S(1)} %get-tuple-element.47), channel_id=1, source_target_pairs={{0,2},{1,3},{2,4},{3,5},{4,6},{5,7},{6,8},{7,9},{8,10},{9,11},{10,... | collective-permute-start | bytes 393224 | tf_op jit(solution)/shard_map/ppermute | solution.py:363
  29.9 8.9 %collective-permute-start.6 = (bf16[128,512]{1,0:T(8,128)(2,1)S(1)}, bf16[128,512]{1,0:T(8,128)(2,1)S(1)}, u32[]{:S(2)}, u32[]{:S(2)}) collective-permute-start(bf16[128,512]{1,0:T(8,128)(2,1)S(1)} %get-tuple-element.48), channel_id=1, source_target_pairs={{0,3},{1,2},{2,5},{3,4},{4,7},{5,6},{6,9},{7,8},{8,11},{9,10},{10,... | collective-permute-start | bytes 393224 | tf_op jit(solution)/shard_map/ppermute | solution.py:363
  30.7 8.1 %collective-permute-start.7 = (bf16[128,512]{1,0:T(8,128)(2,1)S(1)}, bf16[128,512]{1,0:T(8,128)(2,1)S(1)}, u32[]{:S(2)}, u32[]{:S(2)}) collective-permute-start(bf16[128,512]{1,0:T(8,128)(2,1)S(1)} %get-tuple-element.49), channel_id=1, source_target_pairs={{0,1},{1,0},{2,3},{3,2},{4,5},{5,4},{6,7},{7,6},{8,9},{9,8},{10,11... | collective-permute-start | bytes 393224 | tf_op jit(solution)/shard_map/ppermute | solution.py:363

commit v5 on v4

--- a/solution.py
+++ b/solution.py
@@ -206,7 +206,7 @@
     for index, pair in enumerate(window_notes):
         for offset, lanes in enumerate(pair):
             notes[pl.ds(2 * index + offset, 1), :] = lanes
-    project(local, gains[0:1], attend_in, 0, query, key, value)
+    project(local, gains[0, 0:1], attend_in, 0, query, key, value)
 
 
 def window_a_kernel(
@@ -219,7 +219,7 @@
         whole[pl.ds(0, cells), :] = near[pl.ds(0, cells), :]
     local = cells_here[pl.ds(0, cells), :].astype(F32)
     remote = taken[pl.ds(0, cells), :].astype(F32)
-    project(remote, gains[0:1], attend_in, cells, query, key, value)
+    project(remote, gains[0, 0:1], attend_in, cells, query, key, value)
     row_bands = notes[0:1, :cells]
     masks, _ = meta_of(taken, cells)
     set_bias(
@@ -232,7 +232,7 @@
     def write(index, out):
         (home, away)[index][...] = out.astype(BF16)
 
-    finish([local, remote], context, (0, cells), attend_out, gains[1:2], expand, contract, write)
+    finish([local, remote], context, (0, cells), attend_out, gains[0, 1:2], expand, contract, write)
 
 
 def window_b_away_kernel(
@@ -253,7 +253,7 @@
         masks_here.append(masks)
         bands_here.append(row_bands)
     bands_here[2] = bands_here[0]
-    project(jnp.concatenate(fields, 0), gains[0:1], attend_in, cells, query, key, value)
+    project(jnp.concatenate(fields, 0), gains[0, 0:1], attend_in, cells, query, key, value)
     set_bias(bias, jnp.concatenate(bands_here, 1), jnp.concatenate(masks_here, 1))
     attend(query, key, value, bias, context, cells, 3 * cells)
 
@@ -265,12 +265,12 @@
             home_end[...] = out
 
     fields = [jnp.concatenate(fields[1:], 0), fields[0]]
-    finish(fields, context, (2 * cells, cells), attend_out, gains[1:2], expand, contract, write)
+    finish(fields, context, (2 * cells, cells), attend_out, gains[0, 1:2], expand, contract, write)
 
 
 def between_kernel(
     cells_here, query, key, value, bias, gains, attend_out, expand, contract,
-    home, notes, next_gains, next_attend_in,
+    home, far, notes, next_gains, next_attend_in,
     home_side, next_query, next_key, next_value, next_bias, context,
 ):
     part = home_side.shape[0]
@@ -282,14 +282,15 @@
         home_side[...] = out.astype(BF16)
         kept.append(out.astype(BF16).astype(F32))
 
-    finish([near.astype(F32)], context, (0,), attend_out, gains[1:2], expand, contract, write)
+    finish([near.astype(F32)], context, (0,), attend_out, gains[0, 1:2], expand, contract, write)
     for index in range(2):
         set_bias(next_bias.at[index], notes[2 * index + 2 : 2 * index + 3],
                  notes[2 * index + 3 : 2 * index + 4])
     pieces = ((0, part, home[:part].astype(F32)),
-              (1, 0, jnp.concatenate([home[part:].astype(F32), kept[0]], 0)))
+              (0, 3 * part, far[:part].astype(F32)),
+              (1, 0, jnp.concatenate([home[part:].astype(F32), kept[0], far[part:].astype(F32)], 0)))
     for index, at, field in pieces:
-        project(field, next_gains[0:1], next_attend_in, at,
+        project(field, next_gains[1, 0:1], next_attend_in.at[1], at,
                 next_query.at[index], next_key.at[index], next_value.at[index])
 
 
@@ -297,19 +298,19 @@
     home, home_side, far, far_side, far_corner, near_end,
     early_query, early_key, early_value, bias,
     gains, attend_in, attend_out, expand, contract,
-    out_ref, query, key, value, context,
+    out_hbm, query, key, value, context, out_ref, sems,
 ):
     part = SH * SW
+    copies = []
     low, high = slice(0, part), slice(part, 2 * part)
     windows = (
         (near_end[...], home[low], far_corner[...], far[low]),
         (home[high], home_side[...], far[high], far_side[...]),
     )
     windows = [[piece.astype(F32) for piece in parts] for parts in windows]
-    pieces = ((0, 0, windows[0][0]), (0, 2 * part, jnp.concatenate(windows[0][2:], 0)),
-              (1, 2 * part, jnp.concatenate(windows[1][2:], 0)))
+    pieces = ((0, 0, windows[0][0]), (0, 2 * part, windows[0][2]), (1, 3 * part, windows[1][3]))
     for index, at, field in pieces:
-        project(field, gains[0:1], attend_in, at, query.at[index], key.at[index], value.at[index])
+        project(field, gains[1, 0:1], attend_in.at[1], at, query.at[index], key.at[index], value.at[index])
     for index in range(len(windows)):
         attend(
             query.at[index], key.at[index], value.at[index], bias.at[index],
@@ -324,13 +325,18 @@
             near[window] = out
             return
         both = [piece.reshape(WH, SW, D) for piece in (out, near.pop(window))]
-        out_ref[pl.ds(window * WH, WH)] = jnp.concatenate(both, 1).astype(BF16)
+        rows = pl.ds(window * WH, WH)
+        out_ref[rows] = jnp.concatenate(both, 1).astype(BF16)
+        copies.append(pltpu.make_async_copy(out_ref.at[rows], out_hbm.at[rows], sems.at[window]))
+        copies[-1].start()
 
     lows = [2 * part * at for at in range(len(fields))]
-    finish(fields, context, lows, attend_out, gains[1:2], expand, contract, write)
-
-
-def call(kernel, name, shapes, specs, scratch, flops, *operands, limit=40, aliases=()):
+    finish(fields, context, lows, attend_out.at[1], gains[1, 1:2], expand.at[1], contract.at[1], write)
+    for copy in copies:
+        copy.wait()
+
+
+def call(kernel, name, shapes, specs, scratch, flops, *operands, limit=40, aliases=(), outs=VMEM):
     size = sum(operand.size * operand.dtype.itemsize for operand in operands)
     shapes = [shape if isinstance(shape, jax.ShapeDtypeStruct) else jax.ShapeDtypeStruct(shape, BF16)
               for shape in shapes]
@@ -338,7 +344,7 @@
         kernel,
         out_shape=shapes,
         in_specs=specs,
-        out_specs=[VMEM] * len(shapes),
+        out_specs=[outs] + [VMEM] * (len(shapes) - 1),
         scratch_shapes=scratch,
         compiler_params=pltpu.CompilerParams(vmem_limit_bytes=limit * 2**20),
         cost_estimate=pl.CostEstimate(flops=flops, bytes_accessed=size, transcendentals=0),
@@ -381,7 +387,8 @@
     far_main = moved(main, -1, 0)
 
     weights = [
-        (norm_gains[k], attend_in[k], attend_out[k], expand[k], contract[k]) for k in range(2)
+        (norm_gains, attend_in[0], attend_out[0], expand[0], contract[0]),
+        (norm_gains, attend_in, attend_out, expand, contract),
     ]
     side, corner, row_end, here, *near, notes = call(
         early_kernel, "early",
@@ -410,19 +417,20 @@
     home_side, *inside = call(
         between_kernel, "between",
         [(quarter, D)] + [pair] * 3 + [jax.ShapeDtypeStruct((2, cells, cells), F32)],
-        [VMEM] * 13, [wide], flops // 4 + each * 3 * quarter,
+        [VMEM] * 14, [wide], flops // 4 + each * 5 * quarter,
         here, *inside, weights[0][0], *weights[0][2:],
-        home, notes, *weights[1][:2],
+        home, back_main, notes, *weights[1][:2],
     )
     back_side = moved(away_side, 1, 0)
     back_corner = moved(away_corner, 1, 1)
     back_end = moved(home_end, 0, 1)
     return call(
         second_kernel, "second", [(height, breadth, D)] + [pair] * 3, [VMEM] * 15,
-        [pltpu.VMEM((2 * cells, D), BF16)],
+        [pltpu.VMEM((2 * cells, D), BF16), pltpu.VMEM(atmosphere.shape, BF16),
+         pltpu.SemaphoreType.DMA((2,))],
         2 * flops + each * 5 * quarter,
         home, home_side, back_main, back_side, back_corner, back_end, *inside, *weights[1],
-        aliases=((6, 1), (7, 2), (8, 3)),
+        aliases=((6, 1), (7, 2), (8, 3)), outs=HBM,
     )[0]
 
 

time: 50.5 us -> 49.3 us (0.976)
  Pallas kernels: 28.4 us -> 31.8 us
  local copies, waits for them, and re-layouts: 4.54 us -> 1.72 us
  waiting for transfers between devices: 5.03 us -> 3.1 us
    pallas_call x6, Pallas kernels: 28.4 us -> 31.8 us  [call(): pl.pallas_call(kernel, out_shape=shapes, in_specs=specs, out_specs=[outs]...]
    ppermute x8, waiting for transfers between devices: 5.03 us -> 3.1 us  [moved(): return lax.ppermute(value, ('lon', 'lat'), pairs)]
    squeeze x5 -> x4, local copies, waits for them, and re-layouts: 3.25 us -> 1.68 us  [the longest x1 1.51 us: on_device(): attend_in[0]]
    unnamed x14 -> x16, local copies, waits for them, and re-layouts: 1.28 us -> 0.04 us
  transfers between devices with their start and end apart: 8 -> 8, of which waited for: 2 -> 3; matrix products, arithmetic and copies ran while one was open for 6% -> 3% of each run, Pallas kernels for 30% -> 36%
where the time goes in v5:
time: 49.3 us; the launch traced here: 48.6 us
  Pallas kernels  31.8 us (65%)
  starting transfers between devices  11.7 us (24%)
  waiting for transfers between devices  3.1 us (6%)
  local copies, waits for them, and re-layouts  1.72 us (3%)
    pallas_call x6, Pallas kernels, call(): pl.pallas_call(kernel, out_shape=shapes, in_specs=specs, out_specs=[outs]...  31.8 us
    ppermute x8, starting transfers between devices, moved(): return lax.ppermute(value, ('lon', 'lat'), pairs)  11.7 us
    ppermute x8, waiting for transfers between devices, moved(): return lax.ppermute(value, ('lon', 'lat'), pairs)  3.1 us
    squeeze x1, local copies, waits for them, and re-layouts, on_device(): attend_in[0]  1.51 us
  transfers between devices with their start and end apart: 8, of which 3 were waited for; matrix products, arithmetic and copies ran while one was open for 3% of the time, Pallas kernels for 36%

profile of v5, /device:TPU:0, one launch (start us, length us, event | category | flops | bytes accessed | tf_op | source)
XLA Modules:
  0.0 48.6 jit_solution(16480908121212652654)
XLA Ops:
  0.0 1.9 %pack_main.1 = (bf16[272,512]{1,0:T(8,128)(2,1)}, bf16[16,128]{1,0:T(8,128)(2,1)}) custom-call(bf16[64,16,512]{2,1,0:T(8,128)(2,1)} %block.1, s32[16,64]{1,0:T(8,128)} %bitcast.9), custom_call_target="tpu_custom_call" | custom-call | flops 1000000 | bytes 1052672 | tf_op jit(solution)/shard_map/pack_main/pallas_call | solution.py:343
  1.9 6.1 %collective-permute-start = (bf16[272,512]{1,0:T(8,128)(2,1)}, bf16[272,512]{1,0:T(8,128)(2,1)S(1)}, u32[]{:S(2)}, u32[]{:S(2)}) collective-permute-start(bf16[272,512]{1,0:T(8,128)(2,1)} %get-tuple-element.33), channel_id=1, source_target_pairs={{0,14},{1,15},{2,0},{3,1},{4,2},{5,3},{6,4},{7,5},{8,6},{9,7},{10,... | collective-permute-start | bytes 835592 | tf_op jit(solution)/shard_map/ppermute | solution.py:369
  8.0 1.5 %slice_bitcast_fusion.attend_in = bf16[512,1536]{1,0:T(8,128)(2,1)S(1)} fusion(bf16[2,512,1536]{2,1,0:T(8,128)(2,1)} %attend_in.1), kind=kLoop, calls=%fused_computation | loop fusion | bytes 3145728 | tf_op jit(solution)/shard_map/squeeze | solution.py:390
  9.5 0.0 copy-start.1
  9.6 0.0 copy-start.3
  9.6 1.6 %early.1 = (bf16[144,512]{1,0:T(8,128)(2,1)S(1)}, bf16[144,512]{1,0:T(8,128)(2,1)S(1)}, bf16[144,512]{1,0:T(8,128)(2,1)S(1)}, bf16[384,512]{1,0:T(8,128)(2,1)S(1...) custom-call(bf16[64,16,512]{2,1,0:T(8,128)(2,1)S(1)} %copy-done, ...), custom_call_target="tpu_custom_call" | custom-call | flops 603979776 | bytes 2638080 | tf_op jit(solution)/shard_map/early/pallas_call | solution.py:343
  11.2 0.0 copy-start.2
  11.2 0.6 %collective-permute-start.1 = (bf16[144,512]{1,0:T(8,128)(2,1)S(1)}, bf16[144,512]{1,0:T(8,128)(2,1)S(1)}, u32[]{:S(2)}, u32[]{:S(2)}) collective-permute-start(bf16[144,512]{1,0:T(8,128)(2,1)S(1)} %get-tuple-element.38), channel_id=1, source_target_pairs={{0,14},{1,15},{2,0},{3,1},{4,2},{5,3},{6,4},{7,5},{8,6},{9,7},{10,... | collective-permute-start | bytes 442376 | tf_op jit(solution)/shard_map/ppermute | solution.py:369
  11.8 0.3 collective-permute-start.2
  12.0 1.2 %collective-permute-start.3 = (bf16[144,512]{1,0:T(8,128)(2,1)S(1)}, bf16[144,512]{1,0:T(8,128)(2,1)S(1)}, u32[]{:S(2)}, u32[]{:S(2)}) collective-permute-start(bf16[144,512]{1,0:T(8,128)(2,1)S(1)} %get-tuple-element.40), channel_id=1, source_target_pairs={{0,1},{1,0},{2,3},{3,2},{4,5},{5,4},{6,7},{7,6},{8,9},{9,8},{10,11... | collective-permute-start | bytes 442376 | tf_op jit(solution)/shard_map/ppermute | solution.py:369
  13.3 0.1 slice_bitcast_fusion.2.expand
  13.4 0.1 slice_bitcast_fusion.1.contract
  13.5 1.9 %collective-permute-done.taken = bf16[272,512]{1,0:T(8,128)(2,1)S(1)} collective-permute-done((bf16[272,512]{1,0:T(8,128)(2,1)}, bf16[272,512]{1,0:T(8,128)(2,1)S(1)}, u32[]{:S(2)}, u32[]{:S(2)}) %collective-permute-start) | collective-permute-done | bytes 278560 | tf_op jit(solution)/shard_map/ppermute | solution.py:369
  15.4 5.3 %window_a.1 = (bf16[256,512]{1,0:T(8,128)(2,1)S(1)}, bf16[256,512]{1,0:T(8,128)(2,1)S(1)}) custom-call(bf16[384,512]{1,0:T(8,128)(2,1)S(1)} %get-tuple-element.31.cells_here, f32[16,512]{1,0:T(8,128)S(1)} %get-tuple-element.32.notes, bf16[272,512]{1,0:T(8,128)(2,1)S(1)} %collective-permute-done.taken, bf16[384,512]{1,0:T(8,128)(2,1)S(1)} %get-tuple-element.34.near_query, ...), custom_call_target="tpu_custom_call" | custom-call | flops 2281701376 | bytes 6086656 | tf_op jit(solution)/shard_map/window_a/pallas_call | solution.py:343
  20.7 0.3 collective-permute-start.4
  21.0 0.0 collective-permute-done.3.taken_end
  21.0 5.0 %window_b_away.1 = (bf16[128,512]{1,0:T(8,128)(2,1)S(1)}, bf16[128,512]{1,0:T(8,128)(2,1)S(1)}, bf16[128,512]{1,0:T(8,128)(2,1)S(1)}, bf16[512,512]{1,0:T(8,128)...) custom-call(bf16[256,512]{1,0:T(8,128)(2,1)S(1)} %get-tuple-element.37.window_a_first., ...), custom_call_target="tpu_custom_call" | custom-call | flops 2013265920 | bytes 6119424 | tf_op jit(solution)/shard_map/window_b_away/pallas_call | solution.py:343
  26.1 1.0 %collective-permute-start.5 = (bf16[128,512]{1,0:T(8,128)(2,1)S(1)}, bf16[128,512]{1,0:T(8,128)(2,1)S(1)}, u32[]{:S(2)}, u32[]{:S(2)}) collective-permute-start(bf16[128,512]{1,0:T(8,128)(2,1)S(1)} %get-tuple-element.47), channel_id=1, source_target_pairs={{0,2},{1,3},{2,4},{3,5},{4,6},{5,7},{6,8},{7,9},{8,10},{9,11},{10,... | collective-permute-start | bytes 393224 | tf_op jit(solution)/shard_map/ppermute | solution.py:369
  27.1 0.0 collective-permute-start.6
  27.1 2.2 %collective-permute-start.7 = (bf16[128,512]{1,0:T(8,128)(2,1)S(1)}, bf16[128,512]{1,0:T(8,128)(2,1)S(1)}, u32[]{:S(2)}, u32[]{:S(2)}) collective-permute-start(bf16[128,512]{1,0:T(8,128)(2,1)S(1)} %get-tuple-element.49), channel_id=1, source_target_pairs={{0,1},{1,0},{2,3},{3,2},{4,5},{5,4},{6,7},{7,6},{8,9},{9,8},{10,11... | collective-permute-start | bytes 393224 | tf_op jit(solution)/shard_map/ppermute | solution.py:369
  29.3 0.9 %collective-permute-done.4.far = bf16[256,512]{1,0:T(8,128)(2,1)S(1)} collective-permute-done((bf16[256,512]{1,0:T(8,128)(2,1)S(1)}, bf16[256,512]{1,0:T(8,128)(2,1)S(1)}, u32[]{:S(2)}, u32[]{:S(2)}) %collective-permute-start.4) | collective-permute-done | bytes 262176 | tf_op jit(solution)/shard_map/ppermute | solution.py:369
  30.2 5.3 %between.1 = (bf16[128,512]{1,0:T(8,128)(2,1)S(1)}, bf16[2,512,512]{2,1,0:T(8,128)(2,1)S(1)}, bf16[2,512,512]{2,1,0:T(8,128)(2,1)S(1)}, bf16[2,512,512]{2,1,0:T(8,128)(2,1)S(1)}, f32[2,512,512]{2,1,0:T(8,128)S(1)}) custom-call(bf16[384,512]{1,0:T(8,128)(2,1)S(1)} %get-tuple-element.31.cells_here, bf16[512,512]{1,0:T(8,128)(2,1)S(1)} %get-tuple-element.41.query, ...), custom_call_target="tpu_custom_call" | custom-call | flops 1476395008 | bytes 9355264 | tf_op jit(solution)/shard_map/between/pallas_call | solution.py:343
  35.5 0.3 collective-permute-done.6.far_corner
  35.9 12.6 %second.1 = (bf16[64,16,512]{2,1,0:T(8,128)(2,1)}, bf16[2,512,512]{2,1,0:T(8,128)(2,1)S(1)}, bf16[2,512,512]{2,1,0:T(8,128)(2,1)S(1)}, bf16[2,512,512]{2,1,0:T(8,128)(2,1)S(1)}) custom-call(bf16[256,512]{1,0:T(8,128)(2,1)S(1)} %get-tuple-element.37.window_a_first.home, ...), custom_call_target="tpu_custom_call", output_to_operand_aliasing={{1}: (6, {}), {2}: (7, {}), {3}: (8, {})} | custom-call | flops 4764729344 | bytes 14688256 | tf_op jit(solution)/shard_map/second/pallas_call | solution.py:343
  (18 shorter events, 0.1 us)
Async XLA Ops:
  0.0 9.5 %copy-start = (bf16[64,16,512]{2,1,0:T(8,128)(2,1)S(1)}, bf16[64,16,512]{2,1,0:T(8,128)(2,1)}, u32[]{:S(2)}) copy-start(bf16[64,16,512]{2,1,0:T(8,128)(2,1)} %block.1) | copy-start | bytes 3145732
  0.0 9.5 %copy-start.4 = (f32[2,2,512]{2,1,0:T(2,128)S(1)}, f32[2,2,512]{2,1,0:T(2,128)}, u32[]{:S(2)}) copy-start(f32[2,2,512]{2,1,0:T(2,128)} %gains.9) | copy-start | bytes 24580
  0.0 9.5 %copy-start.5 = (s32[64,16]{0,1:T(8,128)S(1)}, s32[64,16]{0,1:T(8,128)}, u32[]{:S(2)}) copy-start(s32[64,16]{0,1:T(8,128)} %param.10) | copy-start | bytes 12292
  0.0 9.5 %copy-start.7 = (s32[64]{0:T(128)S(1)}, s32[64]{0:T(128)}, u32[]{:S(2)}) copy-start(s32[64]{0:T(128)} %bands.1) | copy-start | bytes 772
  1.9 7.6 %copy-start.6 = (bf16[16,128]{1,0:T(8,128)(2,1)S(1)}, bf16[16,128]{1,0:T(8,128)(2,1)}, u32[]{:S(2)}) copy-start(bf16[16,128]{1,0:T(8,128)(2,1)} %get-tuple-element.30.token) | copy-start | bytes 12292
  1.9 13.4 %collective-permute-start = (bf16[272,512]{1,0:T(8,128)(2,1)}, bf16[272,512]{1,0:T(8,128)(2,1)S(1)}, u32[]{:S(2)}, u32[]{:S(2)}) collective-permute-start(bf16[272,512]{1,0:T(8,128)(2,1)} %get-tuple-element.33), channel_id=1, source_target_pairs={{0,14},{1,15},{2,0},{3,1},{4,2},{5,3},{6,4},{7,5},{8,6},{9,7},{10,... | collective-permute-start | bytes 835592 | tf_op jit(solution)/shard_map/ppermute | solution.py:369
  9.5 3.8 %copy-start.1 = (bf16[2,512,1024]{2,1,0:T(8,128)(2,1)S(1)}, bf16[2,512,1024]{2,1,0:T(8,128)(2,1)}, u32[]{:S(2)}) copy-start(bf16[2,512,1024]{2,1,0:T(8,128)(2,1)} %expand.1) | copy-start | bytes 6291460
  9.6 3.8 %copy-start.3 = (bf16[2,512,512]{2,1,0:T(8,128)(2,1)S(1)}, bf16[2,512,512]{2,1,0:T(8,128)(2,1)}, u32[]{:S(2)}) copy-start(bf16[2,512,512]{2,1,0:T(8,128)(2,1)} %attend_out.1) | copy-start | bytes 3145732
  11.2 2.2 %copy-start.2 = (bf16[2,1024,512]{2,1,0:T(8,128)(2,1)S(1)}, bf16[2,1024,512]{2,1,0:T(8,128)(2,1)}, u32[]{:S(2)}) copy-start(bf16[2,1024,512]{2,1,0:T(8,128)(2,1)} %contract.1) | copy-start | bytes 6291460
  11.2 9.8 %collective-permute-start.1 = (bf16[144,512]{1,0:T(8,128)(2,1)S(1)}, bf16[144,512]{1,0:T(8,128)(2,1)S(1)}, u32[]{:S(2)}, u32[]{:S(2)}) collective-permute-start(bf16[144,512]{1,0:T(8,128)(2,1)S(1)} %get-tuple-element.38), channel_id=1, source_target_pairs={{0,14},{1,15},{2,0},{3,1},{4,2},{5,3},{6,4},{7,5},{8,6},{9,7},{10,... | collective-permute-start | bytes 442376 | tf_op jit(solution)/shard_map/ppermute | solution.py:369
  11.8 9.2 %collective-permute-start.2 = (bf16[144,512]{1,0:T(8,128)(2,1)S(1)}, bf16[144,512]{1,0:T(8,128)(2,1)S(1)}, u32[]{:S(2)}, u32[]{:S(2)}) collective-permute-start(bf16[144,512]{1,0:T(8,128)(2,1)S(1)} %get-tuple-element.39), channel_id=1, source_target_pairs={{0,15},{1,14},{2,1},{3,0},{4,3},{5,2},{6,5},{7,4},{8,7},{9,6},{10,... | collective-permute-start | bytes 442376 | tf_op jit(solution)/shard_map/ppermute | solution.py:369
  12.0 9.0 %collective-permute-start.3 = (bf16[144,512]{1,0:T(8,128)(2,1)S(1)}, bf16[144,512]{1,0:T(8,128)(2,1)S(1)}, u32[]{:S(2)}, u32[]{:S(2)}) collective-permute-start(bf16[144,512]{1,0:T(8,128)(2,1)S(1)} %get-tuple-element.40), channel_id=1, source_target_pairs={{0,1},{1,0},{2,3},{3,2},{4,5},{5,4},{6,7},{7,6},{8,9},{9,8},{10,11... | collective-permute-start | bytes 442376 | tf_op jit(solution)/shard_map/ppermute | solution.py:369
  20.7 9.5 %collective-permute-start.4 = (bf16[256,512]{1,0:T(8,128)(2,1)S(1)}, bf16[256,512]{1,0:T(8,128)(2,1)S(1)}, u32[]{:S(2)}, u32[]{:S(2)}) collective-permute-start(bf16[256,512]{1,0:T(8,128)(2,1)S(1)} %get-tuple-element.45), channel_id=1, source_target_pairs={{0,2},{1,3},{2,4},{3,5},{4,6},{5,7},{6,8},{7,9},{8,10},{9,11},{10,... | collective-permute-start | bytes 786440 | tf_op jit(solution)/shard_map/ppermute | solution.py:369
  26.1 9.5 %collective-permute-start.5 = (bf16[128,512]{1,0:T(8,128)(2,1)S(1)}, bf16[128,512]{1,0:T(8,128)(2,1)S(1)}, u32[]{:S(2)}, u32[]{:S(2)}) collective-permute-start(bf16[128,512]{1,0:T(8,128)(2,1)S(1)} %get-tuple-element.47), channel_id=1, source_target_pairs={{0,2},{1,3},{2,4},{3,5},{4,6},{5,7},{6,8},{7,9},{8,10},{9,11},{10,... | collective-permute-start | bytes 393224 | tf_op jit(solution)/shard_map/ppermute | solution.py:369
  27.1 8.8 %collective-permute-start.6 = (bf16[128,512]{1,0:T(8,128)(2,1)S(1)}, bf16[128,512]{1,0:T(8,128)(2,1)S(1)}, u32[]{:S(2)}, u32[]{:S(2)}) collective-permute-start(bf16[128,512]{1,0:T(8,128)(2,1)S(1)} %get-tuple-element.48), channel_id=1, source_target_pairs={{0,3},{1,2},{2,5},{3,4},{4,7},{5,6},{6,9},{7,8},{8,11},{9,10},{10,... | collective-permute-start | bytes 393224 | tf_op jit(solution)/shard_map/ppermute | solution.py:369
  27.1 8.8 %collective-permute-start.7 = (bf16[128,512]{1,0:T(8,128)(2,1)S(1)}, bf16[128,512]{1,0:T(8,128)(2,1)S(1)}, u32[]{:S(2)}, u32[]{:S(2)}) collective-permute-start(bf16[128,512]{1,0:T(8,128)(2,1)S(1)} %get-tuple-element.49), channel_id=1, source_target_pairs={{0,1},{1,0},{2,3},{3,2},{4,5},{5,4},{6,7},{7,6},{8,9},{9,8},{10,11... | collective-permute-start | bytes 393224 | tf_op jit(solution)/shard_map/ppermute | solution.py:369

commit v6 on v5

--- a/solution.py
+++ b/solution.py
@@ -270,9 +270,20 @@
 
 def between_kernel(
     cells_here, query, key, value, bias, gains, attend_out, expand, contract,
-    home, far, notes, next_gains, next_attend_in,
-    home_side, next_query, next_key, next_value, next_bias, context,
-):
+    home, far, notes, next_gains, attend_in_hbm, attend_out_hbm, expand_hbm, contract_hbm,
+    home_side, next_query, next_key, next_value, next_bias,
+    next_attend_in, next_attend_out, next_expand, next_contract, context, sems,
+):
+    loads = (
+        (attend_in_hbm, next_attend_in), (attend_out_hbm, next_attend_out),
+        (expand_hbm, next_expand), (contract_hbm, next_contract),
+    )
+    copies = [
+        pltpu.make_async_copy(source.at[1], target, sems.at[index])
+        for index, (source, target) in enumerate(loads)
+    ]
+    for copy in copies:
+        copy.start()
     part = home_side.shape[0]
     attend(query, key, value, bias, context, 0, part)
     near = cells_here[pl.ds(cells_here.shape[0] - part, part), :]
@@ -289,9 +300,12 @@
     pieces = ((0, part, home[:part].astype(F32)),
               (0, 3 * part, far[:part].astype(F32)),
               (1, 0, jnp.concatenate([home[part:].astype(F32), kept[0], far[part:].astype(F32)], 0)))
+    copies[0].wait()
     for index, at, field in pieces:
-        project(field, next_gains[1, 0:1], next_attend_in.at[1], at,
+        project(field, next_gains[1, 0:1], next_attend_in, at,
                 next_query.at[index], next_key.at[index], next_value.at[index])
+    for copy in copies[1:]:
+        copy.wait()
 
 
 def second_kernel(
@@ -310,7 +324,7 @@
     windows = [[piece.astype(F32) for piece in parts] for parts in windows]
     pieces = ((0, 0, windows[0][0]), (0, 2 * part, windows[0][2]), (1, 3 * part, windows[1][3]))
     for index, at, field in pieces:
-        project(field, gains[1, 0:1], attend_in.at[1], at, query.at[index], key.at[index], value.at[index])
+        project(field, gains[1, 0:1], attend_in, at, query.at[index], key.at[index], value.at[index])
     for index in range(len(windows)):
         attend(
             query.at[index], key.at[index], value.at[index], bias.at[index],
@@ -331,12 +345,12 @@
         copies[-1].start()
 
     lows = [2 * part * at for at in range(len(fields))]
-    finish(fields, context, lows, attend_out.at[1], gains[1, 1:2], expand.at[1], contract.at[1], write)
+    finish(fields, context, lows, attend_out, gains[1, 1:2], expand, contract, write)
     for copy in copies:
         copy.wait()
 
 
-def call(kernel, name, shapes, specs, scratch, flops, *operands, limit=40, aliases=(), outs=VMEM):
+def call(kernel, name, shapes, specs, scratch, flops, *operands, limit=32, aliases=(), outs=VMEM):
     size = sum(operand.size * operand.dtype.itemsize for operand in operands)
     shapes = [shape if isinstance(shape, jax.ShapeDtypeStruct) else jax.ShapeDtypeStruct(shape, BF16)
               for shape in shapes]
@@ -416,10 +430,11 @@
     pair = (2, cells, D)
     home_side, *inside = call(
         between_kernel, "between",
-        [(quarter, D)] + [pair] * 3 + [jax.ShapeDtypeStruct((2, cells, cells), F32)],
-        [VMEM] * 14, [wide], flops // 4 + each * 5 * quarter,
+        [(quarter, D)] + [pair] * 3 + [jax.ShapeDtypeStruct((2, cells, cells), F32)]
+        + [array.shape[1:] for array in weights[1][1:]],
+        [VMEM] * 13 + [HBM] * 4, [wide, pltpu.SemaphoreType.DMA((4,))], flops // 4 + each * 5 * quarter,
         here, *inside, weights[0][0], *weights[0][2:],
-        home, back_main, notes, *weights[1][:2],
+        home, back_main, notes, *weights[1],
     )
     back_side = moved(away_side, 1, 0)
     back_corner = moved(away_corner, 1, 1)
@@ -429,7 +444,7 @@
         [pltpu.VMEM((2 * cells, D), BF16), pltpu.VMEM(atmosphere.shape, BF16),
          pltpu.SemaphoreType.DMA((2,))],
         2 * flops + each * 5 * quarter,
-        home, home_side, back_main, back_side, back_corner, back_end, *inside, *weights[1],
+        home, home_side, back_main, back_side, back_corner, back_end, *inside[:4], norm_gains, *inside[4:],
         aliases=((6, 1), (7, 2), (8, 3)), outs=HBM,
     )[0]
 

time: 49.3 us -> 47.4 us (0.961)
  Pallas kernels: 31.8 us -> 28.6 us
  waiting for transfers between devices: 3.1 us -> 4.37 us
    pallas_call x6, Pallas kernels: 31.8 us -> 28.6 us  [call(): pl.pallas_call(kernel, out_shape=shapes, in_specs=specs, out_specs=[outs]...]
    ppermute x8, waiting for transfers between devices: 3.1 us -> 4.37 us  [moved(): return lax.ppermute(value, ('lon', 'lat'), pairs)]
  transfers between devices with their start and end apart: 8 -> 8, of which waited for: 3 -> 4; matrix products, arithmetic and copies ran while one was open for 3% -> 4% of each run, Pallas kernels for 36% -> 34%
where the time goes in v6:
time: 47.4 us; the launch traced here: 46.7 us
  Pallas kernels  28.6 us (60%)
  starting transfers between devices  11.7 us (25%)
  waiting for transfers between devices  4.37 us (9%)
  local copies, waits for them, and re-layouts  1.72 us (4%)
    pallas_call x6, Pallas kernels, call(): pl.pallas_call(kernel, out_shape=shapes, in_specs=specs, out_specs=[outs]...  28.6 us
    ppermute x8, starting transfers between devices, moved(): return lax.ppermute(value, ('lon', 'lat'), pairs)  11.7 us
    ppermute x8, waiting for transfers between devices, moved(): return lax.ppermute(value, ('lon', 'lat'), pairs)  4.37 us
    squeeze x1, local copies, waits for them, and re-layouts, on_device(): attend_in[0]  1.51 us
  transfers between devices with their start and end apart: 8, of which 4 were waited for; matrix products, arithmetic and copies ran while one was open for 4% of the time, Pallas kernels for 34%

profile of v6, /device:TPU:0, one launch (start us, length us, event | category | flops | bytes accessed | tf_op | source)
XLA Modules:
  0.0 46.7 jit_solution(12161268633041326115)
XLA Ops:
  0.0 1.9 %pack_main.1 = (bf16[272,512]{1,0:T(8,128)(2,1)}, bf16[16,128]{1,0:T(8,128)(2,1)}) custom-call(bf16[64,16,512]{2,1,0:T(8,128)(2,1)} %block.1, s32[16,64]{1,0:T(8,128)} %bitcast.9), custom_call_target="tpu_custom_call" | custom-call | flops 1000000 | bytes 1052672 | tf_op jit(solution)/shard_map/pack_main/pallas_call | solution.py:357
  1.9 6.1 %collective-permute-start = (bf16[272,512]{1,0:T(8,128)(2,1)}, bf16[272,512]{1,0:T(8,128)(2,1)S(1)}, u32[]{:S(2)}, u32[]{:S(2)}) collective-permute-start(bf16[272,512]{1,0:T(8,128)(2,1)} %get-tuple-element.37), channel_id=1, source_target_pairs={{0,14},{1,15},{2,0},{3,1},{4,2},{5,3},{6,4},{7,5},{8,6},{9,7},{10,... | collective-permute-start | bytes 835592 | tf_op jit(solution)/shard_map/ppermute | solution.py:383
  8.0 1.5 %slice_bitcast_fusion.attend_in = bf16[512,1536]{1,0:T(8,128)(2,1)S(1)} fusion(bf16[2,512,1536]{2,1,0:T(8,128)(2,1)} %attend_in_hbm.1), kind=kLoop, calls=%fused_computation | loop fusion | bytes 3145728 | tf_op jit(solution)/shard_map/squeeze | solution.py:404
  9.5 0.0 copy-start
  9.6 0.0 copy-start.3
  9.6 1.6 %early.1 = (bf16[144,512]{1,0:T(8,128)(2,1)S(1)}, bf16[144,512]{1,0:T(8,128)(2,1)S(1)}, bf16[144,512]{1,0:T(8,128)(2,1)S(1)}, bf16[384,512]{1,0:T(8,128)(2,1)S(1...) custom-call(bf16[64,16,512]{2,1,0:T(8,128)(2,1)S(1)} %copy-done.2, ...), custom_call_target="tpu_custom_call" | custom-call | flops 603979776 | bytes 2638080 | tf_op jit(solution)/shard_map/early/pallas_call | solution.py:357
  11.2 0.0 copy-start.1
  11.2 0.6 %collective-permute-start.1 = (bf16[144,512]{1,0:T(8,128)(2,1)S(1)}, bf16[144,512]{1,0:T(8,128)(2,1)S(1)}, u32[]{:S(2)}, u32[]{:S(2)}) collective-permute-start(bf16[144,512]{1,0:T(8,128)(2,1)S(1)} %get-tuple-element.42), channel_id=1, source_target_pairs={{0,14},{1,15},{2,0},{3,1},{4,2},{5,3},{6,4},{7,5},{8,6},{9,7},{10,... | collective-permute-start | bytes 442376 | tf_op jit(solution)/shard_map/ppermute | solution.py:383
  11.8 0.3 collective-permute-start.2
  12.0 1.2 %collective-permute-start.3 = (bf16[144,512]{1,0:T(8,128)(2,1)S(1)}, bf16[144,512]{1,0:T(8,128)(2,1)S(1)}, u32[]{:S(2)}, u32[]{:S(2)}) collective-permute-start(bf16[144,512]{1,0:T(8,128)(2,1)S(1)} %get-tuple-element.44), channel_id=1, source_target_pairs={{0,1},{1,0},{2,3},{3,2},{4,5},{5,4},{6,7},{7,6},{8,9},{9,8},{10,11... | collective-permute-start | bytes 442376 | tf_op jit(solution)/shard_map/ppermute | solution.py:383
  13.3 0.1 slice_bitcast_fusion.2.expand
  13.4 0.1 slice_bitcast_fusion.1.contract
  13.5 1.9 %collective-permute-done.taken = bf16[272,512]{1,0:T(8,128)(2,1)S(1)} collective-permute-done((bf16[272,512]{1,0:T(8,128)(2,1)}, bf16[272,512]{1,0:T(8,128)(2,1)S(1)}, u32[]{:S(2)}, u32[]{:S(2)}) %collective-permute-start) | collective-permute-done | bytes 278560 | tf_op jit(solution)/shard_map/ppermute | solution.py:383
  15.4 5.3 %window_a.1 = (bf16[256,512]{1,0:T(8,128)(2,1)S(1)}, bf16[256,512]{1,0:T(8,128)(2,1)S(1)}) custom-call(bf16[384,512]{1,0:T(8,128)(2,1)S(1)} %get-tuple-element.35.cells_here, f32[16,512]{1,0:T(8,128)S(1)} %get-tuple-element.36.notes, bf16[272,512]{1,0:T(8,128)(2,1)S(1)} %collective-permute-done.taken, bf16[384,512]{1,0:T(8,128)(2,1)S(1)} %get-tuple-element.38.near_query, ...), custom_call_target="tpu_custom_call" | custom-call | flops 2281701376 | bytes 6086656 | tf_op jit(solution)/shard_map/window_a/pallas_call | solution.py:357
  20.7 0.3 collective-permute-start.4
  21.0 0.0 collective-permute-done.1.taken_side
  21.0 5.0 %window_b_away.1 = (bf16[128,512]{1,0:T(8,128)(2,1)S(1)}, bf16[128,512]{1,0:T(8,128)(2,1)S(1)}, bf16[128,512]{1,0:T(8,128)(2,1)S(1)}, bf16[512,512]{1,0:T(8,128)...) custom-call(bf16[256,512]{1,0:T(8,128)(2,1)S(1)} %get-tuple-element.41.window_a_first., ...), custom_call_target="tpu_custom_call" | custom-call | flops 2013265920 | bytes 6119424 | tf_op jit(solution)/shard_map/window_b_away/pallas_call | solution.py:357
  26.1 1.0 %collective-permute-start.5 = (bf16[128,512]{1,0:T(8,128)(2,1)S(1)}, bf16[128,512]{1,0:T(8,128)(2,1)S(1)}, u32[]{:S(2)}, u32[]{:S(2)}) collective-permute-start(bf16[128,512]{1,0:T(8,128)(2,1)S(1)} %get-tuple-element.51), channel_id=1, source_target_pairs={{0,2},{1,3},{2,4},{3,5},{4,6},{5,7},{6,8},{7,9},{8,10},{9,11},{10,... | collective-permute-start | bytes 393224 | tf_op jit(solution)/shard_map/ppermute | solution.py:383
  27.1 2.2 %collective-permute-start.7 = (bf16[128,512]{1,0:T(8,128)(2,1)S(1)}, bf16[128,512]{1,0:T(8,128)(2,1)S(1)}, u32[]{:S(2)}, u32[]{:S(2)}) collective-permute-start(bf16[128,512]{1,0:T(8,128)(2,1)S(1)} %get-tuple-element.53), channel_id=1, source_target_pairs={{0,1},{1,0},{2,3},{3,2},{4,5},{5,4},{6,7},{7,6},{8,9},{9,8},{10,11... | collective-permute-start | bytes 393224 | tf_op jit(solution)/shard_map/ppermute | solution.py:383
  29.3 0.9 %collective-permute-done.4.far = bf16[256,512]{1,0:T(8,128)(2,1)S(1)} collective-permute-done((bf16[256,512]{1,0:T(8,128)(2,1)S(1)}, bf16[256,512]{1,0:T(8,128)(2,1)S(1)}, u32[]{:S(2)}, u32[]{:S(2)}) %collective-permute-start.4) | collective-permute-done | bytes 262176 | tf_op jit(solution)/shard_map/ppermute | solution.py:383
  30.2 4.1 %between.1 = (bf16[128,512]{1,0:T(8,128)(2,1)S(1)}, bf16[2,512,512]{2,1,0:T(8,128)(2,1)S(1)}, bf16[2,512,512]{2,1,0:T(8,128)(2,1)S(1)}, bf16[2,512,512]{2,1,0:T(...) custom-call(bf16[384,512]{1,0:T(8,128)(2,1)S(1)} %get-tuple-element., ...), custom_call_target="tpu_custom_call" | custom-call | flops 1476395008 | bytes 14598144 | tf_op jit(solution)/shard_map/between/pallas_call | solution.py:357
  34.3 1.1 %collective-permute-done.5.far_side = bf16[128,512]{1,0:T(8,128)(2,1)S(1)} collective-permute-done((bf16[128,512]{1,0:T(8,128)(2,1)S(1)}, bf16[128,512]{1,0:T(8,128)(2,1)S(1)}, u32[]{:S(2)}, u32[]{:S(2)}) %collective-permute-start.5) | collective-permute-done | bytes 131104 | tf_op jit(solution)/shard_map/ppermute | solution.py:383
  35.3 0.5 %collective-permute-done.6.far_corner = bf16[128,512]{1,0:T(8,128)(2,1)S(1)} collective-permute-done((bf16[128,512]{1,0:T(8,128)(2,1)S(1)}, bf16[128,512]{1,0:T(8,128)(2,1)S(1)}, u32[]{:S(2)}, u32[]{:S(2)}) %collective-permute-start.6) | collective-permute-done | bytes 131104 | tf_op jit(solution)/shard_map/ppermute | solution.py:383
  35.9 10.7 %second.1 = (bf16[64,16,512]{2,1,0:T(8,128)(2,1)}, bf16[2,512,512]{2,1,0:T(8,128)(2,1)S(1)}, bf16[2,512,512]{2,1,0:T(8,128)(2,1)S(1)}, bf16[2,512,512]{2,1,0:T(8,128)(2,1)S(1)}) custom-call(bf16[256,512]{1,0:T(8,128)(2,1)S(1)} %get-tuple-element.41.window_a_first.home, ...), custom_call_target="tpu_custom_call", output_to_operand_aliasing={{1}: (6, {}), {2}: (7, {}), {3}: (8, {})} | custom-call | flops 4764729344 | bytes 10493952 | tf_op jit(solution)/shard_map/second/pallas_call | solution.py:357
  (18 shorter events, 0.1 us)
Async XLA Ops:
  0.0 9.5 %copy-start.2 = (bf16[64,16,512]{2,1,0:T(8,128)(2,1)S(1)}, bf16[64,16,512]{2,1,0:T(8,128)(2,1)}, u32[]{:S(2)}) copy-start(bf16[64,16,512]{2,1,0:T(8,128)(2,1)} %block.1) | copy-start | bytes 3145732
  0.0 9.5 %copy-start.4 = (f32[2,2,512]{2,1,0:T(2,128)S(1)}, f32[2,2,512]{2,1,0:T(2,128)}, u32[]{:S(2)}) copy-start(f32[2,2,512]{2,1,0:T(2,128)} %gains.9) | copy-start | bytes 24580
  0.0 9.5 %copy-start.5 = (s32[64,16]{0,1:T(8,128)S(1)}, s32[64,16]{0,1:T(8,128)}, u32[]{:S(2)}) copy-start(s32[64,16]{0,1:T(8,128)} %param.10) | copy-start | bytes 12292
  0.0 9.5 %copy-start.7 = (s32[64]{0:T(128)S(1)}, s32[64]{0:T(128)}, u32[]{:S(2)}) copy-start(s32[64]{0:T(128)} %bands.1) | copy-start | bytes 772
  1.9 7.6 %copy-start.6 = (bf16[16,128]{1,0:T(8,128)(2,1)S(1)}, bf16[16,128]{1,0:T(8,128)(2,1)}, u32[]{:S(2)}) copy-start(bf16[16,128]{1,0:T(8,128)(2,1)} %get-tuple-element.34.token) | copy-start | bytes 12292
  1.9 13.4 %collective-permute-start = (bf16[272,512]{1,0:T(8,128)(2,1)}, bf16[272,512]{1,0:T(8,128)(2,1)S(1)}, u32[]{:S(2)}, u32[]{:S(2)}) collective-permute-start(bf16[272,512]{1,0:T(8,128)(2,1)} %get-tuple-element.37), channel_id=1, source_target_pairs={{0,14},{1,15},{2,0},{3,1},{4,2},{5,3},{6,4},{7,5},{8,6},{9,7},{10,... | collective-permute-start | bytes 835592 | tf_op jit(solution)/shard_map/ppermute | solution.py:383
  9.5 3.8 %copy-start = (bf16[2,512,1024]{2,1,0:T(8,128)(2,1)S(1)}, bf16[2,512,1024]{2,1,0:T(8,128)(2,1)}, u32[]{:S(2)}) copy-start(bf16[2,512,1024]{2,1,0:T(8,128)(2,1)} %expand_hbm.1) | copy-start | bytes 6291460
  9.6 3.8 %copy-start.3 = (bf16[2,512,512]{2,1,0:T(8,128)(2,1)S(1)}, bf16[2,512,512]{2,1,0:T(8,128)(2,1)}, u32[]{:S(2)}) copy-start(bf16[2,512,512]{2,1,0:T(8,128)(2,1)} %attend_out_hbm.1) | copy-start | bytes 3145732
  11.2 2.2 %copy-start.1 = (bf16[2,1024,512]{2,1,0:T(8,128)(2,1)S(1)}, bf16[2,1024,512]{2,1,0:T(8,128)(2,1)}, u32[]{:S(2)}) copy-start(bf16[2,1024,512]{2,1,0:T(8,128)(2,1)} %contract_hbm.1) | copy-start | bytes 6291460
  11.2 9.8 %collective-permute-start.1 = (bf16[144,512]{1,0:T(8,128)(2,1)S(1)}, bf16[144,512]{1,0:T(8,128)(2,1)S(1)}, u32[]{:S(2)}, u32[]{:S(2)}) collective-permute-start(bf16[144,512]{1,0:T(8,128)(2,1)S(1)} %get-tuple-element.42), channel_id=1, source_target_pairs={{0,14},{1,15},{2,0},{3,1},{4,2},{5,3},{6,4},{7,5},{8,6},{9,7},{10,... | collective-permute-start | bytes 442376 | tf_op jit(solution)/shard_map/ppermute | solution.py:383
  11.8 9.2 %collective-permute-start.2 = (bf16[144,512]{1,0:T(8,128)(2,1)S(1)}, bf16[144,512]{1,0:T(8,128)(2,1)S(1)}, u32[]{:S(2)}, u32[]{:S(2)}) collective-permute-start(bf16[144,512]{1,0:T(8,128)(2,1)S(1)} %get-tuple-element.43), channel_id=1, source_target_pairs={{0,15},{1,14},{2,1},{3,0},{4,3},{5,2},{6,5},{7,4},{8,7},{9,6},{10,... | collective-permute-start | bytes 442376 | tf_op jit(solution)/shard_map/ppermute | solution.py:383
  12.0 9.0 %collective-permute-start.3 = (bf16[144,512]{1,0:T(8,128)(2,1)S(1)}, bf16[144,512]{1,0:T(8,128)(2,1)S(1)}, u32[]{:S(2)}, u32[]{:S(2)}) collective-permute-start(bf16[144,512]{1,0:T(8,128)(2,1)S(1)} %get-tuple-element.44), channel_id=1, source_target_pairs={{0,1},{1,0},{2,3},{3,2},{4,5},{5,4},{6,7},{7,6},{8,9},{9,8},{10,11... | collective-permute-start | bytes 442376 | tf_op jit(solution)/shard_map/ppermute | solution.py:383
  20.7 9.5 %collective-permute-start.4 = (bf16[256,512]{1,0:T(8,128)(2,1)S(1)}, bf16[256,512]{1,0:T(8,128)(2,1)S(1)}, u32[]{:S(2)}, u32[]{:S(2)}) collective-permute-start(bf16[256,512]{1,0:T(8,128)(2,1)S(1)} %get-tuple-element.49), channel_id=1, source_target_pairs={{0,2},{1,3},{2,4},{3,5},{4,6},{5,7},{6,8},{7,9},{8,10},{9,11},{10,... | collective-permute-start | bytes 786440 | tf_op jit(solution)/shard_map/ppermute | solution.py:383
  26.1 9.3 %collective-permute-start.5 = (bf16[128,512]{1,0:T(8,128)(2,1)S(1)}, bf16[128,512]{1,0:T(8,128)(2,1)S(1)}, u32[]{:S(2)}, u32[]{:S(2)}) collective-permute-start(bf16[128,512]{1,0:T(8,128)(2,1)S(1)} %get-tuple-element.51), channel_id=1, source_target_pairs={{0,2},{1,3},{2,4},{3,5},{4,6},{5,7},{6,8},{7,9},{8,10},{9,11},{10,... | collective-permute-start | bytes 393224 | tf_op jit(solution)/shard_map/ppermute | solution.py:383
  27.1 8.8 %collective-permute-start.6 = (bf16[128,512]{1,0:T(8,128)(2,1)S(1)}, bf16[128,512]{1,0:T(8,128)(2,1)S(1)}, u32[]{:S(2)}, u32[]{:S(2)}) collective-permute-start(bf16[128,512]{1,0:T(8,128)(2,1)S(1)} %get-tuple-element.52), channel_id=1, source_target_pairs={{0,3},{1,2},{2,5},{3,4},{4,7},{5,6},{6,9},{7,8},{8,11},{9,10},{10,... | collective-permute-start | bytes 393224 | tf_op jit(solution)/shard_map/ppermute | solution.py:383
  27.1 8.8 %collective-permute-start.7 = (bf16[128,512]{1,0:T(8,128)(2,1)S(1)}, bf16[128,512]{1,0:T(8,128)(2,1)S(1)}, u32[]{:S(2)}, u32[]{:S(2)}) collective-permute-start(bf16[128,512]{1,0:T(8,128)(2,1)S(1)} %get-tuple-element.53), channel_id=1, source_target_pairs={{0,1},{1,0},{2,3},{3,2},{4,5},{5,4},{6,7},{7,6},{8,9},{9,8},{10,11... | collective-permute-start | bytes 393224 | tf_op jit(solution)/shard_map/ppermute | solution.py:383

commit v7 on v6

--- a/solution.py
+++ b/solution.py
@@ -22,6 +22,7 @@
 BF16 = jnp.bfloat16
 CLASSES = 128
 META = 16
+CHUNKS = 4
 QSCALE = math.log2(math.e) / math.sqrt(HD)
 TRANSPOSED_RIGHT = (((1,), (1,)), ((), ()))
 TRANSPOSED_LEFT = (((0,), (0,)), ((), ()))
@@ -91,12 +92,15 @@
                 state[piece] = stage(piece, state[piece])
 
 
-def project(field, gain, attend_in, at, query, key, value):
-    rows = pl.ds(at, field.shape[0])
+def project(field, gain, attend_in, *places):
     normed = normalize(field, gain)
-    query[rows, :] = (product(normed, attend_in[:, :D]) * QSCALE).astype(BF16)
-    key[rows, :] = product(normed, attend_in[:, D : 2 * D]).astype(BF16)
-    value[rows, :] = product(normed, attend_in[:, 2 * D :]).astype(BF16)
+    for kind in range(3):
+        result = product(normed, attend_in[:, kind * D : (kind + 1) * D])
+        result = (result * QSCALE if kind == 0 else result).astype(BF16)
+        done = 0
+        for refs, at, count in places:
+            refs[kind][pl.ds(at, count), :] = result[done : done + count]
+            done += count
 
 
 def set_bias(bias, bands, masks):
@@ -163,33 +167,74 @@
     in_turn(len(fields), (start, widen, bend, end))
 
 
-def pack_main_kernel(block_hbm, valid_hbm, main, token, block, valid, sems):
+def pack_main_kernel(block_hbm, valid_hbm, main_hbm, token, block, valid, main, in_sems, out_sems):
+    rows = block.shape[0]
+    cells = rows * SW
+    chunk = rows // CHUNKS
+    loads = [
+        pltpu.make_async_copy(
+            block_hbm.at[pl.ds(SH + at * chunk, chunk)], block.at[pl.ds(at * chunk, chunk)],
+            in_sems.at[at],
+        )
+        for at in range(CHUNKS)
+    ]
+    stores = [
+        pltpu.make_async_copy(main.at[part], main_hbm.at[part], out_sems.at[at])
+        for at, part in enumerate(
+            [pl.ds(at * chunk * SW, chunk * SW) for at in range(CHUNKS)] + [pl.ds(cells, META)]
+        )
+    ]
+    load_valid = pltpu.make_async_copy(valid_hbm, valid, in_sems.at[CHUNKS])
+    load_valid.start()
+    for load in loads:
+        load.start()
+    token[...] = jnp.zeros_like(token)
+    load_valid.wait()
+    masks = mask_lanes(valid, SH, 0, D)
+    main[pl.ds(cells, META), :] = meta_rows(masks, jnp.zeros_like(masks))
+    stores[CHUNKS].start()
+    for at in range(CHUNKS):
+        loads[at].wait()
+        part = half_columns(block[pl.ds(at * chunk, chunk)], 0)
+        main[pl.ds(at * chunk * SW, chunk * SW), :] = part.astype(BF16)
+        stores[at].start()
+    for store in stores:
+        store.wait()
+
+
+def pack_rest_kernel(
+    block_hbm, bands_hbm, valid_hbm, token_hbm, side, corner, row_end,
+    block, bands, valid, sems,
+):
     height = block_hbm.shape[0]
-    rows = height - 2 * SH
-    copies = (
-        pltpu.make_async_copy(valid_hbm, valid, sems.at[0]),
-        pltpu.make_async_copy(block_hbm.at[pl.ds(SH, rows)], block, sems.at[1]),
-    )
+    part = SH * SW
+    copies = [
+        pltpu.make_async_copy(source, target, sems.at[index])
+        for index, (source, target) in enumerate((
+            (bands_hbm, bands), (valid_hbm, valid),
+            (block_hbm.at[pl.ds(0, SH)], block.at[0]),
+            (block_hbm.at[pl.ds(height - SH, SH)], block.at[1]),
+        ))
+    ]
     for copy in copies:
         copy.start()
-    token[...] = jnp.zeros_like(token)
-    copies[0].wait()
-    masks = mask_lanes(valid, SH, 0, D)
-    main[pl.ds(rows * SW, META), :] = meta_rows(masks, jnp.zeros_like(masks))
-    copies[1].wait()
-    main[pl.ds(0, rows * SW), :] = half_columns(block[...], 0).astype(BF16)
-
-
-def early_kernel(
-    block, bands, valid, token, gains, attend_in,
-    side, corner, row_end, cells_here, query, key, value, notes,
+    places = ((side, height - SH, 1, 0), (corner, 0, 0, 0), (row_end, 0, 0, SW))
+    for copy in copies[:2]:
+        copy.wait()
+    for out, low, _, column in places:
+        masks = mask_lanes(valid, low, column, D)
+        out[pl.ds(part, META), :] = meta_rows(masks, band_lanes(bands, low, SH, D))
+    for copy in copies[2:]:
+        copy.wait()
+    for out, _, which, column in places:
+        out[pl.ds(0, part), :] = half_columns(block[which], column).astype(BF16)
+
+
+def near_kernel(
+    block, bands, valid, gains, attend_in, cells_here, query, key, value, notes,
 ):
     height = block.shape[0]
     part = SH * SW
-    for out, low, column in ((side, height - SH, 0), (corner, 0, 0), (row_end, 0, SW)):
-        out[pl.ds(0, part), :] = half_columns(block[low : low + SH], column).astype(BF16)
-        masks = mask_lanes(valid, low, column, D)
-        out[pl.ds(part, META), :] = meta_rows(masks, band_lanes(bands, low, SH, D))
     local = half_columns(block[SH:], SW)
     cells_here[...] = local.astype(BF16)
     window_notes = [
@@ -206,7 +251,7 @@
     for index, pair in enumerate(window_notes):
         for offset, lanes in enumerate(pair):
             notes[pl.ds(2 * index + offset, 1), :] = lanes
-    project(local, gains[0, 0:1], attend_in, 0, query, key, value)
+    project(local, gains[0, 0:1], attend_in, ((query, key, value), 0, local.shape[0]))
 
 
 def window_a_kernel(
@@ -219,7 +264,7 @@
         whole[pl.ds(0, cells), :] = near[pl.ds(0, cells), :]
     local = cells_here[pl.ds(0, cells), :].astype(F32)
     remote = taken[pl.ds(0, cells), :].astype(F32)
-    project(remote, gains[0, 0:1], attend_in, cells, query, key, value)
+    project(remote, gains[0, 0:1], attend_in, ((query, key, value), cells, cells))
     row_bands = notes[0:1, :cells]
     masks, _ = meta_of(taken, cells)
     set_bias(
@@ -253,7 +298,10 @@
         masks_here.append(masks)
         bands_here.append(row_bands)
     bands_here[2] = bands_here[0]
-    project(jnp.concatenate(fields, 0), gains[0, 0:1], attend_in, cells, query, key, value)
+    project(
+        jnp.concatenate(fields, 0), gains[0, 0:1], attend_in,
+        ((query, key, value), cells, 3 * cells),
+    )
     set_bias(bias, jnp.concatenate(bands_here, 1), jnp.concatenate(masks_here, 1))
     attend(query, key, value, bias, context, cells, 3 * cells)
 
@@ -297,13 +345,14 @@
     for index in range(2):
         set_bias(next_bias.at[index], notes[2 * index + 2 : 2 * index + 3],
                  notes[2 * index + 3 : 2 * index + 4])
-    pieces = ((0, part, home[:part].astype(F32)),
-              (0, 3 * part, far[:part].astype(F32)),
-              (1, 0, jnp.concatenate([home[part:].astype(F32), kept[0], far[part:].astype(F32)], 0)))
     copies[0].wait()
-    for index, at, field in pieces:
-        project(field, next_gains[1, 0:1], next_attend_in, at,
-                next_query.at[index], next_key.at[index], next_value.at[index])
+    windows = [(next_query.at[at], next_key.at[at], next_value.at[at]) for at in range(2)]
+    field = [home[:part], far[:part], home[part:]]
+    field = [piece.astype(F32) for piece in field] + [kept[0], far[part:].astype(F32)]
+    project(
+        jnp.concatenate(field, 0), next_gains[1, 0:1], next_attend_in,
+        (windows[0], part, part), (windows[0], 3 * part, part), (windows[1], 0, 3 * part),
+    )
     for copy in copies[1:]:
         copy.wait()
 
@@ -322,9 +371,12 @@
         (home[high], home_side[...], far[high], far_side[...]),
     )
     windows = [[piece.astype(F32) for piece in parts] for parts in windows]
-    pieces = ((0, 0, windows[0][0]), (0, 2 * part, windows[0][2]), (1, 3 * part, windows[1][3]))
-    for index, at, field in pieces:
-        project(field, gains[1, 0:1], attend_in, at, query.at[index], key.at[index], value.at[index])
+    refs = [(query.at[at], key.at[at], value.at[at]) for at in range(2)]
+    project(
+        jnp.concatenate([windows[0][0], windows[0][2], windows[1][3]], 0),
+        gains[1, 0:1], attend_in,
+        (refs[0], 0, part), (refs[0], 2 * part, part), (refs[1], 3 * part, part),
+    )
     for index in range(len(windows)):
         attend(
             query.at[index], key.at[index], value.at[index], bias.at[index],
@@ -395,8 +447,9 @@
     valid_scratch = pltpu.VMEM(valid.shape, valid.dtype)
     main, token = call(
         pack_main_kernel, "pack_main", [(half + META, D), (META, 2 * HD)], [HBM] * 2,
-        [pltpu.VMEM((WH, breadth, D), BF16), valid_scratch, pltpu.SemaphoreType.DMA((2,))],
-        10**6, atmosphere, valid, limit=62,
+        [pltpu.VMEM((WH, breadth, D), BF16), valid_scratch, pltpu.VMEM((half + META, D), BF16),
+         pltpu.SemaphoreType.DMA((CHUNKS + 1,)), pltpu.SemaphoreType.DMA((CHUNKS + 1,))],
+        10**6, atmosphere, valid, limit=62, outs=HBM,
     )
     far_main = moved(main, -1, 0)
 
@@ -404,17 +457,24 @@
         (norm_gains, attend_in[0], attend_out[0], expand[0], contract[0]),
         (norm_gains, attend_in, attend_out, expand, contract),
     ]
-    side, corner, row_end, here, *near, notes = call(
-        early_kernel, "early",
-        [(quarter + META, D)] * 3 + [(half + quarter, D)] * 4
-        + [jax.ShapeDtypeStruct((META, D), F32)],
-        [VMEM, SMEM] + [VMEM] * 4, [], each * (half + quarter),
-        atmosphere, pole_band, valid, token, *weights[0][:2],
+    place = (atmosphere, pole_band, valid)
+    side, corner, row_end = call(
+        pack_rest_kernel, "pack_rest", [(quarter + META, D)] * 3,
+        [HBM] * 4,
+        [pltpu.VMEM((2, SH, breadth, D), BF16), pltpu.SMEM(pole_band.shape, pole_band.dtype),
+         valid_scratch, pltpu.SemaphoreType.DMA((4,))],
+        10**6, *place, token, limit=62,
     )
     far_side = moved(side, -1, 0)
     far_corner = moved(corner, -1, -1)
     near_end = moved(row_end, 0, -1)
 
+    here, *near, notes = call(
+        near_kernel, "near",
+        [(half + quarter, D)] * 4 + [jax.ShapeDtypeStruct((META, D), F32)],
+        [VMEM, SMEM] + [VMEM] * 3, [], each * (half + quarter),
+        *place, *weights[0][:2],
+    )
     away, home = call(
         window_a_kernel, "window_a", [(half, D)] * 2, [VMEM] * 11,
         [wide] * 3 + [bias_scratch, wide], flops + each * half,

time: 47.4 us -> 49.8 us (1.051)
  Pallas kernels: 28.6 us -> 30.8 us
  local copies, waits for them, and re-layouts: 1.72 us -> 2.61 us
    pallas_call x6 -> x7, Pallas kernels: 28.6 us -> 30.8 us  [call(): pl.pallas_call(kernel, out_shape=shapes, in_specs=specs, out_specs=[outs]...]
    squeeze x1, local copies, waits for them, and re-layouts: 1.51 us -> 0.1 us  [on_device(): attend_in[0]]
    squeeze x1, local copies, waits for them, and re-layouts: 0.07 us -> 1.3 us  [on_device(): expand[0]]
    unnamed x16, local copies, waits for them, and re-layouts: 0.04 us -> 1.11 us
  transfers between devices with their start and end apart: 8 -> 8, of which waited for: 4 -> 2; matrix products, arithmetic and copies ran while one was open for 4% -> 3% of each run, Pallas kernels for 34% -> 35%
where the time goes in v7:
time: 49.8 us; the launch traced here: 49.6 us
  Pallas kernels  30.8 us (62%)
  starting transfers between devices  11.5 us (23%)
  waiting for transfers between devices  4.42 us (9%)
  local copies, waits for them, and re-layouts  2.61 us (5%)
    pallas_call x7, Pallas kernels, call(): pl.pallas_call(kernel, out_shape=shapes, in_specs=specs, out_specs=[outs]...  30.8 us
    ppermute x8, starting transfers between devices, moved(): return lax.ppermute(value, ('lon', 'lat'), pairs)  11.5 us
    ppermute x8, waiting for transfers between devices, moved(): return lax.ppermute(value, ('lon', 'lat'), pairs)  4.42 us
    squeeze x1, local copies, waits for them, and re-layouts, on_device(): expand[0]  1.3 us
    unnamed x16, local copies, waits for them, and re-layouts  1.11 us
  transfers between devices with their start and end apart: 8, of which 2 were waited for; matrix products, arithmetic and copies ran while one was open for 3% of the time, Pallas kernels for 35%

profile of v7, /device:TPU:0, one launch (start us, length us, event | category | flops | bytes accessed | tf_op | source)
XLA Modules:
  0.0 49.6 jit_solution(7161359102385770166)
XLA Ops:
  0.0 2.5 %pack_main.1 = (bf16[272,512]{1,0:T(8,128)(2,1)}, bf16[16,128]{1,0:T(8,128)(2,1)}) custom-call(bf16[64,16,512]{2,1,0:T(8,128)(2,1)} %block_hbm.3, s32[16,64]{1,0:T(8,128)} %bitcast.9), custom_call_target="tpu_custom_call" | custom-call | flops 1000000 | bytes 1052672 | tf_op jit(solution)/shard_map/pack_main/pallas_call | solution.py:409
  2.5 6.1 %collective-permute-start = (bf16[272,512]{1,0:T(8,128)(2,1)}, bf16[272,512]{1,0:T(8,128)(2,1)S(1)}, u32[]{:S(2)}, u32[]{:S(2)}) collective-permute-start(bf16[272,512]{1,0:T(8,128)(2,1)} %get-tuple-element.36), channel_id=1, source_target_pairs={{0,14},{1,15},{2,0},{3,1},{4,2},{5,3},{6,4},{7,5},{8,6},{9,7},{10,... | collective-permute-start | bytes 835592 | tf_op jit(solution)/shard_map/ppermute | solution.py:435
  8.6 1.8 %pack_rest.1 = (bf16[144,512]{1,0:T(8,128)(2,1)}, bf16[144,512]{1,0:T(8,128)(2,1)}, bf16[144,512]{1,0:T(8,128)(2,1)}) custom-call(bf16[64,16,512]{2,1,0:T(8,128)(2,1)} %block_hbm.3, s32[64]{0:T(128)} %bands_hbm.1, s32[16,64]{1,0:T(8,128)} %bitcast.10, bf16[16,128]{1,0:T(8,128)(2,1)} %get-tuple-element.41.token_hbm), custom_call_target="tpu_custom_call" | custom-call | flops 1000000 | bytes 1057024 | tf_op jit(solution)/shard_map/pack_rest/pallas_call | solution.py:409
  10.4 0.0 copy-start.7
  10.4 0.6 %collective-permute-start.1 = (bf16[144,512]{1,0:T(8,128)(2,1)}, bf16[144,512]{1,0:T(8,128)(2,1)S(1)}, u32[]{:S(2)}, u32[]{:S(2)}) collective-permute-start(bf16[144,512]{1,0:T(8,128)(2,1)} %get-tuple-element.42), channel_id=1, source_target_pairs={{0,14},{1,15},{2,0},{3,1},{4,2},{5,3},{6,4},{7,5},{8,6},{9,7},{10,... | collective-permute-start | bytes 442376 | tf_op jit(solution)/shard_map/ppermute | solution.py:435
  11.0 0.3 collective-permute-start.2
  11.3 1.2 %collective-permute-start.3 = (bf16[144,512]{1,0:T(8,128)(2,1)}, bf16[144,512]{1,0:T(8,128)(2,1)S(1)}, u32[]{:S(2)}, u32[]{:S(2)}) collective-permute-start(bf16[144,512]{1,0:T(8,128)(2,1)} %get-tuple-element.44), channel_id=1, source_target_pairs={{0,1},{1,0},{2,3},{3,2},{4,5},{5,4},{6,7},{7,6},{8,9},{9,8},{10,11... | collective-permute-start | bytes 442376 | tf_op jit(solution)/shard_map/ppermute | solution.py:435
  12.6 1.3 %slice_bitcast_fusion.2.expand = bf16[512,1024]{1,0:T(8,128)(2,1)S(1)} fusion(bf16[2,512,1024]{2,1,0:T(8,128)(2,1)} %expand_hbm.1), kind=kLoop, calls=%fused_computation.2 | loop fusion | bytes 2097152 | tf_op jit(solution)/shard_map/squeeze | solution.py:457
  13.9 0.0 copy-start
  13.9 0.0 copy-start.4
  13.9 0.0 copy-start.5
  13.9 0.1 slice_bitcast_fusion.attend_in
  14.0 1.1 %copy-done = bf16[64,16,512]{2,1,0:T(8,128)(2,1)S(1)} copy-done((bf16[64,16,512]{2,1,0:T(8,128)(2,1)S(1)}, bf16[64,16,512]{2,1,0:T(8,128)(2,1)}, u32[]{:S(2)}) %copy-start) | copy-done | bytes 1048600
  15.1 1.6 %near.1 = (bf16[384,512]{1,0:T(8,128)(2,1)S(1)}, bf16[384,512]{1,0:T(8,128)(2,1)S(1)}, bf16[384,512]{1,0:T(8,128)(2,1)S(1)}, bf16[384,512]{1,0:T(8,128)(2,1)S(1)}, f32[16,512]{1,0:T(8,128)S(1)}) custom-call(bf16[64,16,512]{2,1,0:T(8,128)(2,1)S(1)} %copy-done, s32[64]{0:T(128)S(1)} %copy-done.6, s32[16,64]{1,0:T(8,128)S(1)} %bitcast.11, ...), custom_call_target="tpu_custom_call" | custom-call | flops 603979776 | bytes 2633984 | tf_op jit(solution)/shard_map/near/pallas_call | solution.py:409
  16.7 0.1 slice_bitcast_fusion.1.contract
  16.8 5.3 %window_a.1 = (bf16[256,512]{1,0:T(8,128)(2,1)S(1)}, bf16[256,512]{1,0:T(8,128)(2,1)S(1)}) custom-call(bf16[384,512]{1,0:T(8,128)(2,1)S(1)} %get-tuple-element.34.cells_here, f32[16,512]{1,0:T(8,128)S(1)} %get-tuple-element.35.notes, bf16[272,512]{1,0:T(8,128)(2,1)S(1)} %collective-permute-done.taken, bf16[384,512]{1,0:T(8,128)(2,1)S(1)} %get-tuple-element.37.near_query, ...), custom_call_target="tpu_custom_call" | custom-call | flops 2281701376 | bytes 6086656 | tf_op jit(solution)/shard_map/window_a/pallas_call | solution.py:409
  22.1 0.7 %collective-permute-start.4 = (bf16[256,512]{1,0:T(8,128)(2,1)S(1)}, bf16[256,512]{1,0:T(8,128)(2,1)S(1)}, u32[]{:S(2)}, u32[]{:S(2)}) collective-permute-start(bf16[256,512]{1,0:T(8,128)(2,1)S(1)} %get-tuple-element.49), channel_id=1, source_target_pairs={{0,2},{1,3},{2,4},{3,5},{4,6},{5,7},{6,8},{7,9},{8,10},{9,11},{10,... | collective-permute-start | bytes 786440 | tf_op jit(solution)/shard_map/ppermute | solution.py:435
  22.8 4.8 %window_b_away.1 = (bf16[128,512]{1,0:T(8,128)(2,1)S(1)}, bf16[128,512]{1,0:T(8,128)(2,1)S(1)}, bf16[128,512]{1,0:T(8,128)(2,1)S(1)}, bf16[512,512]{1,0:T(8,128)...) custom-call(bf16[256,512]{1,0:T(8,128)(2,1)S(1)} %get-tuple-element.40.window_a_first., ...), custom_call_target="tpu_custom_call" | custom-call | flops 2013265920 | bytes 6119424 | tf_op jit(solution)/shard_map/window_b_away/pallas_call | solution.py:409
  27.7 2.5 %collective-permute-start.5 = (bf16[128,512]{1,0:T(8,128)(2,1)S(1)}, bf16[128,512]{1,0:T(8,128)(2,1)S(1)}, u32[]{:S(2)}, u32[]{:S(2)}) collective-permute-start(bf16[128,512]{1,0:T(8,128)(2,1)S(1)} %get-tuple-element.51), channel_id=1, source_target_pairs={{0,2},{1,3},{2,4},{3,5},{4,6},{5,7},{6,8},{7,9},{8,10},{9,11},{10,... | collective-permute-start | bytes 393224 | tf_op jit(solution)/shard_map/ppermute | solution.py:435
  30.2 0.2 collective-permute-start.7
  30.3 3.0 %collective-permute-done.4.far = bf16[256,512]{1,0:T(8,128)(2,1)S(1)} collective-permute-done((bf16[256,512]{1,0:T(8,128)(2,1)S(1)}, bf16[256,512]{1,0:T(8,128)(2,1)S(1)}, u32[]{:S(2)}, u32[]{:S(2)}) %collective-permute-start.4) | collective-permute-done | bytes 262176 | tf_op jit(solution)/shard_map/ppermute | solution.py:435
  33.4 4.0 %between.1 = (bf16[128,512]{1,0:T(8,128)(2,1)S(1)}, bf16[2,512,512]{2,1,0:T(8,128)(2,1)S(1)}, bf16[2,512,512]{2,1,0:T(8,128)(2,1)S(1)}, bf16[2,512,512]{2,1,0:T(...) custom-call(bf16[384,512]{1,0:T(8,128)(2,1)S(1)} %get-tuple-element., ...), custom_call_target="tpu_custom_call" | custom-call | flops 1476395008 | bytes 14598144 | tf_op jit(solution)/shard_map/between/pallas_call | solution.py:409
  37.3 1.4 %collective-permute-done.6.far_corner = bf16[128,512]{1,0:T(8,128)(2,1)S(1)} collective-permute-done((bf16[128,512]{1,0:T(8,128)(2,1)S(1)}, bf16[128,512]{1,0:T(8,128)(2,1)S(1)}, u32[]{:S(2)}, u32[]{:S(2)}) %collective-permute-start.6) | collective-permute-done | bytes 131104 | tf_op jit(solution)/shard_map/ppermute | solution.py:435
  38.7 10.7 %second.1 = (bf16[64,16,512]{2,1,0:T(8,128)(2,1)}, bf16[2,512,512]{2,1,0:T(8,128)(2,1)S(1)}, bf16[2,512,512]{2,1,0:T(8,128)(2,1)S(1)}, bf16[2,512,512]{2,1,0:T(8,128)(2,1)S(1)}) custom-call(bf16[256,512]{1,0:T(8,128)(2,1)S(1)} %get-tuple-element.40.window_a_first.home, ...), custom_call_target="tpu_custom_call", output_to_operand_aliasing={{1}: (6, {}), {2}: (7, {}), {3}: (8, {})} | custom-call | flops 4764729344 | bytes 10493952 | tf_op jit(solution)/shard_map/second/pallas_call | solution.py:409
  (19 shorter events, 0.1 us)
Async XLA Ops:
  0.0 12.5 %copy-start.3 = (bf16[2,512,512]{2,1,0:T(8,128)(2,1)S(1)}, bf16[2,512,512]{2,1,0:T(8,128)(2,1)}, u32[]{:S(2)}) copy-start(bf16[2,512,512]{2,1,0:T(8,128)(2,1)} %attend_out_hbm.1) | copy-start | bytes 3145732
  2.5 14.3 %collective-permute-start = (bf16[272,512]{1,0:T(8,128)(2,1)}, bf16[272,512]{1,0:T(8,128)(2,1)S(1)}, u32[]{:S(2)}, u32[]{:S(2)}) collective-permute-start(bf16[272,512]{1,0:T(8,128)(2,1)} %get-tuple-element.36), channel_id=1, source_target_pairs={{0,14},{1,15},{2,0},{3,1},{4,2},{5,3},{6,4},{7,5},{8,6},{9,7},{10,... | collective-permute-start | bytes 835592 | tf_op jit(solution)/shard_map/ppermute | solution.py:435
  10.4 3.4 %copy-start.7 = (bf16[2,512,1536]{2,1,0:T(8,128)(2,1)S(1)}, bf16[2,512,1536]{2,1,0:T(8,128)(2,1)}, u32[]{:S(2)}) copy-start(bf16[2,512,1536]{2,1,0:T(8,128)(2,1)} %attend_in_hbm.1) | copy-start | bytes 9437188
  10.4 12.4 %collective-permute-start.1 = (bf16[144,512]{1,0:T(8,128)(2,1)}, bf16[144,512]{1,0:T(8,128)(2,1)S(1)}, u32[]{:S(2)}, u32[]{:S(2)}) collective-permute-start(bf16[144,512]{1,0:T(8,128)(2,1)} %get-tuple-element.42), channel_id=1, source_target_pairs={{0,14},{1,15},{2,0},{3,1},{4,2},{5,3},{6,4},{7,5},{8,6},{9,7},{10,... | collective-permute-start | bytes 442376 | tf_op jit(solution)/shard_map/ppermute | solution.py:435
  11.0 11.8 %collective-permute-start.2 = (bf16[144,512]{1,0:T(8,128)(2,1)}, bf16[144,512]{1,0:T(8,128)(2,1)S(1)}, u32[]{:S(2)}, u32[]{:S(2)}) collective-permute-start(bf16[144,512]{1,0:T(8,128)(2,1)} %get-tuple-element.43), channel_id=1, source_target_pairs={{0,15},{1,14},{2,1},{3,0},{4,3},{5,2},{6,5},{7,4},{8,7},{9,6},{10,... | collective-permute-start | bytes 442376 | tf_op jit(solution)/shard_map/ppermute | solution.py:435
  11.3 11.5 %collective-permute-start.3 = (bf16[144,512]{1,0:T(8,128)(2,1)}, bf16[144,512]{1,0:T(8,128)(2,1)S(1)}, u32[]{:S(2)}, u32[]{:S(2)}) collective-permute-start(bf16[144,512]{1,0:T(8,128)(2,1)} %get-tuple-element.44), channel_id=1, source_target_pairs={{0,1},{1,0},{2,3},{3,2},{4,5},{5,4},{6,7},{7,6},{8,9},{9,8},{10,11... | collective-permute-start | bytes 442376 | tf_op jit(solution)/shard_map/ppermute | solution.py:435
  13.9 1.2 %copy-start = (bf16[64,16,512]{2,1,0:T(8,128)(2,1)S(1)}, bf16[64,16,512]{2,1,0:T(8,128)(2,1)}, u32[]{:S(2)}) copy-start(bf16[64,16,512]{2,1,0:T(8,128)(2,1)} %block_hbm.3) | copy-start | bytes 3145732
  13.9 1.2 %copy-start.4 = (s32[64,16]{0,1:T(8,128)S(1)}, s32[64,16]{0,1:T(8,128)}, u32[]{:S(2)}) copy-start(s32[64,16]{0,1:T(8,128)} %param.10) | copy-start | bytes 12292
  13.9 1.2 %copy-start.5 = (f32[2,2,512]{2,1,0:T(2,128)S(1)}, f32[2,2,512]{2,1,0:T(2,128)}, u32[]{:S(2)}) copy-start(f32[2,2,512]{2,1,0:T(2,128)} %gains.9) | copy-start | bytes 24580
  13.9 1.2 %copy-start.6 = (s32[64]{0:T(128)S(1)}, s32[64]{0:T(128)}, u32[]{:S(2)}) copy-start(s32[64]{0:T(128)} %bands_hbm.1) | copy-start | bytes 772
  15.1 1.6 %copy-start.2 = (bf16[2,1024,512]{2,1,0:T(8,128)(2,1)S(1)}, bf16[2,1024,512]{2,1,0:T(8,128)(2,1)}, u32[]{:S(2)}) copy-start(bf16[2,1024,512]{2,1,0:T(8,128)(2,1)} %contract_hbm.1) | copy-start | bytes 6291460
  22.1 11.2 %collective-permute-start.4 = (bf16[256,512]{1,0:T(8,128)(2,1)S(1)}, bf16[256,512]{1,0:T(8,128)(2,1)S(1)}, u32[]{:S(2)}, u32[]{:S(2)}) collective-permute-start(bf16[256,512]{1,0:T(8,128)(2,1)S(1)} %get-tuple-element.49), channel_id=1, source_target_pairs={{0,2},{1,3},{2,4},{3,5},{4,6},{5,7},{6,8},{7,9},{8,10},{9,11},{10,... | collective-permute-start | bytes 786440 | tf_op jit(solution)/shard_map/ppermute | solution.py:435
  22.8 10.6 %copy-start.1 = (bf16[2,512,1024]{2,1,0:T(8,128)(2,1)S(1)}, bf16[2,512,1024]{2,1,0:T(8,128)(2,1)}, u32[]{:S(2)}) copy-start(bf16[2,512,1024]{2,1,0:T(8,128)(2,1)} %expand_hbm.1) | copy-start | bytes 6291460
  27.7 9.7 %collective-permute-start.5 = (bf16[128,512]{1,0:T(8,128)(2,1)S(1)}, bf16[128,512]{1,0:T(8,128)(2,1)S(1)}, u32[]{:S(2)}, u32[]{:S(2)}) collective-permute-start(bf16[128,512]{1,0:T(8,128)(2,1)S(1)} %get-tuple-element.51), channel_id=1, source_target_pairs={{0,2},{1,3},{2,4},{3,5},{4,6},{5,7},{6,8},{7,9},{8,10},{9,11},{10,... | collective-permute-start | bytes 393224 | tf_op jit(solution)/shard_map/ppermute | solution.py:435
  30.1 8.6 %collective-permute-start.6 = (bf16[128,512]{1,0:T(8,128)(2,1)S(1)}, bf16[128,512]{1,0:T(8,128)(2,1)S(1)}, u32[]{:S(2)}, u32[]{:S(2)}) collective-permute-start(bf16[128,512]{1,0:T(8,128)(2,1)S(1)} %get-tuple-element.52), channel_id=1, source_target_pairs={{0,3},{1,2},{2,5},{3,4},{4,7},{5,6},{6,9},{7,8},{8,11},{9,10},{10,... | collective-permute-start | bytes 393224 | tf_op jit(solution)/shard_map/ppermute | solution.py:435
  30.2 8.6 %collective-permute-start.7 = (bf16[128,512]{1,0:T(8,128)(2,1)S(1)}, bf16[128,512]{1,0:T(8,128)(2,1)S(1)}, u32[]{:S(2)}, u32[]{:S(2)}) collective-permute-start(bf16[128,512]{1,0:T(8,128)(2,1)S(1)} %get-tuple-element.53), channel_id=1, source_target_pairs={{0,1},{1,0},{2,3},{3,2},{4,5},{5,4},{6,7},{7,6},{8,9},{9,8},{10,11... | collective-permute-start | bytes 393224 | tf_op jit(solution)/shard_map/ppermute | solution.py:435

commit v8 on v6

--- a/solution.py
+++ b/solution.py
@@ -82,24 +82,31 @@
     return tail[0:1, :cells], tail[1:2, :cells]
 
 
-def in_turn(count, stages):
+def in_turn(count, stages, between=()):
     state = [None] * count
-    for step in range(count + len(stages) - 1):
+    steps = count + len(stages) - 1
+    between = list(between)
+    for step in range(steps):
+        for _ in range(-(-len(between) // (steps - step))):
+            between.pop(0)()
         for index, stage in enumerate(stages):
             piece = step - index
             if 0 <= piece < count:
                 state[piece] = stage(piece, state[piece])
 
 
-def project(field, gain, attend_in, at, query, key, value):
-    rows = pl.ds(at, field.shape[0])
+def project(field, gain, attend_in, *places):
     normed = normalize(field, gain)
-    query[rows, :] = (product(normed, attend_in[:, :D]) * QSCALE).astype(BF16)
-    key[rows, :] = product(normed, attend_in[:, D : 2 * D]).astype(BF16)
-    value[rows, :] = product(normed, attend_in[:, 2 * D :]).astype(BF16)
-
-
-def set_bias(bias, bands, masks):
+    for kind in range(3):
+        result = product(normed, attend_in[:, kind * D : (kind + 1) * D])
+        result = (result * QSCALE if kind == 0 else result).astype(BF16)
+        done = 0
+        for refs, at, count in places:
+            refs[kind][pl.ds(at, count), :] = result[done : done + count]
+            done += count
+
+
+def allowed_pairs(bands, masks):
     cells = bands.shape[1]
     classes = lax.broadcasted_iota(jnp.int32, (CLASSES, cells), 0).astype(F32)
     one_hot = (classes == bands).astype(F32).astype(BF16)
@@ -107,10 +114,14 @@
     asking = lax.broadcasted_iota(jnp.int32, (cells, cells), 0)
     asked = lax.broadcasted_iota(jnp.int32, (cells, cells), 1)
     allowed = (same > 0.5) & ((masks > 0.5) | (asking == asked))
-    bias[...] = jnp.where(allowed, 0.0, -1e30)
-
-
-def attend(query, key, value, bias, context, low, count):
+    return jnp.where(allowed, 0.0, -1e30)
+
+
+def set_bias(bias, bands, masks):
+    bias[...] = allowed_pairs(bands, masks)
+
+
+def attend(query, key, value, bias, context, low, count, between=()):
     first = lax.broadcasted_iota(jnp.int32, (1, 2 * HD), 1) < HD
     rows = pl.ds(low, count)
     sums = {}
@@ -141,7 +152,7 @@
             below = pltpu.roll(jnp.where(first, odd, even), HD, 1)
             context[rows, lanes(unit)] = (above / below).astype(BF16)
 
-    in_turn(H, (score, weigh, gather))
+    in_turn(H, (score, weigh, gather), between)
 
 
 def finish(fields, context, lows, attend_out, gain, expand, contract, write):
@@ -161,6 +172,36 @@
         write(index, state[0] + product(state[1], contract[...]))
 
     in_turn(len(fields), (start, widen, bend, end))
+
+
+def finish_steps(fields, context, lows, attend_out, gain, expand, contract, write):
+    state = {}
+
+    def start(index):
+        rows = pl.ds(lows[index], fields[index].shape[0])
+        added = fields[index] + product(context[rows, :], attend_out[...])
+        resid = added.astype(BF16).astype(F32)
+        state[index] = resid, normalize(resid, gain)
+
+    def widen(index):
+        resid, normed = state[index]
+        state[index] = resid, product(normed, expand[...])
+
+    def bend(index):
+        resid, wide = state[index]
+        state[index] = resid, gelu(wide).astype(BF16)
+
+    def end(index):
+        resid, hidden = state.pop(index)
+        write(index, resid + product(hidden, contract[...]))
+
+    return [
+        functools.partial(stage, index)
+        for step in range(len(fields) + 3)
+        for at, stage in enumerate((start, widen, bend, end))
+        for index in [step - at]
+        if 0 <= index < len(fields)
+    ]
 
 
 def pack_main_kernel(block_hbm, valid_hbm, main, token, block, valid, sems):
@@ -183,6 +224,7 @@
 def early_kernel(
     block, bands, valid, token, gains, attend_in,
     side, corner, row_end, cells_here, query, key, value, notes,
+    first_query, first_key, first_value, first_bias,
 ):
     height = block.shape[0]
     part = SH * SW
@@ -206,27 +248,33 @@
     for index, pair in enumerate(window_notes):
         for offset, lanes in enumerate(pair):
             notes[pl.ds(2 * index + offset, 1), :] = lanes
-    project(local, gains[0, 0:1], attend_in, 0, query, key, value)
+    near = local.shape[0] - part
+    project(
+        local, gains[0, 0:1], attend_in,
+        ((first_query, first_key, first_value), 0, near), ((query, key, value), 0, part),
+    )
+    row_bands, masks = notes[0:1, :near], notes[1:2, :near]
+    set_bias(
+        first_bias,
+        jnp.concatenate([row_bands, row_bands], 1),
+        jnp.concatenate([masks, jnp.ones_like(masks)], 1),
+    )
 
 
 def window_a_kernel(
-    cells_here, notes, taken, near_query, near_key, near_value,
+    cells_here, taken, early_query, early_key, early_value, early_bias,
     gains, attend_in, attend_out, expand, contract,
     away, home, query, key, value, bias, context,
 ):
     cells = away.shape[0]
-    for near, whole in ((near_query, query), (near_key, key), (near_value, value)):
-        whole[pl.ds(0, cells), :] = near[pl.ds(0, cells), :]
     local = cells_here[pl.ds(0, cells), :].astype(F32)
     remote = taken[pl.ds(0, cells), :].astype(F32)
-    project(remote, gains[0, 0:1], attend_in, cells, query, key, value)
-    row_bands = notes[0:1, :cells]
+    project(remote, gains[0, 0:1], attend_in, ((query, key, value), cells, cells))
     masks, _ = meta_of(taken, cells)
-    set_bias(
-        bias,
-        jnp.concatenate([row_bands, row_bands], 1),
-        jnp.concatenate([notes[1:2, :cells], masks], 1),
-    )
+    columns = bias[:, cells:]
+    asking = lax.broadcasted_iota(jnp.int32, columns.shape, 0)
+    asked = lax.broadcasted_iota(jnp.int32, columns.shape, 1) + cells
+    bias[:, cells:] = jnp.where((masks > 0.5) | (asking == asked), columns, -1e30)
     attend(query, key, value, bias, context, 0, 2 * cells)
 
     def write(index, out):
@@ -241,9 +289,9 @@
     away_side, away_corner, home_end, query, key, value, bias, context,
 ):
     cells = away_side.shape[0]
-    skip = near_query.shape[0] - cells
+    skip = 2 * cells
     for near, whole in ((near_query, query), (near_key, key), (near_value, value)):
-        whole[pl.ds(0, cells), :] = near[pl.ds(skip, cells), :]
+        whole[pl.ds(0, cells), :] = near[...]
     fields = []
     bands_here = [notes[0:1, skip : skip + cells]]
     masks_here = [notes[1:2, skip : skip + cells]]
@@ -253,7 +301,10 @@
         masks_here.append(masks)
         bands_here.append(row_bands)
     bands_here[2] = bands_here[0]
-    project(jnp.concatenate(fields, 0), gains[0, 0:1], attend_in, cells, query, key, value)
+    project(
+        jnp.concatenate(fields, 0), gains[0, 0:1], attend_in,
+        ((query, key, value), cells, 3 * cells),
+    )
     set_bias(bias, jnp.concatenate(bands_here, 1), jnp.concatenate(masks_here, 1))
     attend(query, key, value, bias, context, cells, 3 * cells)
 
@@ -297,13 +348,14 @@
     for index in range(2):
         set_bias(next_bias.at[index], notes[2 * index + 2 : 2 * index + 3],
                  notes[2 * index + 3 : 2 * index + 4])
-    pieces = ((0, part, home[:part].astype(F32)),
-              (0, 3 * part, far[:part].astype(F32)),
-              (1, 0, jnp.concatenate([home[part:].astype(F32), kept[0], far[part:].astype(F32)], 0)))
     copies[0].wait()
-    for index, at, field in pieces:
-        project(field, next_gains[1, 0:1], next_attend_in, at,
-                next_query.at[index], next_key.at[index], next_value.at[index])
+    windows = [(next_query.at[at], next_key.at[at], next_value.at[at]) for at in range(2)]
+    field = [home[:part], far[:part], home[part:]]
+    field = [piece.astype(F32) for piece in field] + [kept[0], far[part:].astype(F32)]
+    project(
+        jnp.concatenate(field, 0), next_gains[1, 0:1], next_attend_in,
+        (windows[0], part, part), (windows[0], 3 * part, part), (windows[1], 0, 3 * part),
+    )
     for copy in copies[1:]:
         copy.wait()
 
@@ -322,14 +374,12 @@
         (home[high], home_side[...], far[high], far_side[...]),
     )
     windows = [[piece.astype(F32) for piece in parts] for parts in windows]
-    pieces = ((0, 0, windows[0][0]), (0, 2 * part, windows[0][2]), (1, 3 * part, windows[1][3]))
-    for index, at, field in pieces:
-        project(field, gains[1, 0:1], attend_in, at, query.at[index], key.at[index], value.at[index])
-    for index in range(len(windows)):
-        attend(
-            query.at[index], key.at[index], value.at[index], bias.at[index],
-            context.at[pl.ds(4 * part * index, 4 * part)], 0, 4 * part,
-        )
+    refs = [(query.at[at], key.at[at], value.at[at]) for at in range(2)]
+    project(
+        jnp.concatenate([windows[0][0], windows[0][2], windows[1][3]], 0),
+        gains[1, 0:1], attend_in,
+        (refs[0], 0, part), (refs[0], 2 * part, part), (refs[1], 3 * part, part),
+    )
     fields = [jnp.concatenate(parts[at : at + 2], 0) for parts in windows for at in (0, 2)]
     near = {}
 
@@ -344,8 +394,23 @@
         copies.append(pltpu.make_async_copy(out_ref.at[rows], out_hbm.at[rows], sems.at[window]))
         copies[-1].start()
 
-    lows = [2 * part * at for at in range(len(fields))]
-    finish(fields, context, lows, attend_out, gains[1, 1:2], expand, contract, write)
+    def look(index, between=()):
+        attend(
+            query.at[index], key.at[index], value.at[index], bias.at[index],
+            context.at[pl.ds(4 * part * index, 4 * part)], 0, 4 * part, between,
+        )
+
+    def rest(first):
+        lows = [2 * part * at for at in (first, first + 1)]
+        return finish_steps(
+            fields[first : first + 2], context, lows, attend_out, gains[1, 1:2], expand, contract,
+            lambda index, out: write(first + index, out),
+        )
+
+    look(0)
+    look(1, rest(0))
+    for step in rest(2):
+        step()
     for copy in copies:
         copy.wait()
 
@@ -404,21 +469,23 @@
         (norm_gains, attend_in[0], attend_out[0], expand[0], contract[0]),
         (norm_gains, attend_in, attend_out, expand, contract),
     ]
-    side, corner, row_end, here, *near, notes = call(
+    side, corner, row_end, here, *prepared = call(
         early_kernel, "early",
-        [(quarter + META, D)] * 3 + [(half + quarter, D)] * 4
-        + [jax.ShapeDtypeStruct((META, D), F32)],
+        [(quarter + META, D)] * 3 + [(half + quarter, D)] + [(quarter, D)] * 3
+        + [jax.ShapeDtypeStruct((META, D), F32)] + [(cells, D)] * 3 + [bias_shape],
         [VMEM, SMEM] + [VMEM] * 4, [], each * (half + quarter),
         atmosphere, pole_band, valid, token, *weights[0][:2],
     )
+    near, notes, first = prepared[:3], prepared[3], prepared[4:]
     far_side = moved(side, -1, 0)
     far_corner = moved(corner, -1, -1)
     near_end = moved(row_end, 0, -1)
 
-    away, home = call(
-        window_a_kernel, "window_a", [(half, D)] * 2, [VMEM] * 11,
-        [wide] * 3 + [bias_scratch, wide], flops + each * half,
-        here, notes, far_main, *near, *weights[0],
+    away, home, *_ = call(
+        window_a_kernel, "window_a", [(half, D)] * 2 + [(cells, D)] * 3 + [bias_shape],
+        [VMEM] * 11, [wide], flops + each * half,
+        here, far_main, *first, *weights[0],
+        aliases=((2, 2), (3, 3), (4, 4), (5, 5)),
     )
     back_main = moved(away, 1, 0)
     away_side, away_corner, home_end, *inside = call(

time: 47.4 us -> 48 us (1.013)
  Pallas kernels: 28.6 us -> 29.5 us
    pallas_call x6, Pallas kernels: 28.6 us -> 29.5 us  [call(): pl.pallas_call(kernel, out_shape=shapes, in_specs=specs, out_specs=[outs]...]
  transfers between devices with their start and end apart: 8 -> 8, of which waited for: 4 -> 4; matrix products, arithmetic and copies ran while one was open for 4% -> 4% of each run, Pallas kernels for 34% -> 35%
where the time goes in v8:
time: 48 us; the launch traced here: 47.3 us
  Pallas kernels  29.5 us (61%)
  starting transfers between devices  11.7 us (24%)
  waiting for transfers between devices  4.01 us (8%)
  local copies, waits for them, and re-layouts  1.72 us (4%)
    pallas_call x6, Pallas kernels, call(): pl.pallas_call(kernel, out_shape=shapes, in_specs=specs, out_specs=[outs]...  29.5 us
    ppermute x8, starting transfers between devices, moved(): return lax.ppermute(value, ('lon', 'lat'), pairs)  11.7 us
    ppermute x8, waiting for transfers between devices, moved(): return lax.ppermute(value, ('lon', 'lat'), pairs)  4.01 us
    squeeze x1, local copies, waits for them, and re-layouts, on_device(): attend_in[0]  1.51 us
  transfers between devices with their start and end apart: 8, of which 4 were waited for; matrix products, arithmetic and copies ran while one was open for 4% of the time, Pallas kernels for 35%

profile of v8, /device:TPU:0, one launch (start us, length us, event | category | flops | bytes accessed | tf_op | source)
XLA Modules:
  0.0 47.3 jit_solution(4888839513615160138)
XLA Ops:
  0.0 1.9 %pack_main.1 = (bf16[272,512]{1,0:T(8,128)(2,1)}, bf16[16,128]{1,0:T(8,128)(2,1)}) custom-call(bf16[64,16,512]{2,1,0:T(8,128)(2,1)} %block.1, s32[16,64]{1,0:T(8,128)} %bitcast.9), custom_call_target="tpu_custom_call" | custom-call | flops 1000000 | bytes 1052672 | tf_op jit(solution)/shard_map/pack_main/pallas_call | solution.py:422
  1.9 6.1 %collective-permute-start = (bf16[272,512]{1,0:T(8,128)(2,1)}, bf16[272,512]{1,0:T(8,128)(2,1)S(1)}, u32[]{:S(2)}, u32[]{:S(2)}) collective-permute-start(bf16[272,512]{1,0:T(8,128)(2,1)} %get-tuple-element.40), channel_id=1, source_target_pairs={{0,14},{1,15},{2,0},{3,1},{4,2},{5,3},{6,4},{7,5},{8,6},{9,7},{10,... | collective-permute-start | bytes 835592 | tf_op jit(solution)/shard_map/ppermute | solution.py:448
  8.0 1.5 %slice_bitcast_fusion.attend_in = bf16[512,1536]{1,0:T(8,128)(2,1)S(1)} fusion(bf16[2,512,1536]{2,1,0:T(8,128)(2,1)} %attend_in_hbm.1), kind=kLoop, calls=%fused_computation | loop fusion | bytes 3145728 | tf_op jit(solution)/shard_map/squeeze | solution.py:469
  9.5 0.0 copy-start
  9.6 0.0 copy-start.3
  9.6 1.7 %early.1 = (bf16[144,512]{1,0:T(8,128)(2,1)S(1)}, bf16[144,512]{1,0:T(8,128)(2,1)S(1)}, bf16[144,512]{1,0:T(8,128)(2,1)S(1)}, bf16[384,512]{1,0:T(8,128)(2,1)S(1...) custom-call(bf16[64,16,512]{2,1,0:T(8,128)(2,1)S(1)} %copy-done.2, ...), custom_call_target="tpu_custom_call" | custom-call | flops 603979776 | bytes 2638080 | tf_op jit(solution)/shard_map/early/pallas_call | solution.py:422
  11.3 0.0 copy-start.1
  11.3 0.6 %collective-permute-start.1 = (bf16[144,512]{1,0:T(8,128)(2,1)S(1)}, bf16[144,512]{1,0:T(8,128)(2,1)S(1)}, u32[]{:S(2)}, u32[]{:S(2)}) collective-permute-start(bf16[144,512]{1,0:T(8,128)(2,1)S(1)} %get-tuple-element.47), channel_id=1, source_target_pairs={{0,14},{1,15},{2,0},{3,1},{4,2},{5,3},{6,4},{7,5},{8,6},{9,7},{10,... | collective-permute-start | bytes 442376 | tf_op jit(solution)/shard_map/ppermute | solution.py:448
  11.8 0.3 collective-permute-start.2
  12.1 1.2 %collective-permute-start.3 = (bf16[144,512]{1,0:T(8,128)(2,1)S(1)}, bf16[144,512]{1,0:T(8,128)(2,1)S(1)}, u32[]{:S(2)}, u32[]{:S(2)}) collective-permute-start(bf16[144,512]{1,0:T(8,128)(2,1)S(1)} %get-tuple-element.49), channel_id=1, source_target_pairs={{0,1},{1,0},{2,3},{3,2},{4,5},{5,4},{6,7},{7,6},{8,9},{9,8},{10,11... | collective-permute-start | bytes 442376 | tf_op jit(solution)/shard_map/ppermute | solution.py:448
  13.4 0.1 slice_bitcast_fusion.2.expand
  13.5 0.1 slice_bitcast_fusion.1.contract
  13.6 1.8 %collective-permute-done.taken = bf16[272,512]{1,0:T(8,128)(2,1)S(1)} collective-permute-done((bf16[272,512]{1,0:T(8,128)(2,1)}, bf16[272,512]{1,0:T(8,128)(2,1)S(1)}, u32[]{:S(2)}, u32[]{:S(2)}) %collective-permute-start) | collective-permute-done | bytes 278560 | tf_op jit(solution)/shard_map/ppermute | solution.py:448
  15.4 5.5 %window_a.1 = (bf16[256,512]{1,0:T(8,128)(2,1)S(1)}, bf16[256,512]{1,0:T(8,128)(2,1)S(1)}, bf16[512,512]{1,0:T(8,128)(2,1)S(1)}, bf16[512,512]{1,0:T(8,128)(2,1)...) custom-call(bf16[384,512]{1,0:T(8,128)(2,1)S(1)} %get-tuple-element., ...), custom_call_target="tpu_custom_call", output_to_operand_aliasing={{2}: (2, {}), {3}: (3, {}), {4}: (4, {}), {5}: (5, {})} | custom-call | flops 2281701376 | bytes 7495680 | tf_op jit(solution)/shard_map/window_a/pallas_call | solution.py:422
  20.9 0.3 collective-permute-start.4
  21.2 0.0 collective-permute-done.3.taken_end
  21.2 5.0 %window_b_away.1 = (bf16[128,512]{1,0:T(8,128)(2,1)S(1)}, bf16[128,512]{1,0:T(8,128)(2,1)S(1)}, bf16[128,512]{1,0:T(8,128)(2,1)S(1)}, bf16[512,512]{1,0:T(8,128)...) custom-call(bf16[256,512]{1,0:T(8,128)(2,1)S(1)} %get-tuple-element.45.window_a_first., ...), custom_call_target="tpu_custom_call" | custom-call | flops 2013265920 | bytes 5332992 | tf_op jit(solution)/shard_map/window_b_away/pallas_call | solution.py:422
  26.3 1.1 %collective-permute-start.5 = (bf16[128,512]{1,0:T(8,128)(2,1)S(1)}, bf16[128,512]{1,0:T(8,128)(2,1)S(1)}, u32[]{:S(2)}, u32[]{:S(2)}) collective-permute-start(bf16[128,512]{1,0:T(8,128)(2,1)S(1)} %get-tuple-element.59), channel_id=1, source_target_pairs={{0,2},{1,3},{2,4},{3,5},{4,6},{5,7},{6,8},{7,9},{8,10},{9,11},{10,... | collective-permute-start | bytes 393224 | tf_op jit(solution)/shard_map/ppermute | solution.py:448
  27.3 2.1 %collective-permute-start.7 = (bf16[128,512]{1,0:T(8,128)(2,1)S(1)}, bf16[128,512]{1,0:T(8,128)(2,1)S(1)}, u32[]{:S(2)}, u32[]{:S(2)}) collective-permute-start(bf16[128,512]{1,0:T(8,128)(2,1)S(1)} %get-tuple-element.61), channel_id=1, source_target_pairs={{0,1},{1,0},{2,3},{3,2},{4,5},{5,4},{6,7},{7,6},{8,9},{9,8},{10,11... | collective-permute-start | bytes 393224 | tf_op jit(solution)/shard_map/ppermute | solution.py:448
  29.5 0.9 %collective-permute-done.4.far = bf16[256,512]{1,0:T(8,128)(2,1)S(1)} collective-permute-done((bf16[256,512]{1,0:T(8,128)(2,1)S(1)}, bf16[256,512]{1,0:T(8,128)(2,1)S(1)}, u32[]{:S(2)}, u32[]{:S(2)}) %collective-permute-start.4) | collective-permute-done | bytes 262176 | tf_op jit(solution)/shard_map/ppermute | solution.py:448
  30.4 4.1 %between.1 = (bf16[128,512]{1,0:T(8,128)(2,1)S(1)}, bf16[2,512,512]{2,1,0:T(8,128)(2,1)S(1)}, bf16[2,512,512]{2,1,0:T(8,128)(2,1)S(1)}, bf16[2,512,512]{2,1,0:T(...) custom-call(bf16[384,512]{1,0:T(8,128)(2,1)S(1)} %get-tuple-element., ...), custom_call_target="tpu_custom_call" | custom-call | flops 1476395008 | bytes 14598144 | tf_op jit(solution)/shard_map/between/pallas_call | solution.py:422
  34.5 0.8 %collective-permute-done.5.far_side = bf16[128,512]{1,0:T(8,128)(2,1)S(1)} collective-permute-done((bf16[128,512]{1,0:T(8,128)(2,1)S(1)}, bf16[128,512]{1,0:T(8,128)(2,1)S(1)}, u32[]{:S(2)}, u32[]{:S(2)}) %collective-permute-start.5) | collective-permute-done | bytes 131104 | tf_op jit(solution)/shard_map/ppermute | solution.py:448
  35.4 0.5 %collective-permute-done.6.far_corner = bf16[128,512]{1,0:T(8,128)(2,1)S(1)} collective-permute-done((bf16[128,512]{1,0:T(8,128)(2,1)S(1)}, bf16[128,512]{1,0:T(8,128)(2,1)S(1)}, u32[]{:S(2)}, u32[]{:S(2)}) %collective-permute-start.6) | collective-permute-done | bytes 131104 | tf_op jit(solution)/shard_map/ppermute | solution.py:448
  35.8 11.3 %second.1 = (bf16[64,16,512]{2,1,0:T(8,128)(2,1)}, bf16[2,512,512]{2,1,0:T(8,128)(2,1)S(1)}, bf16[2,512,512]{2,1,0:T(8,128)(2,1)S(1)}, bf16[2,512,512]{2,1,0:T(8,128)(2,1)S(1)}) custom-call(bf16[256,512]{1,0:T(8,128)(2,1)S(1)} %get-tuple-element.45.window_a_first.home, ...), custom_call_target="tpu_custom_call", output_to_operand_aliasing={{1}: (6, {}), {2}: (7, {}), {3}: (8, {})} | custom-call | flops 4764729344 | bytes 10493952 | tf_op jit(solution)/shard_map/second/pallas_call | solution.py:422
  (18 shorter events, 0.1 us)
Async XLA Ops:
  0.0 9.5 %copy-start.2 = (bf16[64,16,512]{2,1,0:T(8,128)(2,1)S(1)}, bf16[64,16,512]{2,1,0:T(8,128)(2,1)}, u32[]{:S(2)}) copy-start(bf16[64,16,512]{2,1,0:T(8,128)(2,1)} %block.1) | copy-start | bytes 3145732
  0.0 9.5 %copy-start.4 = (f32[2,2,512]{2,1,0:T(2,128)S(1)}, f32[2,2,512]{2,1,0:T(2,128)}, u32[]{:S(2)}) copy-start(f32[2,2,512]{2,1,0:T(2,128)} %gains.9) | copy-start | bytes 24580
  0.0 9.5 %copy-start.5 = (s32[64,16]{0,1:T(8,128)S(1)}, s32[64,16]{0,1:T(8,128)}, u32[]{:S(2)}) copy-start(s32[64,16]{0,1:T(8,128)} %param.10) | copy-start | bytes 12292
  0.0 9.5 %copy-start.7 = (s32[64]{0:T(128)S(1)}, s32[64]{0:T(128)}, u32[]{:S(2)}) copy-start(s32[64]{0:T(128)} %bands.1) | copy-start | bytes 772
  1.9 7.6 %copy-start.6 = (bf16[16,128]{1,0:T(8,128)(2,1)S(1)}, bf16[16,128]{1,0:T(8,128)(2,1)}, u32[]{:S(2)}) copy-start(bf16[16,128]{1,0:T(8,128)(2,1)} %get-tuple-element.38.token) | copy-start | bytes 12292
  1.9 13.4 %collective-permute-start = (bf16[272,512]{1,0:T(8,128)(2,1)}, bf16[272,512]{1,0:T(8,128)(2,1)S(1)}, u32[]{:S(2)}, u32[]{:S(2)}) collective-permute-start(bf16[272,512]{1,0:T(8,128)(2,1)} %get-tuple-element.40), channel_id=1, source_target_pairs={{0,14},{1,15},{2,0},{3,1},{4,2},{5,3},{6,4},{7,5},{8,6},{9,7},{10,... | collective-permute-start | bytes 835592 | tf_op jit(solution)/shard_map/ppermute | solution.py:448
  9.5 3.9 %copy-start = (bf16[2,512,1024]{2,1,0:T(8,128)(2,1)S(1)}, bf16[2,512,1024]{2,1,0:T(8,128)(2,1)}, u32[]{:S(2)}) copy-start(bf16[2,512,1024]{2,1,0:T(8,128)(2,1)} %expand_hbm.1) | copy-start | bytes 6291460
  9.6 3.9 %copy-start.3 = (bf16[2,512,512]{2,1,0:T(8,128)(2,1)S(1)}, bf16[2,512,512]{2,1,0:T(8,128)(2,1)}, u32[]{:S(2)}) copy-start(bf16[2,512,512]{2,1,0:T(8,128)(2,1)} %attend_out_hbm.1) | copy-start | bytes 3145732
  11.3 2.2 %copy-start.1 = (bf16[2,1024,512]{2,1,0:T(8,128)(2,1)S(1)}, bf16[2,1024,512]{2,1,0:T(8,128)(2,1)}, u32[]{:S(2)}) copy-start(bf16[2,1024,512]{2,1,0:T(8,128)(2,1)} %contract_hbm.1) | copy-start | bytes 6291460
  11.3 9.9 %collective-permute-start.1 = (bf16[144,512]{1,0:T(8,128)(2,1)S(1)}, bf16[144,512]{1,0:T(8,128)(2,1)S(1)}, u32[]{:S(2)}, u32[]{:S(2)}) collective-permute-start(bf16[144,512]{1,0:T(8,128)(2,1)S(1)} %get-tuple-element.47), channel_id=1, source_target_pairs={{0,14},{1,15},{2,0},{3,1},{4,2},{5,3},{6,4},{7,5},{8,6},{9,7},{10,... | collective-permute-start | bytes 442376 | tf_op jit(solution)/shard_map/ppermute | solution.py:448
  11.8 9.4 %collective-permute-start.2 = (bf16[144,512]{1,0:T(8,128)(2,1)S(1)}, bf16[144,512]{1,0:T(8,128)(2,1)S(1)}, u32[]{:S(2)}, u32[]{:S(2)}) collective-permute-start(bf16[144,512]{1,0:T(8,128)(2,1)S(1)} %get-tuple-element.48), channel_id=1, source_target_pairs={{0,15},{1,14},{2,1},{3,0},{4,3},{5,2},{6,5},{7,4},{8,7},{9,6},{10,... | collective-permute-start | bytes 442376 | tf_op jit(solution)/shard_map/ppermute | solution.py:448
  12.1 9.1 %collective-permute-start.3 = (bf16[144,512]{1,0:T(8,128)(2,1)S(1)}, bf16[144,512]{1,0:T(8,128)(2,1)S(1)}, u32[]{:S(2)}, u32[]{:S(2)}) collective-permute-start(bf16[144,512]{1,0:T(8,128)(2,1)S(1)} %get-tuple-element.49), channel_id=1, source_target_pairs={{0,1},{1,0},{2,3},{3,2},{4,5},{5,4},{6,7},{7,6},{8,9},{9,8},{10,11... | collective-permute-start | bytes 442376 | tf_op jit(solution)/shard_map/ppermute | solution.py:448
  20.9 9.5 %collective-permute-start.4 = (bf16[256,512]{1,0:T(8,128)(2,1)S(1)}, bf16[256,512]{1,0:T(8,128)(2,1)S(1)}, u32[]{:S(2)}, u32[]{:S(2)}) collective-permute-start(bf16[256,512]{1,0:T(8,128)(2,1)S(1)} %get-tuple-element.57), channel_id=1, source_target_pairs={{0,2},{1,3},{2,4},{3,5},{4,6},{5,7},{6,8},{7,9},{8,10},{9,11},{10,... | collective-permute-start | bytes 786440 | tf_op jit(solution)/shard_map/ppermute | solution.py:448
  26.3 9.1 %collective-permute-start.5 = (bf16[128,512]{1,0:T(8,128)(2,1)S(1)}, bf16[128,512]{1,0:T(8,128)(2,1)S(1)}, u32[]{:S(2)}, u32[]{:S(2)}) collective-permute-start(bf16[128,512]{1,0:T(8,128)(2,1)S(1)} %get-tuple-element.59), channel_id=1, source_target_pairs={{0,2},{1,3},{2,4},{3,5},{4,6},{5,7},{6,8},{7,9},{8,10},{9,11},{10,... | collective-permute-start | bytes 393224 | tf_op jit(solution)/shard_map/ppermute | solution.py:448
  27.3 8.5 %collective-permute-start.6 = (bf16[128,512]{1,0:T(8,128)(2,1)S(1)}, bf16[128,512]{1,0:T(8,128)(2,1)S(1)}, u32[]{:S(2)}, u32[]{:S(2)}) collective-permute-start(bf16[128,512]{1,0:T(8,128)(2,1)S(1)} %get-tuple-element.60), channel_id=1, source_target_pairs={{0,3},{1,2},{2,5},{3,4},{4,7},{5,6},{6,9},{7,8},{8,11},{9,10},{10,... | collective-permute-start | bytes 393224 | tf_op jit(solution)/shard_map/ppermute | solution.py:448
  27.3 8.5 %collective-permute-start.7 = (bf16[128,512]{1,0:T(8,128)(2,1)S(1)}, bf16[128,512]{1,0:T(8,128)(2,1)S(1)}, u32[]{:S(2)}, u32[]{:S(2)}) collective-permute-start(bf16[128,512]{1,0:T(8,128)(2,1)S(1)} %get-tuple-element.61), channel_id=1, source_target_pairs={{0,1},{1,0},{2,3},{3,2},{4,5},{5,4},{6,7},{7,6},{8,9},{9,8},{10,11... | collective-permute-start | bytes 393224 | tf_op jit(solution)/shard_map/ppermute | solution.py:448

commit v9 on v6

--- a/solution.py
+++ b/solution.py
@@ -91,12 +91,15 @@
                 state[piece] = stage(piece, state[piece])
 
 
-def project(field, gain, attend_in, at, query, key, value):
-    rows = pl.ds(at, field.shape[0])
+def project(field, gain, attend_in, *places):
     normed = normalize(field, gain)
-    query[rows, :] = (product(normed, attend_in[:, :D]) * QSCALE).astype(BF16)
-    key[rows, :] = product(normed, attend_in[:, D : 2 * D]).astype(BF16)
-    value[rows, :] = product(normed, attend_in[:, 2 * D :]).astype(BF16)
+    for kind in range(3):
+        result = product(normed, attend_in[:, kind * D : (kind + 1) * D])
+        result = (result * QSCALE if kind == 0 else result).astype(BF16)
+        done = 0
+        for refs, at, count in places:
+            refs[kind][pl.ds(at, count), :] = result[done : done + count]
+            done += count
 
 
 def set_bias(bias, bands, masks):
@@ -111,17 +114,22 @@
 
 
 def attend(query, key, value, bias, context, low, count):
+    attend_windows([(query, key, value, bias, context)], low, count)
+
+
+def attend_windows(windows, low, count):
     first = lax.broadcasted_iota(jnp.int32, (1, 2 * HD), 1) < HD
     rows = pl.ds(low, count)
     sums = {}
 
     def lanes(unit):
-        return slice(2 * HD * (unit // 2), 2 * HD * (unit // 2 + 1))
+        return slice(2 * HD * (unit % H // 2), 2 * HD * (unit % H // 2 + 1))
 
     def own(unit, inside, outside):
         return jnp.where(first, inside, outside) if unit % 2 == 0 else jnp.where(first, outside, inside)
 
     def score(unit, _):
+        query, key, _, bias, _ = windows[unit // H]
         queries = query[rows, lanes(unit)]
         queries = own(unit, queries, jnp.zeros_like(queries))
         scores = lax.dot_general(
@@ -133,6 +141,7 @@
         return jnp.exp2(scores - jnp.max(scores, -1, keepdims=True)).astype(BF16)
 
     def gather(unit, weights):
+        _, _, value, _, context = windows[unit // H]
         values = value[:, lanes(unit)]
         sums[unit] = product(weights, own(unit, values, jnp.ones_like(values)))
         if unit % 2 == 1:
@@ -141,7 +150,7 @@
             below = pltpu.roll(jnp.where(first, odd, even), HD, 1)
             context[rows, lanes(unit)] = (above / below).astype(BF16)
 
-    in_turn(H, (score, weigh, gather))
+    in_turn(len(windows) * H, (score, weigh, gather))
 
 
 def finish(fields, context, lows, attend_out, gain, expand, contract, write):
@@ -206,7 +215,7 @@
     for index, pair in enumerate(window_notes):
         for offset, lanes in enumerate(pair):
             notes[pl.ds(2 * index + offset, 1), :] = lanes
-    project(local, gains[0, 0:1], attend_in, 0, query, key, value)
+    project(local, gains[0, 0:1], attend_in, ((query, key, value), 0, local.shape[0]))
 
 
 def window_a_kernel(
@@ -219,7 +228,7 @@
         whole[pl.ds(0, cells), :] = near[pl.ds(0, cells), :]
     local = cells_here[pl.ds(0, cells), :].astype(F32)
     remote = taken[pl.ds(0, cells), :].astype(F32)
-    project(remote, gains[0, 0:1], attend_in, cells, query, key, value)
+    project(remote, gains[0, 0:1], attend_in, ((query, key, value), cells, cells))
     row_bands = notes[0:1, :cells]
     masks, _ = meta_of(taken, cells)
     set_bias(
@@ -253,7 +262,10 @@
         masks_here.append(masks)
         bands_here.append(row_bands)
     bands_here[2] = bands_here[0]
-    project(jnp.concatenate(fields, 0), gains[0, 0:1], attend_in, cells, query, key, value)
+    project(
+        jnp.concatenate(fields, 0), gains[0, 0:1], attend_in,
+        ((query, key, value), cells, 3 * cells),
+    )
     set_bias(bias, jnp.concatenate(bands_here, 1), jnp.concatenate(masks_here, 1))
     attend(query, key, value, bias, context, cells, 3 * cells)
 
@@ -297,13 +309,14 @@
     for index in range(2):
         set_bias(next_bias.at[index], notes[2 * index + 2 : 2 * index + 3],
                  notes[2 * index + 3 : 2 * index + 4])
-    pieces = ((0, part, home[:part].astype(F32)),
-              (0, 3 * part, far[:part].astype(F32)),
-              (1, 0, jnp.concatenate([home[part:].astype(F32), kept[0], far[part:].astype(F32)], 0)))
     copies[0].wait()
-    for index, at, field in pieces:
-        project(field, next_gains[1, 0:1], next_attend_in, at,
-                next_query.at[index], next_key.at[index], next_value.at[index])
+    windows = [(next_query.at[at], next_key.at[at], next_value.at[at]) for at in range(2)]
+    field = [home[:part], far[:part], home[part:]]
+    field = [piece.astype(F32) for piece in field] + [kept[0], far[part:].astype(F32)]
+    project(
+        jnp.concatenate(field, 0), next_gains[1, 0:1], next_attend_in,
+        (windows[0], part, part), (windows[0], 3 * part, part), (windows[1], 0, 3 * part),
+    )
     for copy in copies[1:]:
         copy.wait()
 
@@ -322,14 +335,19 @@
         (home[high], home_side[...], far[high], far_side[...]),
     )
     windows = [[piece.astype(F32) for piece in parts] for parts in windows]
-    pieces = ((0, 0, windows[0][0]), (0, 2 * part, windows[0][2]), (1, 3 * part, windows[1][3]))
-    for index, at, field in pieces:
-        project(field, gains[1, 0:1], attend_in, at, query.at[index], key.at[index], value.at[index])
-    for index in range(len(windows)):
-        attend(
-            query.at[index], key.at[index], value.at[index], bias.at[index],
-            context.at[pl.ds(4 * part * index, 4 * part)], 0, 4 * part,
-        )
+    refs = [(query.at[at], key.at[at], value.at[at]) for at in range(2)]
+    project(
+        jnp.concatenate([windows[0][0], windows[0][2], windows[1][3]], 0),
+        gains[1, 0:1], attend_in,
+        (refs[0], 0, part), (refs[0], 2 * part, part), (refs[1], 3 * part, part),
+    )
+    attend_windows(
+        [
+            (*refs[at], bias.at[at], context.at[pl.ds(4 * part * at, 4 * part)])
+            for at in range(len(windows))
+        ],
+        0, 4 * part,
+    )
     fields = [jnp.concatenate(parts[at : at + 2], 0) for parts in windows for at in (0, 2)]
     near = {}
 

time: 47.4 us -> 47.4 us (level)
  no operation moved by 1% of the time
where the time goes in v9:
time: 47.4 us; the launch traced here: 46.7 us
  Pallas kernels  28.5 us (60%)
  starting transfers between devices  11.7 us (25%)
  waiting for transfers between devices  4.54 us (10%)
  local copies, waits for them, and re-layouts  1.72 us (4%)
    pallas_call x6, Pallas kernels, call(): pl.pallas_call(kernel, out_shape=shapes, in_specs=specs, out_specs=[outs]...  28.5 us
    ppermute x8, starting transfers between devices, moved(): return lax.ppermute(value, ('lon', 'lat'), pairs)  11.7 us
    ppermute x8, waiting for transfers between devices, moved(): return lax.ppermute(value, ('lon', 'lat'), pairs)  4.54 us
    squeeze x1, local copies, waits for them, and re-layouts, on_device(): attend_in[0]  1.51 us
  transfers between devices with their start and end apart: 8, of which 4 were waited for; matrix products, arithmetic and copies ran while one was open for 4% of the time, Pallas kernels for 34%

profile of v9, /device:TPU:0, one launch (start us, length us, event | category | flops | bytes accessed | tf_op | source)
XLA Modules:
  0.0 46.7 jit_solution(2762080171398206101)
XLA Ops:
  0.0 1.9 %pack_main.1 = (bf16[272,512]{1,0:T(8,128)(2,1)}, bf16[16,128]{1,0:T(8,128)(2,1)}) custom-call(bf16[64,16,512]{2,1,0:T(8,128)(2,1)} %block.1, s32[16,64]{1,0:T(8,128)} %bitcast.9), custom_call_target="tpu_custom_call" | custom-call | flops 1000000 | bytes 1052672 | tf_op jit(solution)/shard_map/pack_main/pallas_call | solution.py:375
  1.9 6.1 %collective-permute-start = (bf16[272,512]{1,0:T(8,128)(2,1)}, bf16[272,512]{1,0:T(8,128)(2,1)S(1)}, u32[]{:S(2)}, u32[]{:S(2)}) collective-permute-start(bf16[272,512]{1,0:T(8,128)(2,1)} %get-tuple-element.37), channel_id=1, source_target_pairs={{0,14},{1,15},{2,0},{3,1},{4,2},{5,3},{6,4},{7,5},{8,6},{9,7},{10,... | collective-permute-start | bytes 835592 | tf_op jit(solution)/shard_map/ppermute | solution.py:401
  8.0 1.5 %slice_bitcast_fusion.attend_in = bf16[512,1536]{1,0:T(8,128)(2,1)S(1)} fusion(bf16[2,512,1536]{2,1,0:T(8,128)(2,1)} %attend_in_hbm.1), kind=kLoop, calls=%fused_computation | loop fusion | bytes 3145728 | tf_op jit(solution)/shard_map/squeeze | solution.py:422
  9.5 0.0 copy-start
  9.6 0.0 copy-start.3
  9.6 1.6 %early.1 = (bf16[144,512]{1,0:T(8,128)(2,1)S(1)}, bf16[144,512]{1,0:T(8,128)(2,1)S(1)}, bf16[144,512]{1,0:T(8,128)(2,1)S(1)}, bf16[384,512]{1,0:T(8,128)(2,1)S(1...) custom-call(bf16[64,16,512]{2,1,0:T(8,128)(2,1)S(1)} %copy-done.2, ...), custom_call_target="tpu_custom_call" | custom-call | flops 603979776 | bytes 2638080 | tf_op jit(solution)/shard_map/early/pallas_call | solution.py:375
  11.2 0.0 copy-start.1
  11.2 0.6 %collective-permute-start.1 = (bf16[144,512]{1,0:T(8,128)(2,1)S(1)}, bf16[144,512]{1,0:T(8,128)(2,1)S(1)}, u32[]{:S(2)}, u32[]{:S(2)}) collective-permute-start(bf16[144,512]{1,0:T(8,128)(2,1)S(1)} %get-tuple-element.42), channel_id=1, source_target_pairs={{0,14},{1,15},{2,0},{3,1},{4,2},{5,3},{6,4},{7,5},{8,6},{9,7},{10,... | collective-permute-start | bytes 442376 | tf_op jit(solution)/shard_map/ppermute | solution.py:401
  11.8 0.3 collective-permute-start.2
  12.0 1.2 %collective-permute-start.3 = (bf16[144,512]{1,0:T(8,128)(2,1)S(1)}, bf16[144,512]{1,0:T(8,128)(2,1)S(1)}, u32[]{:S(2)}, u32[]{:S(2)}) collective-permute-start(bf16[144,512]{1,0:T(8,128)(2,1)S(1)} %get-tuple-element.44), channel_id=1, source_target_pairs={{0,1},{1,0},{2,3},{3,2},{4,5},{5,4},{6,7},{7,6},{8,9},{9,8},{10,11... | collective-permute-start | bytes 442376 | tf_op jit(solution)/shard_map/ppermute | solution.py:401
  13.3 0.1 slice_bitcast_fusion.2.expand
  13.4 0.1 slice_bitcast_fusion.1.contract
  13.5 1.9 %collective-permute-done.taken = bf16[272,512]{1,0:T(8,128)(2,1)S(1)} collective-permute-done((bf16[272,512]{1,0:T(8,128)(2,1)}, bf16[272,512]{1,0:T(8,128)(2,1)S(1)}, u32[]{:S(2)}, u32[]{:S(2)}) %collective-permute-start) | collective-permute-done | bytes 278560 | tf_op jit(solution)/shard_map/ppermute | solution.py:401
  15.4 5.3 %window_a.1 = (bf16[256,512]{1,0:T(8,128)(2,1)S(1)}, bf16[256,512]{1,0:T(8,128)(2,1)S(1)}) custom-call(bf16[384,512]{1,0:T(8,128)(2,1)S(1)} %get-tuple-element.35.cells_here, f32[16,512]{1,0:T(8,128)S(1)} %get-tuple-element.36.notes, bf16[272,512]{1,0:T(8,128)(2,1)S(1)} %collective-permute-done.taken, bf16[384,512]{1,0:T(8,128)(2,1)S(1)} %get-tuple-element.38.near_query, ...), custom_call_target="tpu_custom_call" | custom-call | flops 2281701376 | bytes 6086656 | tf_op jit(solution)/shard_map/window_a/pallas_call | solution.py:375
  20.7 0.3 collective-permute-start.4
  21.0 5.0 %window_b_away.1 = (bf16[128,512]{1,0:T(8,128)(2,1)S(1)}, bf16[128,512]{1,0:T(8,128)(2,1)S(1)}, bf16[128,512]{1,0:T(8,128)(2,1)S(1)}, bf16[512,512]{1,0:T(8,128)...) custom-call(bf16[256,512]{1,0:T(8,128)(2,1)S(1)} %get-tuple-element.41.window_a_first., ...), custom_call_target="tpu_custom_call" | custom-call | flops 2013265920 | bytes 6119424 | tf_op jit(solution)/shard_map/window_b_away/pallas_call | solution.py:375
  26.1 1.0 %collective-permute-start.5 = (bf16[128,512]{1,0:T(8,128)(2,1)S(1)}, bf16[128,512]{1,0:T(8,128)(2,1)S(1)}, u32[]{:S(2)}, u32[]{:S(2)}) collective-permute-start(bf16[128,512]{1,0:T(8,128)(2,1)S(1)} %get-tuple-element.51), channel_id=1, source_target_pairs={{0,2},{1,3},{2,4},{3,5},{4,6},{5,7},{6,8},{7,9},{8,10},{9,11},{10,... | collective-permute-start | bytes 393224 | tf_op jit(solution)/shard_map/ppermute | solution.py:401
  27.1 0.0 collective-permute-start.6
  27.1 2.2 %collective-permute-start.7 = (bf16[128,512]{1,0:T(8,128)(2,1)S(1)}, bf16[128,512]{1,0:T(8,128)(2,1)S(1)}, u32[]{:S(2)}, u32[]{:S(2)}) collective-permute-start(bf16[128,512]{1,0:T(8,128)(2,1)S(1)} %get-tuple-element.53), channel_id=1, source_target_pairs={{0,1},{1,0},{2,3},{3,2},{4,5},{5,4},{6,7},{7,6},{8,9},{9,8},{10,11... | collective-permute-start | bytes 393224 | tf_op jit(solution)/shard_map/ppermute | solution.py:401
  29.3 0.9 %collective-permute-done.4.far = bf16[256,512]{1,0:T(8,128)(2,1)S(1)} collective-permute-done((bf16[256,512]{1,0:T(8,128)(2,1)S(1)}, bf16[256,512]{1,0:T(8,128)(2,1)S(1)}, u32[]{:S(2)}, u32[]{:S(2)}) %collective-permute-start.4) | collective-permute-done | bytes 262176 | tf_op jit(solution)/shard_map/ppermute | solution.py:401
  30.2 3.9 %between.1 = (bf16[128,512]{1,0:T(8,128)(2,1)S(1)}, bf16[2,512,512]{2,1,0:T(8,128)(2,1)S(1)}, bf16[2,512,512]{2,1,0:T(8,128)(2,1)S(1)}, bf16[2,512,512]{2,1,0:T(...) custom-call(bf16[384,512]{1,0:T(8,128)(2,1)S(1)} %get-tuple-element., ...), custom_call_target="tpu_custom_call" | custom-call | flops 1476395008 | bytes 14598144 | tf_op jit(solution)/shard_map/between/pallas_call | solution.py:375
  34.1 1.2 %collective-permute-done.5.far_side = bf16[128,512]{1,0:T(8,128)(2,1)S(1)} collective-permute-done((bf16[128,512]{1,0:T(8,128)(2,1)S(1)}, bf16[128,512]{1,0:T(8,128)(2,1)S(1)}, u32[]{:S(2)}, u32[]{:S(2)}) %collective-permute-start.5) | collective-permute-done | bytes 131104 | tf_op jit(solution)/shard_map/ppermute | solution.py:401
  35.3 0.5 %collective-permute-done.6.far_corner = bf16[128,512]{1,0:T(8,128)(2,1)S(1)} collective-permute-done((bf16[128,512]{1,0:T(8,128)(2,1)S(1)}, bf16[128,512]{1,0:T(8,128)(2,1)S(1)}, u32[]{:S(2)}, u32[]{:S(2)}) %collective-permute-start.6) | collective-permute-done | bytes 131104 | tf_op jit(solution)/shard_map/ppermute | solution.py:401
  35.9 10.7 %second.1 = (bf16[64,16,512]{2,1,0:T(8,128)(2,1)}, bf16[2,512,512]{2,1,0:T(8,128)(2,1)S(1)}, bf16[2,512,512]{2,1,0:T(8,128)(2,1)S(1)}, bf16[2,512,512]{2,1,0:T(8,128)(2,1)S(1)}) custom-call(bf16[256,512]{1,0:T(8,128)(2,1)S(1)} %get-tuple-element.41.window_a_first.home, ...), custom_call_target="tpu_custom_call", output_to_operand_aliasing={{1}: (6, {}), {2}: (7, {}), {3}: (8, {})} | custom-call | flops 4764729344 | bytes 10493952 | tf_op jit(solution)/shard_map/second/pallas_call | solution.py:375
  (18 shorter events, 0.1 us)
Async XLA Ops:
  0.0 9.5 %copy-start.2 = (bf16[64,16,512]{2,1,0:T(8,128)(2,1)S(1)}, bf16[64,16,512]{2,1,0:T(8,128)(2,1)}, u32[]{:S(2)}) copy-start(bf16[64,16,512]{2,1,0:T(8,128)(2,1)} %block.1) | copy-start | bytes 3145732
  0.0 9.5 %copy-start.4 = (f32[2,2,512]{2,1,0:T(2,128)S(1)}, f32[2,2,512]{2,1,0:T(2,128)}, u32[]{:S(2)}) copy-start(f32[2,2,512]{2,1,0:T(2,128)} %gains.9) | copy-start | bytes 24580
  0.0 9.5 %copy-start.5 = (s32[64,16]{0,1:T(8,128)S(1)}, s32[64,16]{0,1:T(8,128)}, u32[]{:S(2)}) copy-start(s32[64,16]{0,1:T(8,128)} %param.10) | copy-start | bytes 12292
  0.0 9.5 %copy-start.7 = (s32[64]{0:T(128)S(1)}, s32[64]{0:T(128)}, u32[]{:S(2)}) copy-start(s32[64]{0:T(128)} %bands.1) | copy-start | bytes 772
  1.9 7.6 %copy-start.6 = (bf16[16,128]{1,0:T(8,128)(2,1)S(1)}, bf16[16,128]{1,0:T(8,128)(2,1)}, u32[]{:S(2)}) copy-start(bf16[16,128]{1,0:T(8,128)(2,1)} %get-tuple-element.34.token) | copy-start | bytes 12292
  1.9 13.4 %collective-permute-start = (bf16[272,512]{1,0:T(8,128)(2,1)}, bf16[272,512]{1,0:T(8,128)(2,1)S(1)}, u32[]{:S(2)}, u32[]{:S(2)}) collective-permute-start(bf16[272,512]{1,0:T(8,128)(2,1)} %get-tuple-element.37), channel_id=1, source_target_pairs={{0,14},{1,15},{2,0},{3,1},{4,2},{5,3},{6,4},{7,5},{8,6},{9,7},{10,... | collective-permute-start | bytes 835592 | tf_op jit(solution)/shard_map/ppermute | solution.py:401
  9.5 3.8 %copy-start = (bf16[2,512,1024]{2,1,0:T(8,128)(2,1)S(1)}, bf16[2,512,1024]{2,1,0:T(8,128)(2,1)}, u32[]{:S(2)}) copy-start(bf16[2,512,1024]{2,1,0:T(8,128)(2,1)} %expand_hbm.1) | copy-start | bytes 6291460
  9.6 3.8 %copy-start.3 = (bf16[2,512,512]{2,1,0:T(8,128)(2,1)S(1)}, bf16[2,512,512]{2,1,0:T(8,128)(2,1)}, u32[]{:S(2)}) copy-start(bf16[2,512,512]{2,1,0:T(8,128)(2,1)} %attend_out_hbm.1) | copy-start | bytes 3145732
  11.2 2.2 %copy-start.1 = (bf16[2,1024,512]{2,1,0:T(8,128)(2,1)S(1)}, bf16[2,1024,512]{2,1,0:T(8,128)(2,1)}, u32[]{:S(2)}) copy-start(bf16[2,1024,512]{2,1,0:T(8,128)(2,1)} %contract_hbm.1) | copy-start | bytes 6291460
  11.2 9.8 %collective-permute-start.1 = (bf16[144,512]{1,0:T(8,128)(2,1)S(1)}, bf16[144,512]{1,0:T(8,128)(2,1)S(1)}, u32[]{:S(2)}, u32[]{:S(2)}) collective-permute-start(bf16[144,512]{1,0:T(8,128)(2,1)S(1)} %get-tuple-element.42), channel_id=1, source_target_pairs={{0,14},{1,15},{2,0},{3,1},{4,2},{5,3},{6,4},{7,5},{8,6},{9,7},{10,... | collective-permute-start | bytes 442376 | tf_op jit(solution)/shard_map/ppermute | solution.py:401
  11.8 9.2 %collective-permute-start.2 = (bf16[144,512]{1,0:T(8,128)(2,1)S(1)}, bf16[144,512]{1,0:T(8,128)(2,1)S(1)}, u32[]{:S(2)}, u32[]{:S(2)}) collective-permute-start(bf16[144,512]{1,0:T(8,128)(2,1)S(1)} %get-tuple-element.43), channel_id=1, source_target_pairs={{0,15},{1,14},{2,1},{3,0},{4,3},{5,2},{6,5},{7,4},{8,7},{9,6},{10,... | collective-permute-start | bytes 442376 | tf_op jit(solution)/shard_map/ppermute | solution.py:401
  12.0 9.0 %collective-permute-start.3 = (bf16[144,512]{1,0:T(8,128)(2,1)S(1)}, bf16[144,512]{1,0:T(8,128)(2,1)S(1)}, u32[]{:S(2)}, u32[]{:S(2)}) collective-permute-start(bf16[144,512]{1,0:T(8,128)(2,1)S(1)} %get-tuple-element.44), channel_id=1, source_target_pairs={{0,1},{1,0},{2,3},{3,2},{4,5},{5,4},{6,7},{7,6},{8,9},{9,8},{10,11... | collective-permute-start | bytes 442376 | tf_op jit(solution)/shard_map/ppermute | solution.py:401
  20.7 9.5 %collective-permute-start.4 = (bf16[256,512]{1,0:T(8,128)(2,1)S(1)}, bf16[256,512]{1,0:T(8,128)(2,1)S(1)}, u32[]{:S(2)}, u32[]{:S(2)}) collective-permute-start(bf16[256,512]{1,0:T(8,128)(2,1)S(1)} %get-tuple-element.49), channel_id=1, source_target_pairs={{0,2},{1,3},{2,4},{3,5},{4,6},{5,7},{6,8},{7,9},{8,10},{9,11},{10,... | collective-permute-start | bytes 786440 | tf_op jit(solution)/shard_map/ppermute | solution.py:401
  26.1 9.3 %collective-permute-start.5 = (bf16[128,512]{1,0:T(8,128)(2,1)S(1)}, bf16[128,512]{1,0:T(8,128)(2,1)S(1)}, u32[]{:S(2)}, u32[]{:S(2)}) collective-permute-start(bf16[128,512]{1,0:T(8,128)(2,1)S(1)} %get-tuple-element.51), channel_id=1, source_target_pairs={{0,2},{1,3},{2,4},{3,5},{4,6},{5,7},{6,8},{7,9},{8,10},{9,11},{10,... | collective-permute-start | bytes 393224 | tf_op jit(solution)/shard_map/ppermute | solution.py:401
  27.1 8.8 %collective-permute-start.6 = (bf16[128,512]{1,0:T(8,128)(2,1)S(1)}, bf16[128,512]{1,0:T(8,128)(2,1)S(1)}, u32[]{:S(2)}, u32[]{:S(2)}) collective-permute-start(bf16[128,512]{1,0:T(8,128)(2,1)S(1)} %get-tuple-element.52), channel_id=1, source_target_pairs={{0,3},{1,2},{2,5},{3,4},{4,7},{5,6},{6,9},{7,8},{8,11},{9,10},{10,... | collective-permute-start | bytes 393224 | tf_op jit(solution)/shard_map/ppermute | solution.py:401
  27.1 8.8 %collective-permute-start.7 = (bf16[128,512]{1,0:T(8,128)(2,1)S(1)}, bf16[128,512]{1,0:T(8,128)(2,1)S(1)}, u32[]{:S(2)}, u32[]{:S(2)}) collective-permute-start(bf16[128,512]{1,0:T(8,128)(2,1)S(1)} %get-tuple-element.53), channel_id=1, source_target_pairs={{0,1},{1,0},{2,3},{3,2},{4,5},{5,4},{6,7},{7,6},{8,9},{9,8},{10,11... | collective-permute-start | bytes 393224 | tf_op jit(solution)/shard_map/ppermute | solution.py:401

commit v10 on v9

--- a/solution.py
+++ b/solution.py
@@ -348,21 +348,16 @@
         ],
         0, 4 * part,
     )
-    fields = [jnp.concatenate(parts[at : at + 2], 0) for parts in windows for at in (0, 2)]
-    near = {}
-
-    def write(index, out):
-        window = index // 2
-        if index % 2 == 0:
-            near[window] = out
-            return
-        both = [piece.reshape(WH, SW, D) for piece in (out, near.pop(window))]
+    fields = [jnp.concatenate(parts, 0) for parts in windows]
+
+    def write(window, out):
         rows = pl.ds(window * WH, WH)
+        both = [out[at : at + 2 * part].reshape(WH, SW, D) for at in (2 * part, 0)]
         out_ref[rows] = jnp.concatenate(both, 1).astype(BF16)
         copies.append(pltpu.make_async_copy(out_ref.at[rows], out_hbm.at[rows], sems.at[window]))
         copies[-1].start()
 
-    lows = [2 * part * at for at in range(len(fields))]
+    lows = [4 * part * at for at in range(len(fields))]
     finish(fields, context, lows, attend_out, gains[1, 1:2], expand, contract, write)
     for copy in copies:
         copy.wait()

time: 47.4 us -> 47.3 us (level)
  no operation moved by 1% of the time
where the time goes in v10:
time: 47.3 us; the launch traced here: 46.6 us
  Pallas kernels  28.4 us (60%)
  starting transfers between devices  11.7 us (25%)
  waiting for transfers between devices  4.54 us (10%)
  local copies, waits for them, and re-layouts  1.72 us (4%)
    pallas_call x6, Pallas kernels, call(): pl.pallas_call(kernel, out_shape=shapes, in_specs=specs, out_specs=[outs]...  28.4 us
    ppermute x8, starting transfers between devices, moved(): return lax.ppermute(value, ('lon', 'lat'), pairs)  11.7 us
    ppermute x8, waiting for transfers between devices, moved(): return lax.ppermute(value, ('lon', 'lat'), pairs)  4.54 us
    squeeze x1, local copies, waits for them, and re-layouts, on_device(): attend_in[0]  1.51 us
  transfers between devices with their start and end apart: 8, of which 4 were waited for; matrix products, arithmetic and copies ran while one was open for 4% of the time, Pallas kernels for 34%

profile of v10, /device:TPU:0, one launch (start us, length us, event | category | flops | bytes accessed | tf_op | source)
XLA Modules:
  0.0 46.6 jit_solution(13463523226446332578)
XLA Ops:
  0.0 1.9 %pack_main.1 = (bf16[272,512]{1,0:T(8,128)(2,1)}, bf16[16,128]{1,0:T(8,128)(2,1)}) custom-call(bf16[64,16,512]{2,1,0:T(8,128)(2,1)} %block.1, s32[16,64]{1,0:T(8,128)} %bitcast.9), custom_call_target="tpu_custom_call" | custom-call | flops 1000000 | bytes 1052672 | tf_op jit(solution)/shard_map/pack_main/pallas_call | solution.py:370
  1.9 6.1 %collective-permute-start = (bf16[272,512]{1,0:T(8,128)(2,1)}, bf16[272,512]{1,0:T(8,128)(2,1)S(1)}, u32[]{:S(2)}, u32[]{:S(2)}) collective-permute-start(bf16[272,512]{1,0:T(8,128)(2,1)} %get-tuple-element.37), channel_id=1, source_target_pairs={{0,14},{1,15},{2,0},{3,1},{4,2},{5,3},{6,4},{7,5},{8,6},{9,7},{10,... | collective-permute-start | bytes 835592 | tf_op jit(solution)/shard_map/ppermute | solution.py:396
  8.0 1.5 %slice_bitcast_fusion.attend_in = bf16[512,1536]{1,0:T(8,128)(2,1)S(1)} fusion(bf16[2,512,1536]{2,1,0:T(8,128)(2,1)} %attend_in_hbm.1), kind=kLoop, calls=%fused_computation | loop fusion | bytes 3145728 | tf_op jit(solution)/shard_map/squeeze | solution.py:417
  9.5 0.0 copy-start
  9.6 0.0 copy-start.3
  9.6 1.6 %early.1 = (bf16[144,512]{1,0:T(8,128)(2,1)S(1)}, bf16[144,512]{1,0:T(8,128)(2,1)S(1)}, bf16[144,512]{1,0:T(8,128)(2,1)S(1)}, bf16[384,512]{1,0:T(8,128)(2,1)S(1...) custom-call(bf16[64,16,512]{2,1,0:T(8,128)(2,1)S(1)} %copy-done.2, ...), custom_call_target="tpu_custom_call" | custom-call | flops 603979776 | bytes 2638080 | tf_op jit(solution)/shard_map/early/pallas_call | solution.py:370
  11.2 0.0 copy-start.1
  11.2 0.6 %collective-permute-start.1 = (bf16[144,512]{1,0:T(8,128)(2,1)S(1)}, bf16[144,512]{1,0:T(8,128)(2,1)S(1)}, u32[]{:S(2)}, u32[]{:S(2)}) collective-permute-start(bf16[144,512]{1,0:T(8,128)(2,1)S(1)} %get-tuple-element.42), channel_id=1, source_target_pairs={{0,14},{1,15},{2,0},{3,1},{4,2},{5,3},{6,4},{7,5},{8,6},{9,7},{10,... | collective-permute-start | bytes 442376 | tf_op jit(solution)/shard_map/ppermute | solution.py:396
  11.8 0.3 collective-permute-start.2
  12.0 1.2 %collective-permute-start.3 = (bf16[144,512]{1,0:T(8,128)(2,1)S(1)}, bf16[144,512]{1,0:T(8,128)(2,1)S(1)}, u32[]{:S(2)}, u32[]{:S(2)}) collective-permute-start(bf16[144,512]{1,0:T(8,128)(2,1)S(1)} %get-tuple-element.44), channel_id=1, source_target_pairs={{0,1},{1,0},{2,3},{3,2},{4,5},{5,4},{6,7},{7,6},{8,9},{9,8},{10,11... | collective-permute-start | bytes 442376 | tf_op jit(solution)/shard_map/ppermute | solution.py:396
  13.3 0.1 slice_bitcast_fusion.2.expand
  13.4 0.1 slice_bitcast_fusion.1.contract
  13.5 1.9 %collective-permute-done.taken = bf16[272,512]{1,0:T(8,128)(2,1)S(1)} collective-permute-done((bf16[272,512]{1,0:T(8,128)(2,1)}, bf16[272,512]{1,0:T(8,128)(2,1)S(1)}, u32[]{:S(2)}, u32[]{:S(2)}) %collective-permute-start) | collective-permute-done | bytes 278560 | tf_op jit(solution)/shard_map/ppermute | solution.py:396
  15.4 5.3 %window_a.1 = (bf16[256,512]{1,0:T(8,128)(2,1)S(1)}, bf16[256,512]{1,0:T(8,128)(2,1)S(1)}) custom-call(bf16[384,512]{1,0:T(8,128)(2,1)S(1)} %get-tuple-element.35.cells_here, f32[16,512]{1,0:T(8,128)S(1)} %get-tuple-element.36.notes, bf16[272,512]{1,0:T(8,128)(2,1)S(1)} %collective-permute-done.taken, bf16[384,512]{1,0:T(8,128)(2,1)S(1)} %get-tuple-element.38.near_query, ...), custom_call_target="tpu_custom_call" | custom-call | flops 2281701376 | bytes 6086656 | tf_op jit(solution)/shard_map/window_a/pallas_call | solution.py:370
  20.7 0.3 collective-permute-start.4
  21.0 5.0 %window_b_away.1 = (bf16[128,512]{1,0:T(8,128)(2,1)S(1)}, bf16[128,512]{1,0:T(8,128)(2,1)S(1)}, bf16[128,512]{1,0:T(8,128)(2,1)S(1)}, bf16[512,512]{1,0:T(8,128)...) custom-call(bf16[256,512]{1,0:T(8,128)(2,1)S(1)} %get-tuple-element.41.window_a_first., ...), custom_call_target="tpu_custom_call" | custom-call | flops 2013265920 | bytes 6119424 | tf_op jit(solution)/shard_map/window_b_away/pallas_call | solution.py:370
  26.1 1.0 %collective-permute-start.5 = (bf16[128,512]{1,0:T(8,128)(2,1)S(1)}, bf16[128,512]{1,0:T(8,128)(2,1)S(1)}, u32[]{:S(2)}, u32[]{:S(2)}) collective-permute-start(bf16[128,512]{1,0:T(8,128)(2,1)S(1)} %get-tuple-element.51), channel_id=1, source_target_pairs={{0,2},{1,3},{2,4},{3,5},{4,6},{5,7},{6,8},{7,9},{8,10},{9,11},{10,... | collective-permute-start | bytes 393224 | tf_op jit(solution)/shard_map/ppermute | solution.py:396
  27.1 0.0 collective-permute-start.6
  27.1 2.2 %collective-permute-start.7 = (bf16[128,512]{1,0:T(8,128)(2,1)S(1)}, bf16[128,512]{1,0:T(8,128)(2,1)S(1)}, u32[]{:S(2)}, u32[]{:S(2)}) collective-permute-start(bf16[128,512]{1,0:T(8,128)(2,1)S(1)} %get-tuple-element.53), channel_id=1, source_target_pairs={{0,1},{1,0},{2,3},{3,2},{4,5},{5,4},{6,7},{7,6},{8,9},{9,8},{10,11... | collective-permute-start | bytes 393224 | tf_op jit(solution)/shard_map/ppermute | solution.py:396
  29.3 0.9 %collective-permute-done.4.far = bf16[256,512]{1,0:T(8,128)(2,1)S(1)} collective-permute-done((bf16[256,512]{1,0:T(8,128)(2,1)S(1)}, bf16[256,512]{1,0:T(8,128)(2,1)S(1)}, u32[]{:S(2)}, u32[]{:S(2)}) %collective-permute-start.4) | collective-permute-done | bytes 262176 | tf_op jit(solution)/shard_map/ppermute | solution.py:396
  30.2 3.9 %between.1 = (bf16[128,512]{1,0:T(8,128)(2,1)S(1)}, bf16[2,512,512]{2,1,0:T(8,128)(2,1)S(1)}, bf16[2,512,512]{2,1,0:T(8,128)(2,1)S(1)}, bf16[2,512,512]{2,1,0:T(...) custom-call(bf16[384,512]{1,0:T(8,128)(2,1)S(1)} %get-tuple-element., ...), custom_call_target="tpu_custom_call" | custom-call | flops 1476395008 | bytes 14598144 | tf_op jit(solution)/shard_map/between/pallas_call | solution.py:370
  34.1 1.2 %collective-permute-done.5.far_side = bf16[128,512]{1,0:T(8,128)(2,1)S(1)} collective-permute-done((bf16[128,512]{1,0:T(8,128)(2,1)S(1)}, bf16[128,512]{1,0:T(8,128)(2,1)S(1)}, u32[]{:S(2)}, u32[]{:S(2)}) %collective-permute-start.5) | collective-permute-done | bytes 131104 | tf_op jit(solution)/shard_map/ppermute | solution.py:396
  35.3 0.5 %collective-permute-done.6.far_corner = bf16[128,512]{1,0:T(8,128)(2,1)S(1)} collective-permute-done((bf16[128,512]{1,0:T(8,128)(2,1)S(1)}, bf16[128,512]{1,0:T(8,128)(2,1)S(1)}, u32[]{:S(2)}, u32[]{:S(2)}) %collective-permute-start.6) | collective-permute-done | bytes 131104 | tf_op jit(solution)/shard_map/ppermute | solution.py:396
  35.9 10.6 %second.1 = (bf16[64,16,512]{2,1,0:T(8,128)(2,1)}, bf16[2,512,512]{2,1,0:T(8,128)(2,1)S(1)}, bf16[2,512,512]{2,1,0:T(8,128)(2,1)S(1)}, bf16[2,512,512]{2,1,0:T(8,128)(2,1)S(1)}) custom-call(bf16[256,512]{1,0:T(8,128)(2,1)S(1)} %get-tuple-element.41.window_a_first.home, ...), custom_call_target="tpu_custom_call", output_to_operand_aliasing={{1}: (6, {}), {2}: (7, {}), {3}: (8, {})} | custom-call | flops 4764729344 | bytes 10493952 | tf_op jit(solution)/shard_map/second/pallas_call | solution.py:370
  (18 shorter events, 0.1 us)
Async XLA Ops:
  0.0 9.5 %copy-start.2 = (bf16[64,16,512]{2,1,0:T(8,128)(2,1)S(1)}, bf16[64,16,512]{2,1,0:T(8,128)(2,1)}, u32[]{:S(2)}) copy-start(bf16[64,16,512]{2,1,0:T(8,128)(2,1)} %block.1) | copy-start | bytes 3145732
  0.0 9.5 %copy-start.4 = (f32[2,2,512]{2,1,0:T(2,128)S(1)}, f32[2,2,512]{2,1,0:T(2,128)}, u32[]{:S(2)}) copy-start(f32[2,2,512]{2,1,0:T(2,128)} %gains.9) | copy-start | bytes 24580
  0.0 9.5 %copy-start.5 = (s32[64,16]{0,1:T(8,128)S(1)}, s32[64,16]{0,1:T(8,128)}, u32[]{:S(2)}) copy-start(s32[64,16]{0,1:T(8,128)} %param.10) | copy-start | bytes 12292
  0.0 9.5 %copy-start.7 = (s32[64]{0:T(128)S(1)}, s32[64]{0:T(128)}, u32[]{:S(2)}) copy-start(s32[64]{0:T(128)} %bands.1) | copy-start | bytes 772
  1.9 7.6 %copy-start.6 = (bf16[16,128]{1,0:T(8,128)(2,1)S(1)}, bf16[16,128]{1,0:T(8,128)(2,1)}, u32[]{:S(2)}) copy-start(bf16[16,128]{1,0:T(8,128)(2,1)} %get-tuple-element.34.token) | copy-start | bytes 12292
  1.9 13.4 %collective-permute-start = (bf16[272,512]{1,0:T(8,128)(2,1)}, bf16[272,512]{1,0:T(8,128)(2,1)S(1)}, u32[]{:S(2)}, u32[]{:S(2)}) collective-permute-start(bf16[272,512]{1,0:T(8,128)(2,1)} %get-tuple-element.37), channel_id=1, source_target_pairs={{0,14},{1,15},{2,0},{3,1},{4,2},{5,3},{6,4},{7,5},{8,6},{9,7},{10,... | collective-permute-start | bytes 835592 | tf_op jit(solution)/shard_map/ppermute | solution.py:396
  9.5 3.8 %copy-start = (bf16[2,512,1024]{2,1,0:T(8,128)(2,1)S(1)}, bf16[2,512,1024]{2,1,0:T(8,128)(2,1)}, u32[]{:S(2)}) copy-start(bf16[2,512,1024]{2,1,0:T(8,128)(2,1)} %expand_hbm.1) | copy-start | bytes 6291460
  9.6 3.8 %copy-start.3 = (bf16[2,512,512]{2,1,0:T(8,128)(2,1)S(1)}, bf16[2,512,512]{2,1,0:T(8,128)(2,1)}, u32[]{:S(2)}) copy-start(bf16[2,512,512]{2,1,0:T(8,128)(2,1)} %attend_out_hbm.1) | copy-start | bytes 3145732
  11.2 2.2 %copy-start.1 = (bf16[2,1024,512]{2,1,0:T(8,128)(2,1)S(1)}, bf16[2,1024,512]{2,1,0:T(8,128)(2,1)}, u32[]{:S(2)}) copy-start(bf16[2,1024,512]{2,1,0:T(8,128)(2,1)} %contract_hbm.1) | copy-start | bytes 6291460
  11.2 9.8 %collective-permute-start.1 = (bf16[144,512]{1,0:T(8,128)(2,1)S(1)}, bf16[144,512]{1,0:T(8,128)(2,1)S(1)}, u32[]{:S(2)}, u32[]{:S(2)}) collective-permute-start(bf16[144,512]{1,0:T(8,128)(2,1)S(1)} %get-tuple-element.42), channel_id=1, source_target_pairs={{0,14},{1,15},{2,0},{3,1},{4,2},{5,3},{6,4},{7,5},{8,6},{9,7},{10,... | collective-permute-start | bytes 442376 | tf_op jit(solution)/shard_map/ppermute | solution.py:396
  11.8 9.2 %collective-permute-start.2 = (bf16[144,512]{1,0:T(8,128)(2,1)S(1)}, bf16[144,512]{1,0:T(8,128)(2,1)S(1)}, u32[]{:S(2)}, u32[]{:S(2)}) collective-permute-start(bf16[144,512]{1,0:T(8,128)(2,1)S(1)} %get-tuple-element.43), channel_id=1, source_target_pairs={{0,15},{1,14},{2,1},{3,0},{4,3},{5,2},{6,5},{7,4},{8,7},{9,6},{10,... | collective-permute-start | bytes 442376 | tf_op jit(solution)/shard_map/ppermute | solution.py:396
  12.0 9.0 %collective-permute-start.3 = (bf16[144,512]{1,0:T(8,128)(2,1)S(1)}, bf16[144,512]{1,0:T(8,128)(2,1)S(1)}, u32[]{:S(2)}, u32[]{:S(2)}) collective-permute-start(bf16[144,512]{1,0:T(8,128)(2,1)S(1)} %get-tuple-element.44), channel_id=1, source_target_pairs={{0,1},{1,0},{2,3},{3,2},{4,5},{5,4},{6,7},{7,6},{8,9},{9,8},{10,11... | collective-permute-start | bytes 442376 | tf_op jit(solution)/shard_map/ppermute | solution.py:396
  20.7 9.5 %collective-permute-start.4 = (bf16[256,512]{1,0:T(8,128)(2,1)S(1)}, bf16[256,512]{1,0:T(8,128)(2,1)S(1)}, u32[]{:S(2)}, u32[]{:S(2)}) collective-permute-start(bf16[256,512]{1,0:T(8,128)(2,1)S(1)} %get-tuple-element.49), channel_id=1, source_target_pairs={{0,2},{1,3},{2,4},{3,5},{4,6},{5,7},{6,8},{7,9},{8,10},{9,11},{10,... | collective-permute-start | bytes 786440 | tf_op jit(solution)/shard_map/ppermute | solution.py:396
  26.1 9.3 %collective-permute-start.5 = (bf16[128,512]{1,0:T(8,128)(2,1)S(1)}, bf16[128,512]{1,0:T(8,128)(2,1)S(1)}, u32[]{:S(2)}, u32[]{:S(2)}) collective-permute-start(bf16[128,512]{1,0:T(8,128)(2,1)S(1)} %get-tuple-element.51), channel_id=1, source_target_pairs={{0,2},{1,3},{2,4},{3,5},{4,6},{5,7},{6,8},{7,9},{8,10},{9,11},{10,... | collective-permute-start | bytes 393224 | tf_op jit(solution)/shard_map/ppermute | solution.py:396
  27.1 8.8 %collective-permute-start.6 = (bf16[128,512]{1,0:T(8,128)(2,1)S(1)}, bf16[128,512]{1,0:T(8,128)(2,1)S(1)}, u32[]{:S(2)}, u32[]{:S(2)}) collective-permute-start(bf16[128,512]{1,0:T(8,128)(2,1)S(1)} %get-tuple-element.52), channel_id=1, source_target_pairs={{0,3},{1,2},{2,5},{3,4},{4,7},{5,6},{6,9},{7,8},{8,11},{9,10},{10,... | collective-permute-start | bytes 393224 | tf_op jit(solution)/shard_map/ppermute | solution.py:396
  27.1 8.8 %collective-permute-start.7 = (bf16[128,512]{1,0:T(8,128)(2,1)S(1)}, bf16[128,512]{1,0:T(8,128)(2,1)S(1)}, u32[]{:S(2)}, u32[]{:S(2)}) collective-permute-start(bf16[128,512]{1,0:T(8,128)(2,1)S(1)} %get-tuple-element.53), channel_id=1, source_target_pairs={{0,1},{1,0},{2,3},{3,2},{4,5},{5,4},{6,7},{7,6},{8,9},{9,8},{10,11... | collective-permute-start | bytes 393224 | tf_op jit(solution)/shard_map/ppermute | solution.py:396
